TPU v7x, 32 devices: a whole 2x2x4 slice. The times are simulated.
32 devices in a mesh: head: 4 (over x, core), track: 8 (over z, y).
Axes of the slice: x: 2, y: 2, z: 4, core: 2. Of those that a mesh axis runs over, the one named last changes fastest.
Arguments:
- potential: float32 [256, 1024, 128], P('head', 'track'), may hold values from -6 to 6
- source: float32 [256, 1024, 128], P('head', 'track'), may hold values from -6 to 6
- depth_kernel: float32 [3, 128], replicated, may hold values from -0.5 to 0.5
- magnet: float32 [3, 8, 16384], P(None, 'track', 'head'), may hold values from -0.8 to 0.8
- footprint: int32 [8, 16384], P('track', 'head'), may hold values from 0 to 65535, as said below
- temp_index: int32 [8, 16384], P('track', 'head'), may hold values from 0 to 127
- temp_profile: float32 [128], replicated, may hold values from 0.3 to 1.4
- self_tiles: float32 [8, 128, 128, 128], P('track', 'head'), may hold values from -0.5 to 0.5
- next_tiles: float32 [8, 128, 128, 128], P('track', 'head'), may hold values from -0.5 to 0.5
Outputs:
- relaxed: float32 [256, 1024, 128], P('head', 'track')
- magnet_out: float32 [3, 8, 16384], P(None, 'track', 'head')
Inputs may be any that keep to these rules, and one draw needn't show every extreme that they name: Within the 4096 grains of one device (an aligned block of a track tile), no more than 1024 have footprint cells in any one pole block of 8192 cells; in every draw one pole block, the same for every device, takes exactly 1024 grains of every device.
All inputs are finite; a program needn't handle non-finite values.
Results may differ from a plain program's by a relative error of at most 0.0001.
Values sent between devices are 32-bit elements; how exact they have to be, the bound alone decides.
No kernel may reach another device: no remote copies, remote signals or barrier semaphores. Data moves between devices by JAX's collectives and lax.ppermute only.
A program may use at most 320 MiB of HBM per device.

v0:
```python
import jax
import jax.numpy as jnp
from jax import lax
from jax.sharding import PartitionSpec as P

HIGH = lax.Precision.HIGHEST


def extended(block, sides, width):
    for axis, dim in sides:
        count = lax.axis_size(axis)
        forward = [(i, i + 1) for i in range(count - 1)]
        backward = [(target, source) for source, target in forward]
        low = lax.ppermute(
            lax.slice_in_dim(block, block.shape[dim] - width, None, axis=dim), axis, forward
        )
        high = lax.ppermute(lax.slice_in_dim(block, 0, width, axis=dim), axis, backward)
        block = jnp.concatenate([low, block, high], axis=dim)
    return block


def relax_sweep(padded, source):
    center = padded[1:-1, 1:-1]
    deep = jnp.pad(center, ((0, 0), (0, 0), (1, 1)))
    others = [
        padded[2:, 1:-1],
        padded[:-2, 1:-1],
        padded[1:-1, 2:],
        padded[1:-1, :-2],
        deep[:, :, 2:],
        deep[:, :, :-2],
    ]
    numer = source
    denom = jnp.ones_like(center)
    for other in others:
        differ = other - center
        perm = 1.0 + 4.0 / (1.0 + 4.0 * differ * differ)
        numer = numer + perm * differ
        denom = denom + perm
    return center + 0.8 * numer / denom


def cross_comp(a_vec, b_vec):
    return jnp.stack(
        [
            a_vec[1] * b_vec[2] - a_vec[2] * b_vec[1],
            a_vec[2] * b_vec[0] - a_vec[0] * b_vec[2],
            a_vec[0] * b_vec[1] - a_vec[1] * b_vec[0],
        ]
    )


def llb_section(state, field, target):
    sq_norm = jnp.sum(state * state, axis=0)
    total = field + 0.5 * (1.0 - sq_norm / target) * state
    turn = cross_comp(state, total)
    damp = cross_comp(state, turn)
    along = jnp.sum(state * total, axis=0)
    return state + 0.1 * (-turn - 0.5 * damp + 0.3 * along * state)


def per_device(
    potential,
    source,
    depth_kernel,
    magnet,
    footprint,
    temp_index,
    temp_profile,
    self_tiles,
    next_tiles,
):
    rows_x, rows_y, depth = potential.shape
    relaxed = potential
    for sweep_idx in range(2):
        padded = extended(relaxed, (("head", 0), ("track", 1)), 1)
        relaxed = relax_sweep(padded, source)
    surface = jnp.einsum("kz,xyz->kxy", depth_kernel, relaxed, precision=HIGH).reshape(
        3, rows_x * rows_y
    )
    cells = footprint[0]
    table = lax.all_gather(surface, "track", axis=1, tiled=True)
    applied = jnp.take(table, cells, axis=1)
    n_prof = temp_profile.shape[0]
    onehot = (temp_index[0][None, :] == jnp.arange(n_prof, dtype=jnp.int32)[:, None]).astype(
        jnp.float32
    )
    temp = jnp.dot(temp_profile[None, :], onehot, precision=HIGH)[0]
    target = 0.05 + jnp.maximum(1.0 - temp, 0.0)
    couple_self = self_tiles[0]
    couple_next = next_tiles[0]
    n_tiles, tile_w = (couple_self.shape[0], couple_self.shape[1])
    state = magnet[:, 0, :]
    for section in range(2):
        rimmed = extended(state, (("head", 1),), tile_w)
        tiles = rimmed.reshape(3, n_tiles + 2, tile_w)
        ex = jnp.einsum("kij,ckj->cki", couple_self, tiles[:, 1:-1], precision=HIGH)
        ex = ex + jnp.einsum("kij,ckj->cki", couple_next, tiles[:, :-2], precision=HIGH)
        ex = ex + jnp.einsum("kji,ckj->cki", couple_next, tiles[:, 2:], precision=HIGH)
        state = llb_section(state, applied + ex.reshape(3, n_tiles * tile_w), target)
    return (relaxed, state[:, None, :])


def solution(mesh):
    in_specs = (
        P("head", "track", None),
        P("head", "track", None),
        P(),
        P(None, "track", "head"),
        P("track", "head"),
        P("track", "head"),
        P(),
        P("track", "head", None, None),
        P("track", "head", None, None),
    )
    out_specs = (P("head", "track", None), P(None, "track", "head"))
    return jax.shard_map(
        per_device, mesh=mesh, in_specs=in_specs, out_specs=out_specs, check_vma=False
    )
```

profile of v0, /device:TPU:0, one launch (start us, length us, event | category | flops | bytes accessed | tf_op | source)
XLA Modules:
  0.0 763.0 jit_solution(16704305644081721051)
XLA Ops:
  1.7 2.4 collective-permute-start.1
  6.2 5.1 collective-permute-start.8
  15.8 2.6 constant_dynamic-update-slice_fusion.1
  18.5 1.6 collective-permute-start.2
  20.1 4.5 collective-permute-start.3
  24.7 1.7 collective-permute-done.3
  26.3 12.3 %divide_add_fusion.1 = f32[64,128,128]{2,1,0:T(8,128)S(1)} fusion(f32[64,128,128]{2,1,0:T(8,128)S(1)} %copy-done.1, f32[66,128,128]{2,1,0:T(8,128)S(1)} %constant_dynamic-update-slice_fusion, f32[66,1,128]{2,1,0:T(1,128)S(1)} %collective-permute-done.3, f32[66,1,128]{2,1,0:T(1,128)S(1)} %collective-permute-done.2, ...), kind=kLoop, calls=%fused_computation.77 | loop fusion | flops 63963136 | bytes 17106944 | tf_op jit(solution)/shard_map/add | solution.py:40
  40.0 3.7 collective-permute-start.5
  43.7 1.9 fusion.50
  46.9 5.1 collective-permute-start.7
  52.0 3.3 fusion.52
  55.4 14.4 %divide_add_fusion = f32[64,128,128]{2,1,0:T(8,128)S(1)} fusion(f32[64,128,128]{2,1,0:T(8,128)S(1)} %divide_add_fusion.1, f32[1,128,128]{2,1,0:T(8,128)S(1)} %collective-permute-done.4, f32[1,128,128]{2,1,0:T(8,128)S(1)} %collective-permute-done.5, f32[66,1,128]{2,1,0:T(1,128)S(1)} %collective-permute-done.7, f32[66,1,128]{2,1,0:T(1,128)S(1)} %collective-permute-done.6, ...), kind=kLoop, calls=%fused_computation.76 | loop fusion | flops 68157440 | bytes 12781568 | tf_op jit(solution)/shard_map/add | solution.py:40
  69.8 2.0 copy-done.3
  71.8 3.6 convolution_bitcast_fusion
  75.5 2.7 copy.106
  78.2 635.2 %all_gather.3 = f32[3,65536]{0,1:T(8,128)} all-gather(f32[3,8192]{0,1:T(8,128)} %copy.106), channel_id=1, replica_groups=mesh['head'=4,'track'=8] {'track'}, dimensions={1}, use_global_device_ids=true | all-gather | bytes 884736 | tf_op jit(solution)/shard_map/all_gather | solution.py:82
  713.4 24.6 %gather_fusion = f32[4096,3]{1,0:T(8,128)} fusion(f32[3,65536]{0,1:T(8,128)} %all_gather.3, s32[4096]{0:T(1024)S(1)} %broadcast_clamp_fusion), kind=kCustom, calls=%fused_computation | custom fusion | bytes 114688 | tf_op jit(solution)/shard_map/jit(_take)/gather | solution.py:83
  738.1 2.2 copy.107
  740.3 5.0 multiply_reduce_fusion.2
  745.6 3.4 collective-permute-start.10
  750.6 2.7 collective-permute-done.11
  753.3 3.3 fusion.48
  756.7 1.9 fusion.46
  758.5 3.4 multiply_reduce_fusion
  (56 shorter events, 13.3 us)
Async XLA Ops:
  0.6 43.0 %copy-start = (f32[1,32,128,128]{3,2,1,0:T(8,128)S(1)}, f32[1,32,128,128]{3,2,1,0:T(8,128)}, u32[]{:S(2)}) copy-start(f32[1,32,128,128]{3,2,1,0:T(8,128)} %param.17) | copy-start | bytes 6291460
  1.7 14.1 %collective-permute-start.1 = (f32[1,128,128]{2,1,0:T(8,128)S(1)}, f32[1,128,128]{2,1,0:T(8,128)S(1)}, u32[]{:S(2)}, u32[]{:S(2)}) collective-permute-start(f32[1,128,128]{2,1,0:T(8,128)S(1)} %get-tuple-element.21), channel_id=1, source_target_pairs={{0,8},{8,16},{16,24},{1,9},{9,17},{17,25},{2,10},{10,18},{18,26},{... | collective-permute-start | bytes 196616 | tf_op jit(solution)/shard_map/ppermute | solution.py:14
  4.0 14.4 %collective-permute-start = (f32[1,128,128]{2,1,0:T(8,128)S(1)}, f32[1,128,128]{2,1,0:T(8,128)S(1)}, u32[]{:S(2)}, u32[]{:S(2)}) collective-permute-start(f32[1,128,128]{2,1,0:T(8,128)S(1)} %get-tuple-element.20), channel_id=1, source_target_pairs={{8,0},{16,8},{24,16},{9,1},{17,9},{25,17},{10,2},{18,10},{26,18},{... | collective-permute-start | bytes 196616 | tf_op jit(solution)/shard_map/ppermute | solution.py:17
  6.2 37.4 %collective-permute-start.8 = (f32[3,128]{1,0:T(4,128)S(1)}, f32[3,128]{1,0:T(4,128)S(1)}, u32[]{:S(2)}, u32[]{:S(2)}) collective-permute-start(f32[3,128]{1,0:T(4,128)S(1)} %get-tuple-element.24), channel_id=1, source_target_pairs={{0,8},{8,16},{16,24},{1,9},{9,17},{17,25},{2,10},{10,18},{18,26},{... | collective-permute-start | bytes 4616 | tf_op jit(solution)/shard_map/ppermute | solution.py:14
  11.3 32.3 %collective-permute-start.9 = (f32[3,128]{1,0:T(4,128)S(1)}, f32[3,128]{1,0:T(4,128)S(1)}, u32[]{:S(2)}, u32[]{:S(2)}) collective-permute-start(f32[3,128]{1,0:T(4,128)S(1)} %get-tuple-element.25), channel_id=1, source_target_pairs={{8,0},{16,8},{24,16},{9,1},{17,9},{25,17},{10,2},{18,10},{26,18},{... | collective-permute-start | bytes 4616 | tf_op jit(solution)/shard_map/ppermute | solution.py:17
  15.8 8.9 %copy-start.6 = (s32[1,4096]{1,0:T(1,128)S(1)}, s32[1,4096]{1,0:T(1,128)}, u32[]{:S(2)}) copy-start(s32[1,4096]{1,0:T(1,128)} %param.13) | copy-start | bytes 49156
  15.8 10.5 %copy-start.1 = (f32[64,128,128]{2,1,0:T(8,128)S(1)}, f32[64,128,128]{2,1,0:T(8,128)}, u32[]{:S(2)}) copy-start(f32[64,128,128]{2,1,0:T(8,128)} %param.9) | copy-start | bytes 12582916
  15.8 10.5 %copy-start.2 = (f32[64,128,128]{2,1,0:T(8,128)S(1)}, f32[64,128,128]{2,1,0:T(8,128)}, u32[]{:S(2)}) copy-start(f32[64,128,128]{2,1,0:T(8,128)} %param.10) | copy-start | bytes 12582916
  18.5 6.1 collective-permute-start.2
  20.1 6.2 collective-permute-start.3
  38.7 6.9 collective-permute-start.4
  40.0 5.6 collective-permute-start.5
  45.6 9.8 %collective-permute-start.6 = (f32[66,1,128]{2,1,0:T(1,128)S(1)}, f32[66,1,128]{2,1,0:T(1,128)S(1)}, u32[]{:S(2)}, u32[]{:S(2)}) collective-permute-start(f32[66,1,128]{2,1,0:T(1,128)S(1)} %get-tuple-element.14), channel_id=1, source_target_pairs={{1,0},{2,1},{3,2},{4,3},{5,4},{6,5},{7,6},{9,8},{10,9},{11,10},{12... | collective-permute-start | bytes 101384 | tf_op jit(solution)/shard_map/ppermute | solution.py:17
  46.9 8.5 %collective-permute-start.7 = (f32[66,1,128]{2,1,0:T(1,128)S(1)}, f32[66,1,128]{2,1,0:T(1,128)S(1)}, u32[]{:S(2)}, u32[]{:S(2)}) collective-permute-start(f32[66,1,128]{2,1,0:T(1,128)S(1)} %get-tuple-element.15), channel_id=1, source_target_pairs={{0,1},{1,2},{2,3},{3,4},{4,5},{5,6},{6,7},{8,9},{9,10},{10,11},{11... | collective-permute-start | bytes 101384 | tf_op jit(solution)/shard_map/ppermute | solution.py:14
  55.4 16.5 %copy-start.7 = (f32[3,128]{1,0:T(4,128)S(1)}, f32[3,128]{1,0:T(4,128)}, u32[]{:S(2)}) copy-start(f32[3,128]{1,0:T(4,128)} %param.11) | copy-start | bytes 4612
  69.8 2.0 copy-start.3
  78.2 662.0 %copy-start.5 = (f32[3,1,4096]{2,1,0:T(1,128)S(1)}, f32[3,1,4096]{2,1,0:T(1,128)}, u32[]{:S(2)}) copy-start(f32[3,1,4096]{2,1,0:T(1,128)} %param.12) | copy-start | bytes 147460
  745.3 13.3 %copy-start.4 = (f32[1,32,128,128]{3,2,1,0:T(8,128)S(1)}, f32[1,32,128,128]{3,2,1,0:T(8,128)}, u32[]{:S(2)}) copy-start(f32[1,32,128,128]{3,2,1,0:T(8,128)} %param.16) | copy-start | bytes 6291460
  745.6 5.0 collective-permute-start.10
  749.1 4.3 collective-permute-start.11
where the time goes:
time: 766 us; the launch traced here: 763 us
  blocking collectives  635 us (83%)
  local copies, waits for them, and re-layouts  36.2 us (5%)
  starting transfers between devices  32.5 us (4%)
  other arithmetic  29.8 us (4%)
  matrix products  23.9 us (3%)
    all_gather x1, blocking collectives, per_device(): table = lax.all_gather(surface, 'track', axis=1, tiled=True)  635 us
    gather x2, local copies, waits for them, and re-layouts, per_device(): applied = jnp.take(table, cells, axis=1)  26.9 us
    add x2, other arithmetic, relax_sweep(): return center + 0.8 * numer / denom  26.7 us
    ppermute x6, starting transfers between devices, extended(): lax.ppermute(lax.slice_in_dim(block, block.shape[dim] - width, None, axis...  24.2 us
  transfers between devices with their start and end apart: 12, of which 2 were waited for; matrix products, arithmetic and copies ran while one was open for 3% of the time, Pallas kernels for 0%

commit v1 on v0

v1 whole, which is shorter than its diff:
```python
import math

import jax
import jax.numpy as jnp
from jax import lax
from jax.experimental import pallas as pl
from jax.experimental.pallas import tpu as pltpu
from jax.sharding import PartitionSpec as P

F32 = jnp.float32
BF16 = jnp.bfloat16
STRIP = 16
UNIT = 4
TOP = 8
LANES = 128
NT = (((1,), (1,)), ((), ()))
VM = pl.BlockSpec(memory_space=pltpu.VMEM)
SM = pl.BlockSpec(memory_space=pltpu.SMEM)
ANY = pl.BlockSpec(memory_space=pl.ANY)


def mm(a, b):
    return jnp.dot(a, b, preferred_element_type=F32)


def mm_nt(a, b):
    return lax.dot_general(a, b, NT, preferred_element_type=F32)


def split(v):
    hi = v.astype(BF16)
    return hi, (v - hi.astype(F32)).astype(BF16)


def cost(flops, moved):
    return pl.CostEstimate(flops=flops, bytes_accessed=moved, transcendentals=0)


def rcp(v):
    return pl.reciprocal(v, approx=True)


def flux(d):
    mu = 1.0 + rcp(0.25 + d * d)
    return mu * d, mu


def z_flux(c):
    lane = lax.broadcasted_iota(jnp.int32, c.shape, c.ndim - 1)
    n = c.shape[-1]
    zl = jnp.where(lane == 0, 0.0, pltpu.roll(c, 1, c.ndim - 1))
    zr = jnp.where(lane == n - 1, 0.0, pltpu.roll(c, n - 1, c.ndim - 1))
    fl, ml = flux(zl - c)
    fr, mr = flux(zr - c)
    return fl + fr, ml + mr


def both(v):
    hi = v.astype(jnp.bfloat16).astype(jnp.float32)
    return jnp.concatenate([hi, v - hi], axis=0).astype(jnp.bfloat16)


def finish(c, numer, denom):
    return c + 0.8 * (numer * rcp(denom))


def relax_call(nx, ny, nz):
    chunk = UNIT
    rows = ny + 2 * TOP

    def kernel(flags, p_hbm, s_hbm, hlo, hhi, tlo, thi, own_lo, own_hi, kern, o_hbm, table,
               pe, q, sb, ob, fx1, mx1, fx2, mx2, fy1, my1, fy2, my2, psem, ssem, osem):
        n_chunk = nx // chunk

        def pcopy(c):
            return pltpu.make_async_copy(p_hbm.at[pl.ds(c * chunk, chunk)],
                                         pe.at[pl.ds(2 + c * chunk, chunk), pl.ds(TOP, ny)], psem.at[c])

        def scopy(c):
            return pltpu.make_async_copy(s_hbm.at[pl.ds(c * chunk, chunk)],
                                         sb.at[pl.ds(1 + c * chunk, chunk)], ssem.at[c])

        def ocopy(c):
            return pltpu.make_async_copy(ob.at[pl.ds(c * chunk + UNIT, chunk)],
                                         o_hbm.at[pl.ds(c * chunk, chunk)], osem.at[c])

        for c in range(n_chunk):
            pcopy(c).start()
            scopy(c).start()

        has = [flags[n] > 0 for n in range(4)]

        def keep(flag, v):
            return jnp.where(flag, v, 0.0)

        main = pl.ds(TOP, ny)
        for at, ref, first in ((0, hlo, 0), (1, hlo, ny), (nx + 2, hhi, 0), (nx + 3, hhi, ny)):
            pe[at, main, :] = keep(has[0 if at < 2 else 1], ref[pl.ds(first, ny), :])
        sb[0, :, :] = hlo[pl.ds(2 * ny, ny), :]
        sb[nx + 1, :, :] = hhi[pl.ds(2 * ny, ny), :]
        pe2 = pe.reshape((nx + 4) * rows, nz)
        q2 = q.reshape((nx + 2) * rows, nz)
        for side, (ref, own, row) in enumerate(((tlo, own_lo, TOP - 1), (thi, own_hi, TOP + ny))):
            flag = has[2 + side]
            c = keep(flag, ref[pl.ds(0, nx), :])
            far = keep(flag, ref[pl.ds(nx, nx), :])
            src = ref[pl.ds(2 * nx, nx), :]
            near = own[pl.ds(0, nx), :]
            corners = keep(flag, ref[pl.ds(3 * nx, 8), :])
            below = keep(has[0], corners[0:1])
            above = keep(has[1], corners[1:2])
            ix = lax.broadcasted_iota(jnp.int32, c.shape, 0)
            xl = jnp.where(ix == 0, below, pltpu.roll(c, 1, 0))
            xr = jnp.where(ix == nx - 1, above, pltpu.roll(c, nx - 1, 0))
            numer, denom = z_flux(c)
            numer = numer + src
            denom = denom + 1.0
            for other in (far, near, xl, xr):
                f, mu = flux(other - c)
                numer = numer + f
                denom = denom + mu
            pe2[pl.ds(2 * rows + row, nx, stride=rows), :] = c
            pe2[pl.ds(rows + row, 1), :] = below
            pe2[pl.ds((nx + 2) * rows + row, 1), :] = above
            q2[pl.ds(rows + row, nx, stride=rows), :] = keep(flag, finish(c, numer, denom))

        def sweep(a, x, planes, fx, mx, fy, my, src, store):
            for u in range(planes):
                f, mu = flux(a[x + u, pl.ds(1, TOP), :] - a[x + u, pl.ds(0, TOP), :])
                fy[u, pl.ds(0, TOP), :] = f
                my[u, pl.ds(0, TOP), :] = mu
            for k in range(ny // STRIP):
                here = pl.ds(TOP + k * STRIP, STRIP)
                before = pl.ds(TOP + k * STRIP - 1, STRIP)
                after = pl.ds(TOP + k * STRIP + 1, STRIP)
                flat = pl.ds(k * STRIP, STRIP)
                c = a[x, here, :]
                fp = fx[flat, :]
                mp = mx[flat, :]
                for u in range(planes):
                    up = a[x + u + 1, here, :]
                    f, mu = flux(up - c)
                    numer = f - fp
                    denom = mu + mp
                    fp, mp = f, mu
                    f, mu = flux(a[x + u, after, :] - c)
                    fy[u, here, :] = f
                    my[u, here, :] = mu
                    numer = numer + (f - fy[u, before, :])
                    denom = denom + (mu + my[u, before, :])
                    f, mu = z_flux(c)
                    numer = numer + (f + src[u, flat, :])
                    denom = denom + (mu + 1.0)
                    store(u, k, finish(c, numer, denom))
                    c = up
                fx[flat, :] = fp
                mx[flat, :] = mp

        def first_x(a, x, fx, mx):
            for k in range(ny // STRIP):
                here = pl.ds(TOP + k * STRIP, STRIP)
                flat = pl.ds(k * STRIP, STRIP)
                f, mu = flux(a[x + 1, here, :] - a[x, here, :])
                fx[flat, :] = f
                mx[flat, :] = mu

        def sweep1(x, planes, flag=None):
            def store(u, k, v):
                q[x + u + 1, pl.ds(TOP + k * STRIP, STRIP), :] = v if flag is None else keep(flag, v)

            sweep(pe, x + 2, planes, fx1, mx1, fy1, my1, sb.at[pl.ds(x + 1, planes)], store)

        kk = both(kern[...])

        def sweep2(x, planes):
            def store(u, k, v):
                ob[x + u + UNIT, pl.ds(k * STRIP, STRIP), :] = v

            sweep(q, x + 1, planes, fx2, mx2, fy2, my2, sb.at[pl.ds(x + 1, planes)], store)

        def surface(x, planes):
            nt = (((1,), (1,)), ((), ()))
            for u in range(planes):
                v = ob[x + u + UNIT]
                hi = v.astype(jnp.bfloat16)
                lo = (v - hi.astype(jnp.float32)).astype(jnp.bfloat16)
                a = lax.dot_general(kk, hi, nt, preferred_element_type=jnp.float32)
                b = lax.dot_general(kk, lo, nt, preferred_element_type=jnp.float32)
                table[x + u + UNIT] = (a[8:16] + b[0:8]) + a[0:8]

        n_unit = nx // UNIT
        pcopy(0).wait()
        scopy(0).wait()
        first_x(pe, 0, fx1, mx1)
        sweep1(-1, 1, has[0])
        sweep1(0, 1)
        first_x(q, 0, fx2, mx2)
        pcopy(1).wait()
        scopy(1).wait()
        sweep1(1, UNIT)

        def body(b, _):
            @pl.when(b < n_unit - 1)
            def _():
                pcopy(b + 1).wait()
                scopy(b + 1).wait()

            surface((b - 2) * UNIT, UNIT)
            sweep2((b - 1) * UNIT, UNIT)
            sweep1(b * UNIT + 1, UNIT)
            ocopy(b - 1).start()
            return 0

        lax.fori_loop(1, n_unit, body, 0)

        @pl.when(jnp.logical_not(has[1]))
        def _():
            q[nx + 1] = jnp.zeros_like(q[nx + 1])

        surface(nx - 2 * UNIT, UNIT)
        sweep2(nx - UNIT, UNIT)
        ocopy(n_unit - 1).start()
        surface(nx - UNIT, UNIT)
        for c in range(n_chunk):
            ocopy(c).wait()

    f32 = jnp.float32
    vm = pl.BlockSpec(memory_space=pltpu.VMEM)
    hbm = pl.BlockSpec(memory_space=pl.ANY)
    plane = pltpu.VMEM((ny, nz), f32)
    edge = pltpu.VMEM((UNIT, rows, nz), f32)
    return pl.pallas_call(
        kernel,
        out_shape=(jax.ShapeDtypeStruct((nx, ny, nz), f32), jax.ShapeDtypeStruct((nx + UNIT, 8, ny), f32)),
        in_specs=[pl.BlockSpec(memory_space=pltpu.SMEM), hbm, hbm] + [vm] * 7,
        out_specs=(hbm, vm),
        scratch_shapes=[
            pltpu.VMEM((nx + 4, rows, nz), f32), pltpu.VMEM((nx + 2, rows, nz), f32),
            pltpu.VMEM((nx + 2, ny, nz), f32), pltpu.VMEM((nx + UNIT, ny, nz), f32),
            plane, plane, plane, plane, edge, edge, edge, edge,
            pltpu.SemaphoreType.DMA((nx // chunk,)), pltpu.SemaphoreType.DMA((nx // chunk,)),
            pltpu.SemaphoreType.DMA((nx // chunk,)),
        ],
        compiler_params=pltpu.CompilerParams(vmem_limit_bytes=40 * 2**20),
        cost_estimate=pl.CostEstimate(flops=nx * ny * nz * 100, bytes_accessed=nx * ny * nz * 12, transcendentals=nx * ny * nz * 10),
        name="relax",
    )


def pack_call(nx, ny, nz, n_tiles):
    def kernel(p_hbm, s_hbm, m_ref, head_lo, head_hi, track_lo, track_hi, p_lo, p_hi, s_lo, s_hi, sem):
        planes = [
            (p_hbm, 0, head_lo, 0), (p_hbm, 1, head_lo, 1), (s_hbm, 0, head_lo, 2),
            (p_hbm, nx - 2, head_hi, 0), (p_hbm, nx - 1, head_hi, 1), (s_hbm, nx - 1, head_hi, 2),
        ]
        copies = [
            pltpu.make_async_copy(src.at[at], dst.at[pl.ds(n * ny, ny)], sem.at[i])
            for i, (src, at, dst, n) in enumerate(planes)
        ]
        rows = [(p_hbm, 0, p_lo), (p_hbm, ny - 8, p_hi), (s_hbm, 0, s_lo), (s_hbm, ny - 8, s_hi)]
        copies += [
            pltpu.make_async_copy(src.at[:, pl.ds(at, 8)], dst, sem.at[6 + i])
            for i, (src, at, dst) in enumerate(rows)
        ]
        for copy in copies:
            copy.start()
        head_lo[pl.ds(3 * ny, 8), :] = jnp.zeros((8, nz), F32)
        head_hi[pl.ds(3 * ny, 8), :] = jnp.zeros((8, nz), F32)
        for c in range(3):
            head_lo[pl.ds(3 * ny + c, 1), :] = m_ref[pl.ds(c * n_tiles, 1), :]
            head_hi[pl.ds(3 * ny + c, 1), :] = m_ref[pl.ds((c + 1) * n_tiles - 1, 1), :]
        for copy in copies[6:]:
            copy.wait()
        for out, p_ref, s_ref, order in ((track_lo, p_lo, s_lo, (0, 1)), (track_hi, p_hi, s_hi, (7, 6))):
            p2 = p_ref.reshape(nx * 8, nz)
            s2 = s_ref.reshape(nx * 8, nz)
            out[pl.ds(0, nx), :] = p2[pl.ds(order[0], nx, stride=8), :]
            out[pl.ds(nx, nx), :] = p2[pl.ds(order[1], nx, stride=8), :]
            out[pl.ds(2 * nx, nx), :] = s2[pl.ds(order[0], nx, stride=8), :]
            out[pl.ds(3 * nx, 8), :] = jnp.zeros((8, nz), F32)
        for copy in copies[:6]:
            copy.wait()

    head = jax.ShapeDtypeStruct((3 * ny + 8, nz), F32)
    track = jax.ShapeDtypeStruct((3 * nx + 8, nz), F32)
    eight = pltpu.VMEM((nx, 8, nz), F32)
    return pl.pallas_call(
        kernel,
        out_shape=(head, head, track, track),
        in_specs=[ANY, ANY, VM],
        out_specs=(VM,) * 4,
        scratch_shapes=[eight] * 4 + [pltpu.SemaphoreType.DMA((10,))],
        compiler_params=pltpu.CompilerParams(vmem_limit_bytes=16 * 2**20),
        cost_estimate=cost(10**6, 4 * 2**20),
        name="pack",
    )


def corner_call(nx, ny, nz):
    def kernel(lo_in, hi_in, below, above, lo, hi):
        for src, dst, row in ((lo_in, lo, 0), (hi_in, hi, ny - 1)):
            dst[pl.ds(0, 3 * nx), :] = src[pl.ds(0, 3 * nx), :]
            dst[pl.ds(3 * nx, 8), :] = jnp.zeros((8, nz), F32)
            dst[pl.ds(3 * nx, 1), :] = below[pl.ds(ny + row, 1), :]
            dst[pl.ds(3 * nx + 1, 1), :] = above[pl.ds(row, 1), :]

    track = jax.ShapeDtypeStruct((3 * nx + 8, nz), F32)
    return pl.pallas_call(
        kernel, out_shape=(track, track), in_specs=[VM] * 4, out_specs=(VM, VM),
        compiler_params=pltpu.CompilerParams(vmem_limit_bytes=16 * 2**20),
        cost_estimate=cost(10**5, 2**20), name="corners",
    )


def request_call(n_track, n_tiles, cells, width, cap):
    slot_rows = n_track * cap // LANES

    def kernel(foot, index, profile, requests, slots, target):
        fp = foot[...]
        owner = lax.shift_right_logical(fp, int(math.log2(cells)))
        cell = fp & (cells - 1)
        marks = [(owner == o).astype(F32) for o in range(n_track)]
        stacked = jnp.concatenate(marks, axis=0).astype(BF16)
        row = lax.broadcasted_iota(jnp.int32, (LANES, LANES), 0)
        col = lax.broadcasted_iota(jnp.int32, (LANES, LANES), 1)
        within = mm(stacked, (row < col).astype(F32).astype(BF16))
        totals = mm(stacked, jnp.ones((LANES, LANES), BF16)).astype(BF16)
        t_row = lax.broadcasted_iota(jnp.int32, (n_tiles, n_tiles), 0)
        t_col = lax.broadcasted_iota(jnp.int32, (n_tiles, n_tiles), 1)
        lower = (t_col < t_row).astype(F32).astype(BF16)
        rank = jnp.zeros((n_tiles, LANES), F32)
        for o in range(n_track):
            part = slice(o * n_tiles, (o + 1) * n_tiles)
            rank = rank + marks[o] * (within[part] + mm(lower, totals[part]))
        slot = owner * cap + rank.astype(jnp.int32)
        slots[...] = slot
        at_row = lax.shift_right_logical(slot, int(math.log2(LANES)))
        at_lane = slot & (LANES - 1)
        high = lax.shift_right_logical(cell, int(math.log2(width))).astype(F32)
        low = (cell & (width - 1)).astype(F32)
        rows = lax.broadcasted_iota(jnp.int32, (slot_rows, LANES), 0)
        found = jnp.zeros((2 * slot_rows, LANES), F32)
        for k in range(n_tiles):
            here = rows == at_row[k : k + 1]
            values = jnp.concatenate(
                [jnp.where(here, high[k : k + 1], 0.0), jnp.where(here, low[k : k + 1], 0.0)], axis=0
            ).astype(BF16)
            lanes = (row == at_lane[k : k + 1]).astype(F32).astype(BF16)
            found = found + mm_nt(values, lanes)
        requests[...] = found[:slot_rows] * float(width) + found[slot_rows:]
        spread = jnp.broadcast_to(profile[...], (n_tiles, profile.shape[1]))
        temp = jnp.take_along_axis(spread, index[...], axis=1)
        target[...] = 0.05 + jnp.maximum(1.0 - temp, 0.0)

    tiles = (n_tiles, LANES)
    return pl.pallas_call(
        kernel,
        out_shape=(
            jax.ShapeDtypeStruct((slot_rows, LANES), F32),
            jax.ShapeDtypeStruct(tiles, jnp.int32),
            jax.ShapeDtypeStruct(tiles, F32),
        ),
        in_specs=[VM] * 3,
        out_specs=(VM,) * 3,
        compiler_params=pltpu.CompilerParams(vmem_limit_bytes=16 * 2**20),
        cost_estimate=cost(10**8, 2**20),
        name="requests",
    )


def look_up(table, lane, row, rows, width):
    n = lane.shape[1]
    here = (lax.broadcasted_iota(jnp.int32, (width, n), 0) == lane).astype(F32).astype(BF16)
    got = mm(table, jnp.concatenate([here, here], axis=0))
    mine = lax.broadcasted_iota(jnp.int32, (rows, n), 0) == row
    return [
        jnp.sum(jnp.where(mine, got[c * rows : (c + 1) * rows], 0.0), axis=0, keepdims=True) for c in range(3)
    ]


def answer_call(n_track, cap, nx, ny):
    per = cap // LANES

    def kernel(requests, surface, reply, parts):
        flat = surface.reshape(surface.shape[0] * 8, ny)
        for c in range(3):
            hi, lo = split(flat[pl.ds((surface.shape[0] - nx) * 8 + c, nx, stride=8), :])
            parts[pl.ds(c * nx, nx), pl.ds(0, ny)] = hi
            parts[pl.ds(c * nx, nx), pl.ds(ny, ny)] = lo
        table = parts[...]
        group = 8 // per if per < 8 else 1

        def body(o, _):
            asked = requests[pl.ds(pl.multiple_of(o * group * per, 8), group * per), :].astype(jnp.int32)
            at_row = lax.shift_right_logical(asked, int(math.log2(ny)))
            at_lane = asked & (ny - 1)
            for j in range(group * per):
                values = look_up(table, at_lane[j : j + 1], at_row[j : j + 1], nx, ny)
                for c in range(3):
                    reply[o * group + j // per, pl.ds(c * per + j % per, 1), :] = values[c]
            return 0

        lax.fori_loop(0, n_track // group, body, 0)

    return pl.pallas_call(
        kernel,
        out_shape=jax.ShapeDtypeStruct((n_track, 3 * per, LANES), F32),
        in_specs=[VM, VM],
        out_specs=VM,
        scratch_shapes=[pltpu.VMEM((3 * nx, 2 * ny), BF16)],
        compiler_params=pltpu.CompilerParams(vmem_limit_bytes=16 * 2**20),
        cost_estimate=cost(10**9, 2**20),
        name="answer",
    )


def llb(m, field, target):
    sq = m[0] * m[0] + m[1] * m[1] + m[2] * m[2]
    pull = 0.5 * (1.0 - sq / target)
    h = [field[c] + pull * m[c] for c in range(3)]

    def cross(a, b):
        return [a[(c + 1) % 3] * b[(c + 2) % 3] - a[(c + 2) % 3] * b[(c + 1) % 3] for c in range(3)]

    turn = cross(m, h)
    damp = cross(m, turn)
    along = m[0] * h[0] + m[1] * h[1] + m[2] * h[2]
    return [m[c] + 0.1 * (0.3 * along * m[c] - turn[c] - 0.5 * damp[c]) for c in range(3)]


def fold(by_hi, by_lo):
    return (by_hi[8:16] + by_lo[0:8]) + by_hi[0:8]


def tile_major(m_ref, tiles_ref, n_tiles):
    tiles_ref[...] = jnp.zeros_like(tiles_ref)
    flat = tiles_ref.reshape((n_tiles + 2) * 8, LANES)
    for c in range(3):
        flat[pl.ds(8 + c, n_tiles, stride=8), :] = m_ref[pl.ds(c * n_tiles, n_tiles), :]


def exchange(tiles_ref, pair_hi, pair_lo, out_ref, k, n_tiles, at):
    mid = both(tiles_ref[k + 1])
    low = both(tiles_ref[k])
    high = both(tiles_ref[k + 2])
    here = jnp.concatenate([mid, low], axis=1)
    hi = pair_hi[at]
    lo = pair_lo[at]
    field = fold(mm_nt(here, hi), mm_nt(here, lo))
    field = field + fold(mm(high, hi[:, LANES:]), mm(high, lo[:, LANES:]))
    for c in range(3):
        out_ref[pl.ds(c * n_tiles + k, 1), :] = field[c : c + 1]


def first_call(n_tiles, ny):
    step = 8

    def kernel(flags, own, nxt, m_ref, below, above, pair_hi, pair_lo, ex, tiles):
        i = pl.program_id(0)

        @pl.when(i == 0)
        def _():
            tile_major(m_ref, tiles, n_tiles)
            tiles[0] = jnp.where(flags[0] > 0, below[pl.ds(3 * ny, 8), :], 0.0)
            tiles[n_tiles + 1] = jnp.where(flags[1] > 0, above[pl.ds(3 * ny, 8), :], 0.0)

        for j in range(step):
            for ref, lanes in ((own, pl.ds(0, LANES)), (nxt, pl.ds(LANES, LANES))):
                hi, lo = split(ref[j])
                pair_hi[j, :, lanes] = hi
                pair_lo[j, :, lanes] = lo
        for j in range(step):
            exchange(tiles, pair_hi, pair_lo, ex, i * step + j, n_tiles, j)

    tile = pl.BlockSpec((step, LANES, LANES), lambda i: (i, 0, 0))
    pair = pl.BlockSpec((step, LANES, 2 * LANES), lambda i: (i, 0, 0))
    return pl.pallas_call(
        kernel,
        grid=(n_tiles // step,),
        out_shape=(
            jax.ShapeDtypeStruct((n_tiles, LANES, 2 * LANES), BF16),
            jax.ShapeDtypeStruct((n_tiles, LANES, 2 * LANES), BF16),
            jax.ShapeDtypeStruct((3 * n_tiles, LANES), F32),
        ),
        in_specs=[SM, tile, tile, VM, VM, VM],
        out_specs=(pair, pair, VM),
        scratch_shapes=[pltpu.VMEM((n_tiles + 2, 8, LANES), F32)],
        compiler_params=pltpu.CompilerParams(vmem_limit_bytes=24 * 2**20),
        cost_estimate=cost(10**9, 8 * 2**20),
        name="couple_first",
    )


def section_call(n_tiles, n_track, cap):
    per = cap // LANES
    slot_rows = n_track * per

    def kernel(answers, slots, m_ref, ex, target, applied, m_out, edge_lo, edge_hi, parts):
        for c in range(3):
            rows = jnp.concatenate([answers[o, pl.ds(c * per, per), :] for o in range(n_track)], axis=0)
            hi, lo = split(rows)
            parts[pl.ds(c * slot_rows, slot_rows), pl.ds(0, LANES)] = hi
            parts[pl.ds(c * slot_rows, slot_rows), pl.ds(LANES, LANES)] = lo
        table = parts[...]
        slot = slots[...]
        at_row = lax.shift_right_logical(slot, int(math.log2(LANES)))
        at_lane = slot & (LANES - 1)
        for k in range(n_tiles):
            values = look_up(table, at_lane[k : k + 1], at_row[k : k + 1], slot_rows, LANES)
            for c in range(3):
                applied[pl.ds(c * n_tiles + k, 1), :] = values[c]
        part = [pl.ds(c * n_tiles, n_tiles) for c in range(3)]
        m = [m_ref[part[c], :] for c in range(3)]
        m = llb(m, [applied[part[c], :] + ex[part[c], :] for c in range(3)], target[...])
        edge_lo[...] = jnp.zeros((8, LANES), F32)
        edge_hi[...] = jnp.zeros((8, LANES), F32)
        for c in range(3):
            m_out[part[c], :] = m[c]
            edge_lo[pl.ds(c, 1), :] = m[c][0:1]
            edge_hi[pl.ds(c, 1), :] = m[c][n_tiles - 1 :]

    grains = jax.ShapeDtypeStruct((3 * n_tiles, LANES), F32)
    edge = jax.ShapeDtypeStruct((8, LANES), F32)
    return pl.pallas_call(
        kernel,
        out_shape=(grains, grains, edge, edge),
        in_specs=[VM] * 5,
        out_specs=(VM,) * 4,
        scratch_shapes=[pltpu.VMEM((3 * slot_rows, 2 * LANES), BF16)],
        compiler_params=pltpu.CompilerParams(vmem_limit_bytes=16 * 2**20),
        cost_estimate=cost(10**9, 2**20),
        name="section_first",
    )


def second_call(n_tiles):
    def kernel(pair_hi, pair_lo, m_ref, ex, tiles):
        tile_major(m_ref, tiles, n_tiles)
        for k in range(n_tiles):
            exchange(tiles, pair_hi, pair_lo, ex, k, n_tiles, k)

    return pl.pallas_call(
        kernel,
        out_shape=jax.ShapeDtypeStruct((3 * n_tiles, LANES), F32),
        in_specs=[VM] * 3,
        out_specs=VM,
        scratch_shapes=[pltpu.VMEM((n_tiles + 2, 8, LANES), F32)],
        compiler_params=pltpu.CompilerParams(vmem_limit_bytes=24 * 2**20),
        cost_estimate=cost(10**9, 4 * 2**20),
        name="couple_second",
    )


def last_call(n_tiles):
    def kernel(flags, m_ref, ex, applied, target, below, above, hi_first, lo_first, hi_last, lo_last, out):
        low = both(jnp.where(flags[0] > 0, below[...], 0.0))
        high = both(jnp.where(flags[1] > 0, above[...], 0.0))
        beside = slice(LANES, 2 * LANES)
        first = fold(mm_nt(low, hi_first[0][:, beside]), mm_nt(low, lo_first[0][:, beside]))
        last = fold(mm(high, hi_last[0][:, beside]), mm(high, lo_last[0][:, beside]))
        at = lax.broadcasted_iota(jnp.int32, (n_tiles, LANES), 0)
        field = []
        m = []
        for c in range(3):
            part = pl.ds(c * n_tiles, n_tiles)
            extra = jnp.where(at == 0, first[c : c + 1], 0.0) + jnp.where(at == n_tiles - 1, last[c : c + 1], 0.0)
            field.append(applied[part, :] + (ex[part, :] + extra))
            m.append(m_ref[part, :])
        m = llb(m, field, target[...])
        for c in range(3):
            out[pl.ds(c * n_tiles, n_tiles), :] = m[c]

    def at(k):
        return pl.BlockSpec((1, LANES, 2 * LANES), lambda i: (k, 0, 0))

    def full(shape):
        return pl.BlockSpec(shape, lambda i: (0, 0))

    grains = full((3 * n_tiles, LANES))
    edge = full((8, LANES))
    return pl.pallas_call(
        kernel,
        grid=(1,),
        out_shape=jax.ShapeDtypeStruct((3 * n_tiles, LANES), F32),
        in_specs=[SM, grains, grains, grains, full((n_tiles, LANES)), edge, edge,
                  at(0), at(0), at(n_tiles - 1), at(n_tiles - 1)],
        out_specs=grains,
        compiler_params=pltpu.CompilerParams(vmem_limit_bytes=16 * 2**20),
        cost_estimate=cost(10**7, 2**20),
        name="section_last",
    )


def shifted(v, axis, by):
    n = lax.axis_size(axis)
    return lax.ppermute(v, axis, [(i, (i + by) % n) for i in range(n)])


def per_device(
    potential, source, depth_kernel, magnet, footprint, temp_index, temp_profile, self_tiles, next_tiles
):
    nx, ny, nz = potential.shape
    n_track = lax.axis_size("track")
    n_tiles = self_tiles.shape[1]
    grains = footprint.shape[1]
    cap = 2 * grains // n_track
    h = lax.axis_index("head")
    t = lax.axis_index("track")
    flags = jnp.stack([h > 0, h < lax.axis_size("head") - 1, t > 0, t < n_track - 1]).astype(jnp.int32)
    state = magnet.reshape(3 * n_tiles, LANES)

    head_lo, head_hi, track_lo, track_hi = pack_call(nx, ny, nz, n_tiles)(potential, source, state)
    below = shifted(head_hi, "head", 1)
    above = shifted(head_lo, "head", -1)
    requests, slots, target = request_call(n_track, n_tiles, nx * ny, ny, cap)(
        footprint.reshape(n_tiles, LANES), temp_index.reshape(n_tiles, LANES), temp_profile[None, :]
    )
    track_lo, track_hi = corner_call(nx, ny, nz)(track_lo, track_hi, below, above)
    left = shifted(track_hi, "track", 1)
    right = shifted(track_lo, "track", -1)
    asked = lax.all_to_all(requests.reshape(n_track, cap // LANES, LANES), "track", 0, 0)

    kern = jnp.pad(depth_kernel, ((0, 5), (0, 0)))
    relaxed, surface = relax_call(nx, ny, nz)(
        flags, potential, source, below, above, left, right, track_lo, track_hi, kern
    )
    reply = answer_call(n_track, cap, nx, ny)(asked.reshape(n_track * cap // LANES, LANES), surface)
    answers = lax.all_to_all(reply, "track", 0, 0)

    pair_hi, pair_lo, ex = first_call(n_tiles, ny)(flags, self_tiles[0], next_tiles[0], state, below, above)
    applied, state, edge_lo, edge_hi = section_call(n_tiles, n_track, cap)(answers, slots, state, ex, target)
    tile_below = shifted(edge_hi, "head", 1)
    tile_above = shifted(edge_lo, "head", -1)
    ex = second_call(n_tiles)(pair_hi, pair_lo, state)
    state = last_call(n_tiles)(
        flags, state, ex, applied, target, tile_below, tile_above, pair_hi, pair_lo, pair_hi, pair_lo
    )
    return relaxed, state.reshape(3, 1, grains)


def solution(mesh):
    in_specs = (
        P("head", "track", None),
        P("head", "track", None),
        P(),
        P(None, "track", "head"),
        P("track", "head"),
        P("track", "head"),
        P(),
        P("track", "head", None, None),
        P("track", "head", None, None),
    )
    out_specs = (P("head", "track", None), P(None, "track", "head"))
    return jax.shard_map(
        per_device, mesh=mesh, in_specs=in_specs, out_specs=out_specs, check_vma=False
    )
```

time: 766 us -> 70.8 us (0.09)
  blocking collectives: 635 us -> 0 us
  Pallas kernels: 0 us -> 30.4 us
  other arithmetic: 29.8 us -> 0.08 us
  matrix products: 23.9 us -> 0 us
  local copies, waits for them, and re-layouts: 36.2 us -> 14.1 us
  starting transfers between devices: 32.5 us -> 20.5 us
    all_gather x1 -> x0, blocking collectives: 635 us -> none  [per_device(): table = lax.all_gather(surface, 'track', axis=1, tiled=True)]
    pallas_call x0 -> x9, Pallas kernels: none -> 30.4 us  [the longest x1 17.2 us: per_device(): relax_call(nx, ny, nz)]
    add x3 -> x0, other arithmetic: 27.6 us -> none  [the longest x2 26.7 us: relax_sweep(): return center + 0.8 * numer / denom]
    gather x2 -> x0, local copies, waits for them, and re-layouts: 26.9 us -> none  [per_device(): applied = jnp.take(table, cells, axis=1)]
    dot_general x8 -> x0, matrix products: 23.9 us -> none  [the longest x2 8.37 us: per_device(): ex = jnp.einsum('kij,ckj->cki', couple_self, tiles[:, 1:-1], precision=HIGH)]
    ppermute x12 -> x6, starting transfers between devices: 32.5 us -> 9.11 us  [shifted(): return lax.ppermute(v, axis, [(i, (i + by) % n) for i in range(n)])]
    all_to_all x0 -> x2, starting transfers between devices: none -> 11.4 us  [the longest x1 6.59 us: per_device(): lax.all_to_all(requests.reshape(n_track, cap // LANES, LANES), 'track', 0...]
    unnamed x19 -> x28, local copies, waits for them, and re-layouts: 5.51 us -> 14.1 us
  transfers between devices with their start and end apart: 12 -> 8, of which waited for: 2 -> 2; matrix products, arithmetic and copies ran while one was open for 3% -> 0% of each run, Pallas kernels for 0% -> 34%
where the time goes in v1:
time: 70.8 us; the launch traced here: 69.6 us
  Pallas kernels  30.4 us (43%)
  starting transfers between devices  20.5 us (29%)
  local copies, waits for them, and re-layouts  14.1 us (20%)
  waiting for transfers between devices  3.8 us (5%)
  between operations  0.77 us (1%)
    pallas_call x1, Pallas kernels, per_device(): relax_call(nx, ny, nz)  17.2 us
    unnamed x28, local copies, waits for them, and re-layouts  14.1 us
    ppermute x6, starting transfers between devices, shifted(): return lax.ppermute(v, axis, [(i, (i + by) % n) for i in range(n)])  9.11 us
    all_to_all x1, starting transfers between devices, per_device(): lax.all_to_all(requests.reshape(n_track, cap // LANES, LANES), 'track', 0...  6.59 us
    all_to_all x1, starting transfers between devices, per_device(): answers = lax.all_to_all(reply, 'track', 0, 0)  4.77 us
    ppermute x6, waiting for transfers between devices, shifted(): return lax.ppermute(v, axis, [(i, (i + by) % n) for i in range(n)])  3.79 us
    pallas_call x1, Pallas kernels, per_device(): answer_call(n_track, cap, nx, ny)  3.62 us
    pallas_call x1, Pallas kernels, per_device(): first_call(n_tiles, ny)  2.83 us
  transfers between devices with their start and end apart: 8, of which 2 were waited for; matrix products, arithmetic and copies ran while one was open for 0% of the time, Pallas kernels for 34%

profile of v1, /device:TPU:0, one launch (start us, length us, event | category | flops | bytes accessed | tf_op | source)
XLA Modules:
  0.0 69.6 jit_solution(6509022223765684819)
XLA Ops:
  0.6 2.2 %copy-done.2 = f32[64,128,128]{2,1,0:T(8,128)S(1)} copy-done((f32[64,128,128]{2,1,0:T(8,128)S(1)}, f32[64,128,128]{2,1,0:T(8,128)}, u32[]{:S(2)}) %copy-start.2) | copy-done | bytes 4194328
  2.8 2.2 %copy-done.4 = f32[64,128,128]{2,1,0:T(8,128)S(1)} copy-done((f32[64,128,128]{2,1,0:T(8,128)S(1)}, f32[64,128,128]{2,1,0:T(8,128)}, u32[]{:S(2)}) %copy-start.4) | copy-done | bytes 4194328
  5.0 0.8 %copy-done.8 = f32[3,1,4096]{2,1,0:T(1,128)S(1)} copy-done((f32[3,1,4096]{2,1,0:T(1,128)S(1)}, f32[3,1,4096]{2,1,0:T(1,128)}, u32[]{:S(2)}) %copy-start.8) | copy-done | bytes 49176
  5.8 0.8 %pack.1 = (f32[392,128]{1,0:T(8,128)S(1)}, f32[392,128]{1,0:T(8,128)S(1)}, f32[200,128]{1,0:T(8,128)S(1)}, f32[200,128]{1,0:T(8,128)S(1)}) custom-call(f32[64,128,128]{2,1,0:T(8,128)S(1)} %copy-done.2, f32[64,128,128]{2,1,0:T(8,128)S(1)} %copy-done.4, f32[96,128]{1,0:T(8,128)S(1)} %bitcast.15), custom_call_target="tpu_custom_call" | custom-call | flops 1000000 | bytes 4194304 | tf_op jit(solution)/shard_map/pack/pallas_call | solution.py:612
  7.1 2.0 %collective-permute-start.1 = (f32[392,128]{1,0:T(8,128)S(1)}, f32[392,128]{1,0:T(8,128)S(1)}, u32[]{:S(2)}, u32[]{:S(2)}) collective-permute-start(f32[392,128]{1,0:T(8,128)S(1)} %get-tuple-element.21), channel_id=1, source_target_pairs={{0,24},{8,0},{16,8},{24,16},{1,25},{9,1},{17,9},{25,17},{2,26},{10... | collective-permute-start | bytes 602120 | tf_op jit(solution)/shard_map/ppermute | solution.py:596
  9.1 1.8 %requests.1 = (f32[64,128]{1,0:T(8,128)}, s32[32,128]{1,0:T(8,128)S(1)}, f32[32,128]{1,0:T(8,128)S(1)}) custom-call(s32[32,128]{1,0:T(8,128)S(1)} %bitcast.19, s32[32,128]{1,0:T(8,128)S(1)} %bitcast.20, f32[1,128]{1,0:T(1,128)S(1)} %bitcast.21), custom_call_target="tpu_custom_call" | custom-call | flops 100000000 | bytes 1048576 | tf_op jit(solution)/shard_map/requests/pallas_call | solution.py:615
  10.9 6.6 %all-to-all-start = ((f32[8,8,128]{2,1,0:T(8,128)}), f32[8,8,128]{2,1,0:T(8,128)S(1)}, u32[]{:S(2)}, u32[]{:S(2)}) async-start(f32[8,8,128]{2,1,0:T(8,128)} %bitcast.8), calls=%async_computation | async-start | bytes 65536 | tf_op jit(solution)/shard_map/all_to_all | solution.py:621
  17.6 2.1 %collective-permute-start.2 = (f32[200,128]{1,0:T(8,128)S(1)}, f32[200,128]{1,0:T(8,128)S(1)}, u32[]{:S(2)}, u32[]{:S(2)}) collective-permute-start(f32[200,128]{1,0:T(8,128)S(1)} %get-tuple-element.24.own_hi), channel_id=1, source_target_pairs={{0,1},{1,2},{2,3},{3,4},{4,5},{5,6},{6,7},{7,0},{8,9},{9,10},{10,1... | collective-permute-start | bytes 307208 | tf_op jit(solution)/shard_map/ppermute | solution.py:596
  19.6 2.8 %collective-permute-start.3 = (f32[200,128]{1,0:T(8,128)S(1)}, f32[200,128]{1,0:T(8,128)S(1)}, u32[]{:S(2)}, u32[]{:S(2)}) collective-permute-start(f32[200,128]{1,0:T(8,128)S(1)} %get-tuple-element.25.own_lo), channel_id=1, source_target_pairs={{0,7},{1,0},{2,1},{3,2},{4,3},{5,4},{6,5},{7,6},{8,15},{9,8},{10,9... | collective-permute-start | bytes 307208 | tf_op jit(solution)/shard_map/ppermute | solution.py:596
  22.5 2.9 %collective-permute-done.2.tlo = f32[200,128]{1,0:T(8,128)S(1)} collective-permute-done((f32[200,128]{1,0:T(8,128)S(1)}, f32[200,128]{1,0:T(8,128)S(1)}, u32[]{:S(2)}, u32[]{:S(2)}) %collective-permute-start.2) | collective-permute-done | bytes 102432 | tf_op jit(solution)/shard_map/ppermute | solution.py:596
  25.4 0.8 %collective-permute-done.3.thi = f32[200,128]{1,0:T(8,128)S(1)} collective-permute-done((f32[200,128]{1,0:T(8,128)S(1)}, f32[200,128]{1,0:T(8,128)S(1)}, u32[]{:S(2)}, u32[]{:S(2)}) %collective-permute-start.3) | collective-permute-done | bytes 102432 | tf_op jit(solution)/shard_map/ppermute | solution.py:596
  26.2 2.2 %copy-done.3 = f32[64,128,128]{2,1,0:T(8,128)S(1)} copy-done((f32[64,128,128]{2,1,0:T(8,128)S(1)}, f32[64,128,128]{2,1,0:T(8,128)}, u32[]{:S(2)}) %copy-start.3) | copy-done | bytes 4194328
  28.4 2.2 %copy-done.5 = f32[64,128,128]{2,1,0:T(8,128)S(1)} copy-done((f32[64,128,128]{2,1,0:T(8,128)S(1)}, f32[64,128,128]{2,1,0:T(8,128)}, u32[]{:S(2)}) %copy-start.5) | copy-done | bytes 4194328
  30.6 17.2 %relax.1 = (f32[64,128,128]{2,1,0:T(8,128)}, f32[68,8,128]{2,1,0:T(8,128)S(1)}) custom-call(s32[4]{0:T(128)S(1)} %add_convert_fusion.flags, f32[64,128,128]{2,1,0:T(8,128)S(1)} %copy-done.3, f32[64,128,128]{2,1,0:T(8,128)S(1)} %copy-done.5, f32[392,128]{1,0:T(8,128)S(1)} %collective-permute-done.below.hlo, f32[392,128]{1,0:T(8,128)S(1)} %collective-permute-done.1.above.hhi, ...), custom_call_target="tpu_custom_call" | custom-call | flops 104857600 | bytes 12582912 | tf_op jit(solution)/shard_map/relax/pallas_call | solution.py:624
  47.9 3.6 %answer.1 = f32[8,24,128]{2,1,0:T(8,128)} custom-call(f32[64,128]{1,0:T(8,128)S(1)} %bitcast.18, f32[68,8,128]{2,1,0:T(8,128)S(1)} %get-tuple-element.28.surface), custom_call_target="tpu_custom_call" | custom-call | flops 1000000000 | bytes 1048576 | tf_op jit(solution)/shard_map/answer/pallas_call | solution.py:627
  51.5 4.8 %all-to-all-start.1 = ((f32[8,24,128]{2,1,0:T(8,128)}), f32[8,24,128]{2,1,0:T(8,128)S(1)}, u32[]{:S(2)}, u32[]{:S(2)}) async-start(f32[8,24,128]{2,1,0:T(8,128)} %answer.1), calls=%async_computation.1 | async-start | bytes 196608 | tf_op jit(solution)/shard_map/all_to_all | solution.py:628
  56.3 1.6 %copy-done.6 = f32[1,32,128,128]{3,2,1,0:T(8,128)S(1)} copy-done((f32[1,32,128,128]{3,2,1,0:T(8,128)S(1)}, f32[1,32,128,128]{3,2,1,0:T(8,128)}, u32[]{:S(2)}) %copy-start.6) | copy-done | bytes 2097176
  57.9 1.6 %copy-done.7 = f32[1,32,128,128]{3,2,1,0:T(8,128)S(1)} copy-done((f32[1,32,128,128]{3,2,1,0:T(8,128)S(1)}, f32[1,32,128,128]{3,2,1,0:T(8,128)}, u32[]{:S(2)}) %copy-start.7) | copy-done | bytes 2097176
  59.4 2.8 %couple_first.1 = (bf16[32,128,256]{2,1,0:T(8,128)(2,1)S(1)}, bf16[32,128,256]{2,1,0:T(8,128)(2,1)S(1)}, f32[96,128]{1,0:T(8,128)S(1)}) custom-call(s32[4]{0:T(128)S(1)} %add_convert_fusion.flags, f32[32,128,128]{2,1,0:T(8,128)S(1)} %bitcast.13, f32[32,128,128]{2,1,0:T(8,128)S(1)} %bitcast.14, f32[96,128]{1,0:T(8,128)S(1)} %bitcast.16, ...), custom_call_target="tpu_custom_call" | custom-call | flops 1000000000 | bytes 8388608 | tf_op jit(solution)/shard_map/couple_first/pallas_call | solution.py:630
  62.3 1.3 %copy-done = bf16[32,128,256]{2,1,0:T(8,128)(2,1)} copy-done((bf16[32,128,256]{2,1,0:T(8,128)(2,1)}, bf16[32,128,256]{2,1,0:T(8,128)(2,1)S(1)}, u32[]{:S(2)}) %copy-start) | copy-done | bytes 2097176
  63.6 1.0 %section_first.1 = (f32[96,128]{1,0:T(8,128)S(1)}, f32[96,128]{1,0:T(8,128)S(1)}, f32[8,128]{1,0:T(8,128)S(1)}, f32[8,128]{1,0:T(8,128)S(1)}) custom-call(f32[8,24,128]{2,1,0:T(8,128)S(1)} %all-to-all-done.1.answers, s32[32,128]{1,0:T(8,128)S(1)} %get-tuple-element.29.slots, f32[96,128]{1,0:T(8,128)S(1)} %bitcast.17, f32[96,128]{1,0:T(8,128)S(1)} %get-tuple-element.30.ex, ...), custom_call_target="tpu_custom_call" | custom-call | flops 1000000000 | bytes 1048576 | tf_op jit(solution)/shard_map/section_first/pallas_call | solution.py:631
  64.7 1.7 %collective-permute-start.5 = (f32[8,128]{1,0:T(8,128)S(1)}, f32[8,128]{1,0:T(8,128)S(1)}, u32[]{:S(2)}, u32[]{:S(2)}) collective-permute-start(f32[8,128]{1,0:T(8,128)S(1)} %get-tuple-element.37), channel_id=1, source_target_pairs={{0,24},{8,0},{16,8},{24,16},{1,25},{9,1},{17,9},{25,17},{2,26},{10... | collective-permute-start | bytes 12296 | tf_op jit(solution)/shard_map/ppermute | solution.py:596
  66.4 1.8 %couple_second.1.ex = f32[96,128]{1,0:T(8,128)S(1)} custom-call(bf16[32,128,256]{2,1,0:T(8,128)(2,1)S(1)} %get-tuple-element.33.pair_hi.hi_first.hi_last, bf16[32,128,256]{2,1,0:T(8,128)(2,1)S(1)} %copy-done.1, f32[96,128]{1,0:T(8,128)S(1)} %get-tuple-element.32.m_ref), custom_call_target="tpu_custom_call" | custom-call | flops 1000000000 | bytes 4194304 | tf_op jit(solution)/shard_map/couple_second/pallas_call | solution.py:634
  68.3 1.3 %section_last.1 = f32[96,128]{1,0:T(8,128)} custom-call(s32[4]{0:T(128)S(1)} %add_convert_fusion.flags, f32[96,128]{1,0:T(8,128)S(1)} %get-tuple-element.32.m_ref, f32[96,128]{1,0:T(8,128)S(1)} %couple_second.1.ex, f32[96,128]{1,0:T(8,128)S(1)} %get-tuple-element.35.applied, f32[32,128]{1,0:T(8,128)S(1)} %get-tuple-element.31.target, ...), custom_call_target="tpu_custom_call" | custom-call | flops 10000000 | bytes 1048576 | tf_op jit(solution)/shard_map/section_last/pallas_call | solution.py:635
  (31 shorter events, 0.7 us)
Async XLA Ops:
  0.6 2.2 %copy-start.2 = (f32[64,128,128]{2,1,0:T(8,128)S(1)}, f32[64,128,128]{2,1,0:T(8,128)}, u32[]{:S(2)}) copy-start(f32[64,128,128]{2,1,0:T(8,128)} %p_hbm.3) | copy-start | bytes 12582916
  2.8 2.2 %copy-start.4 = (f32[64,128,128]{2,1,0:T(8,128)S(1)}, f32[64,128,128]{2,1,0:T(8,128)}, u32[]{:S(2)}) copy-start(f32[64,128,128]{2,1,0:T(8,128)} %s_hbm.3) | copy-start | bytes 12582916
  5.0 0.8 %copy-start.8 = (f32[3,1,4096]{2,1,0:T(1,128)S(1)}, f32[3,1,4096]{2,1,0:T(1,128)}, u32[]{:S(2)}) copy-start(f32[3,1,4096]{2,1,0:T(1,128)} %param.12) | copy-start | bytes 147460
  5.8 3.3 %copy-start.10 = (s32[1,4096]{1,0:T(1,128)S(1)}, s32[1,4096]{1,0:T(1,128)}, u32[]{:S(2)}) copy-start(s32[1,4096]{1,0:T(1,128)} %param.13) | copy-start | bytes 49156
  5.8 3.3 %copy-start.11 = (s32[1,4096]{1,0:T(1,128)S(1)}, s32[1,4096]{1,0:T(1,128)}, u32[]{:S(2)}) copy-start(s32[1,4096]{1,0:T(1,128)} %param.14) | copy-start | bytes 49156
  5.8 3.3 %copy-start.12 = (f32[128]{0:T(128)S(1)}, f32[128]{0:T(128)}, u32[]{:S(2)}) copy-start(f32[128]{0:T(128)} %param.15) | copy-start | bytes 1540
  5.8 16.6 %copy-start.13 = (f32[3,128]{1,0:T(4,128)S(1)}, f32[3,128]{1,0:T(4,128)}, u32[]{:S(2)}) copy-start(f32[3,128]{1,0:T(4,128)} %param.11) | copy-start | bytes 4612
  6.6 10.9 %collective-permute-start = (f32[392,128]{1,0:T(8,128)S(1)}, f32[392,128]{1,0:T(8,128)S(1)}, u32[]{:S(2)}, u32[]{:S(2)}) collective-permute-start(f32[392,128]{1,0:T(8,128)S(1)} %get-tuple-element.20), channel_id=1, source_target_pairs={{0,8},{8,16},{16,24},{24,0},{1,9},{9,17},{17,25},{25,1},{2,10},{10... | collective-permute-start | bytes 602120 | tf_op jit(solution)/shard_map/ppermute | solution.py:596
  7.1 10.4 %collective-permute-start.1 = (f32[392,128]{1,0:T(8,128)S(1)}, f32[392,128]{1,0:T(8,128)S(1)}, u32[]{:S(2)}, u32[]{:S(2)}) collective-permute-start(f32[392,128]{1,0:T(8,128)S(1)} %get-tuple-element.21), channel_id=1, source_target_pairs={{0,24},{8,0},{16,8},{24,16},{1,25},{9,1},{17,9},{25,17},{2,26},{10... | collective-permute-start | bytes 602120 | tf_op jit(solution)/shard_map/ppermute | solution.py:596
  10.9 36.9 %all-to-all-start = ((f32[8,8,128]{2,1,0:T(8,128)}), f32[8,8,128]{2,1,0:T(8,128)S(1)}, u32[]{:S(2)}, u32[]{:S(2)}) async-start(f32[8,8,128]{2,1,0:T(8,128)} %bitcast.8), calls=%async_computation | async-start | bytes 65536 | tf_op jit(solution)/shard_map/all_to_all | solution.py:621
  17.6 7.9 %collective-permute-start.2 = (f32[200,128]{1,0:T(8,128)S(1)}, f32[200,128]{1,0:T(8,128)S(1)}, u32[]{:S(2)}, u32[]{:S(2)}) collective-permute-start(f32[200,128]{1,0:T(8,128)S(1)} %get-tuple-element.24.own_hi), channel_id=1, source_target_pairs={{0,1},{1,2},{2,3},{3,4},{4,5},{5,6},{6,7},{7,0},{8,9},{9,10},{10,1... | collective-permute-start | bytes 307208 | tf_op jit(solution)/shard_map/ppermute | solution.py:596
  19.6 6.6 %collective-permute-start.3 = (f32[200,128]{1,0:T(8,128)S(1)}, f32[200,128]{1,0:T(8,128)S(1)}, u32[]{:S(2)}, u32[]{:S(2)}) collective-permute-start(f32[200,128]{1,0:T(8,128)S(1)} %get-tuple-element.25.own_lo), channel_id=1, source_target_pairs={{0,7},{1,0},{2,1},{3,2},{4,3},{5,4},{6,5},{7,6},{8,15},{9,8},{10,9... | collective-permute-start | bytes 307208 | tf_op jit(solution)/shard_map/ppermute | solution.py:596
  26.2 2.2 %copy-start.3 = (f32[64,128,128]{2,1,0:T(8,128)S(1)}, f32[64,128,128]{2,1,0:T(8,128)}, u32[]{:S(2)}) copy-start(f32[64,128,128]{2,1,0:T(8,128)} %p_hbm.3) | copy-start | bytes 12582916
  28.4 2.2 %copy-start.5 = (f32[64,128,128]{2,1,0:T(8,128)S(1)}, f32[64,128,128]{2,1,0:T(8,128)}, u32[]{:S(2)}) copy-start(f32[64,128,128]{2,1,0:T(8,128)} %s_hbm.3) | copy-start | bytes 12582916
  47.8 8.4 %copy-start.9 = (f32[3,1,4096]{2,1,0:T(1,128)S(1)}, f32[3,1,4096]{2,1,0:T(1,128)}, u32[]{:S(2)}) copy-start(f32[3,1,4096]{2,1,0:T(1,128)} %param.12) | copy-start | bytes 147460
  51.5 12.2 %all-to-all-start.1 = ((f32[8,24,128]{2,1,0:T(8,128)}), f32[8,24,128]{2,1,0:T(8,128)S(1)}, u32[]{:S(2)}, u32[]{:S(2)}) async-start(f32[8,24,128]{2,1,0:T(8,128)} %answer.1), calls=%async_computation.1 | async-start | bytes 196608 | tf_op jit(solution)/shard_map/all_to_all | solution.py:628
  56.3 1.6 %copy-start.6 = (f32[1,32,128,128]{3,2,1,0:T(8,128)S(1)}, f32[1,32,128,128]{3,2,1,0:T(8,128)}, u32[]{:S(2)}) copy-start(f32[1,32,128,128]{3,2,1,0:T(8,128)} %param.16) | copy-start | bytes 6291460
  57.9 1.6 %copy-start.7 = (f32[1,32,128,128]{3,2,1,0:T(8,128)S(1)}, f32[1,32,128,128]{3,2,1,0:T(8,128)}, u32[]{:S(2)}) copy-start(f32[1,32,128,128]{3,2,1,0:T(8,128)} %param.17) | copy-start | bytes 6291460
  62.3 1.4 %copy-start = (bf16[32,128,256]{2,1,0:T(8,128)(2,1)}, bf16[32,128,256]{2,1,0:T(8,128)(2,1)S(1)}, u32[]{:S(2)}) copy-start(bf16[32,128,256]{2,1,0:T(8,128)(2,1)S(1)} %get-tuple-element.34.pair_lo.lo_first.lo_last) | copy-start | bytes 6291460
  63.6 2.8 %copy-start.1 = (bf16[32,128,256]{2,1,0:T(8,128)(2,1)S(1)}, bf16[32,128,256]{2,1,0:T(8,128)(2,1)}, u32[]{:S(2)}) copy-start(bf16[32,128,256]{2,1,0:T(8,128)(2,1)} %copy-done) | copy-start | bytes 6291460
  64.6 3.6 %collective-permute-start.4 = (f32[8,128]{1,0:T(8,128)S(1)}, f32[8,128]{1,0:T(8,128)S(1)}, u32[]{:S(2)}, u32[]{:S(2)}) collective-permute-start(f32[8,128]{1,0:T(8,128)S(1)} %get-tuple-element.36), channel_id=1, source_target_pairs={{0,8},{8,16},{16,24},{24,0},{1,9},{9,17},{17,25},{25,1},{2,10},{10... | collective-permute-start | bytes 12296 | tf_op jit(solution)/shard_map/ppermute | solution.py:596
  64.7 3.6 %collective-permute-start.5 = (f32[8,128]{1,0:T(8,128)S(1)}, f32[8,128]{1,0:T(8,128)S(1)}, u32[]{:S(2)}, u32[]{:S(2)}) collective-permute-start(f32[8,128]{1,0:T(8,128)S(1)} %get-tuple-element.37), channel_id=1, source_target_pairs={{0,24},{8,0},{16,8},{24,16},{1,25},{9,1},{17,9},{25,17},{2,26},{10... | collective-permute-start | bytes 12296 | tf_op jit(solution)/shard_map/ppermute | solution.py:596

commit v2 on v1

--- a/solution.py
+++ b/solution.py
@@ -12,11 +12,14 @@
 STRIP = 16
 UNIT = 4
 TOP = 8
+AHEAD = 4
 LANES = 128
+SMALL = 16 * 2**20
+LARGE = 52 * 2**20
 NT = (((1,), (1,)), ((), ()))
 VM = pl.BlockSpec(memory_space=pltpu.VMEM)
 SM = pl.BlockSpec(memory_space=pltpu.SMEM)
-ANY = pl.BlockSpec(memory_space=pl.ANY)
+HBM = pl.BlockSpec(memory_space=pltpu.HBM)
 
 
 def mm(a, b):
@@ -64,12 +67,13 @@
     return c + 0.8 * (numer * rcp(denom))
 
 
-def relax_call(nx, ny, nz):
+def relax_call(nx, ny, nz, n_track, cap):
     chunk = UNIT
+    per = cap // LANES
     rows = ny + 2 * TOP
 
-    def kernel(flags, p_hbm, s_hbm, hlo, hhi, tlo, thi, own_lo, own_hi, kern, o_hbm, table,
-               pe, q, sb, ob, fx1, mx1, fx2, mx2, fy1, my1, fy2, my2, psem, ssem, osem):
+    def kernel(flags, p_hbm, s_hbm, hlo, hhi, tlo, thi, own_lo, own_hi, kern, requests, ex_hbm, o_hbm, reply,
+               table, parts, pe, q, sb, ob, fx1, mx1, fx2, mx2, fy1, my1, fy2, my2, psem, ssem, osem):
         n_chunk = nx // chunk
 
         def pcopy(c):
@@ -84,9 +88,12 @@
             return pltpu.make_async_copy(ob.at[pl.ds(c * chunk + UNIT, chunk)],
                                          o_hbm.at[pl.ds(c * chunk, chunk)], osem.at[c])
 
-        for c in range(n_chunk):
+        def fetch(c):
             pcopy(c).start()
             scopy(c).start()
+
+        for c in range(AHEAD):
+            fetch(c)
 
         has = [flags[n] > 0 for n in range(4)]
 
@@ -200,6 +207,10 @@
         sweep1(1, UNIT)
 
         def body(b, _):
+            @pl.when(b + AHEAD <= n_unit)
+            def _():
+                fetch(b + AHEAD - 1)
+
             @pl.when(b < n_unit - 1)
             def _():
                 pcopy(b + 1).wait()
@@ -221,34 +232,51 @@
         sweep2(nx - UNIT, UNIT)
         ocopy(n_unit - 1).start()
         surface(nx - UNIT, UNIT)
+
+        flat = table.reshape((nx + UNIT) * 8, ny)
+        for c in range(3):
+            hi, lo = split(flat[pl.ds(UNIT * 8 + c, nx, stride=8), :])
+            parts[pl.ds(c * nx, nx), pl.ds(0, ny)] = hi
+            parts[pl.ds(c * nx, nx), pl.ds(ny, ny)] = lo
+        asked = requests[...].astype(jnp.int32)
+
+        def answer(j, values):
+            for c in range(3):
+                reply[j // per, pl.ds(c * per + j % per, 1), :] = values[c]
+
+        look_up_all(parts[...], asked & (ny - 1), lax.shift_right_logical(asked, int(math.log2(ny))), nx, ny, answer)
         for c in range(n_chunk):
             ocopy(c).wait()
 
     f32 = jnp.float32
     vm = pl.BlockSpec(memory_space=pltpu.VMEM)
-    hbm = pl.BlockSpec(memory_space=pl.ANY)
+    hbm = pl.BlockSpec(memory_space=pltpu.HBM)
     plane = pltpu.VMEM((ny, nz), f32)
     edge = pltpu.VMEM((UNIT, rows, nz), f32)
     return pl.pallas_call(
         kernel,
-        out_shape=(jax.ShapeDtypeStruct((nx, ny, nz), f32), jax.ShapeDtypeStruct((nx + UNIT, 8, ny), f32)),
-        in_specs=[pl.BlockSpec(memory_space=pltpu.SMEM), hbm, hbm] + [vm] * 7,
+        out_shape=(
+            jax.ShapeDtypeStruct((nx, ny, nz), f32),
+            jax.ShapeDtypeStruct((n_track, 3 * per, 128), f32),
+        ),
+        in_specs=[pl.BlockSpec(memory_space=pltpu.SMEM), hbm, hbm] + [vm] * 8 + [pl.BlockSpec(memory_space=pl.ANY)],
         out_specs=(hbm, vm),
         scratch_shapes=[
+            pltpu.VMEM((nx + UNIT, 8, ny), f32), pltpu.VMEM((3 * nx, 2 * ny), jnp.bfloat16),
             pltpu.VMEM((nx + 4, rows, nz), f32), pltpu.VMEM((nx + 2, rows, nz), f32),
             pltpu.VMEM((nx + 2, ny, nz), f32), pltpu.VMEM((nx + UNIT, ny, nz), f32),
             plane, plane, plane, plane, edge, edge, edge, edge,
             pltpu.SemaphoreType.DMA((nx // chunk,)), pltpu.SemaphoreType.DMA((nx // chunk,)),
             pltpu.SemaphoreType.DMA((nx // chunk,)),
         ],
-        compiler_params=pltpu.CompilerParams(vmem_limit_bytes=40 * 2**20),
+        compiler_params=pltpu.CompilerParams(vmem_limit_bytes=LARGE),
         cost_estimate=pl.CostEstimate(flops=nx * ny * nz * 100, bytes_accessed=nx * ny * nz * 12, transcendentals=nx * ny * nz * 10),
         name="relax",
     )
 
 
 def pack_call(nx, ny, nz, n_tiles):
-    def kernel(p_hbm, s_hbm, m_ref, head_lo, head_hi, track_lo, track_hi, p_lo, p_hi, s_lo, s_hi, sem):
+    def kernel(p_hbm, s_hbm, m_hbm, head_lo, head_hi, track_lo, track_hi, p_lo, p_hi, s_lo, s_hi, m_ends, sem):
         planes = [
             (p_hbm, 0, head_lo, 0), (p_hbm, 1, head_lo, 1), (s_hbm, 0, head_lo, 2),
             (p_hbm, nx - 2, head_hi, 0), (p_hbm, nx - 1, head_hi, 1), (s_hbm, nx - 1, head_hi, 2),
@@ -262,15 +290,22 @@
             pltpu.make_async_copy(src.at[:, pl.ds(at, 8)], dst, sem.at[6 + i])
             for i, (src, at, dst) in enumerate(rows)
         ]
+        copies += [
+            pltpu.make_async_copy(
+                m_hbm.at[pl.ds(c * n_tiles + side * (n_tiles - 8), 8)], m_ends.at[2 * c + side], sem.at[10 + 2 * c + side]
+            )
+            for c in range(3)
+            for side in range(2)
+        ]
         for copy in copies:
             copy.start()
         head_lo[pl.ds(3 * ny, 8), :] = jnp.zeros((8, nz), F32)
         head_hi[pl.ds(3 * ny, 8), :] = jnp.zeros((8, nz), F32)
-        for c in range(3):
-            head_lo[pl.ds(3 * ny + c, 1), :] = m_ref[pl.ds(c * n_tiles, 1), :]
-            head_hi[pl.ds(3 * ny + c, 1), :] = m_ref[pl.ds((c + 1) * n_tiles - 1, 1), :]
         for copy in copies[6:]:
             copy.wait()
+        for c in range(3):
+            head_lo[pl.ds(3 * ny + c, 1), :] = m_ends[2 * c, pl.ds(0, 1), :]
+            head_hi[pl.ds(3 * ny + c, 1), :] = m_ends[2 * c + 1, pl.ds(7, 1), :]
         for out, p_ref, s_ref, order in ((track_lo, p_lo, s_lo, (0, 1)), (track_hi, p_hi, s_hi, (7, 6))):
             p2 = p_ref.reshape(nx * 8, nz)
             s2 = s_ref.reshape(nx * 8, nz)
@@ -287,10 +322,10 @@
     return pl.pallas_call(
         kernel,
         out_shape=(head, head, track, track),
-        in_specs=[ANY, ANY, VM],
+        in_specs=[HBM] * 3,
         out_specs=(VM,) * 4,
-        scratch_shapes=[eight] * 4 + [pltpu.SemaphoreType.DMA((10,))],
-        compiler_params=pltpu.CompilerParams(vmem_limit_bytes=16 * 2**20),
+        scratch_shapes=[eight] * 4 + [pltpu.VMEM((6, 8, LANES), F32), pltpu.SemaphoreType.DMA((16,))],
+        compiler_params=pltpu.CompilerParams(vmem_limit_bytes=LARGE),
         cost_estimate=cost(10**6, 4 * 2**20),
         name="pack",
     )
@@ -307,7 +342,7 @@
     track = jax.ShapeDtypeStruct((3 * nx + 8, nz), F32)
     return pl.pallas_call(
         kernel, out_shape=(track, track), in_specs=[VM] * 4, out_specs=(VM, VM),
-        compiler_params=pltpu.CompilerParams(vmem_limit_bytes=16 * 2**20),
+        compiler_params=pltpu.CompilerParams(vmem_limit_bytes=SMALL),
         cost_estimate=cost(10**5, 2**20), name="corners",
     )
 
@@ -362,7 +397,7 @@
         ),
         in_specs=[VM] * 3,
         out_specs=(VM,) * 3,
-        compiler_params=pltpu.CompilerParams(vmem_limit_bytes=16 * 2**20),
+        compiler_params=pltpu.CompilerParams(vmem_limit_bytes=SMALL),
         cost_estimate=cost(10**8, 2**20),
         name="requests",
     )
@@ -370,7 +405,8 @@
 
 def look_up(table, lane, row, rows, width):
     n = lane.shape[1]
-    here = (lax.broadcasted_iota(jnp.int32, (width, n), 0) == lane).astype(F32).astype(BF16)
+    lanes = lax.broadcasted_iota(jnp.int32, (width, n), 0).astype(F32).astype(BF16)
+    here = jnp.where(lanes == lane.astype(F32).astype(BF16), jnp.array(1, BF16), jnp.array(0, BF16))
     got = mm(table, jnp.concatenate([here, here], axis=0))
     mine = lax.broadcasted_iota(jnp.int32, (rows, n), 0) == row
     return [
@@ -378,40 +414,12 @@
     ]
 
 
-def answer_call(n_track, cap, nx, ny):
-    per = cap // LANES
-
-    def kernel(requests, surface, reply, parts):
-        flat = surface.reshape(surface.shape[0] * 8, ny)
-        for c in range(3):
-            hi, lo = split(flat[pl.ds((surface.shape[0] - nx) * 8 + c, nx, stride=8), :])
-            parts[pl.ds(c * nx, nx), pl.ds(0, ny)] = hi
-            parts[pl.ds(c * nx, nx), pl.ds(ny, ny)] = lo
-        table = parts[...]
-        group = 8 // per if per < 8 else 1
-
-        def body(o, _):
-            asked = requests[pl.ds(pl.multiple_of(o * group * per, 8), group * per), :].astype(jnp.int32)
-            at_row = lax.shift_right_logical(asked, int(math.log2(ny)))
-            at_lane = asked & (ny - 1)
-            for j in range(group * per):
-                values = look_up(table, at_lane[j : j + 1], at_row[j : j + 1], nx, ny)
-                for c in range(3):
-                    reply[o * group + j // per, pl.ds(c * per + j % per, 1), :] = values[c]
-            return 0
-
-        lax.fori_loop(0, n_track // group, body, 0)
-
-    return pl.pallas_call(
-        kernel,
-        out_shape=jax.ShapeDtypeStruct((n_track, 3 * per, LANES), F32),
-        in_specs=[VM, VM],
-        out_specs=VM,
-        scratch_shapes=[pltpu.VMEM((3 * nx, 2 * ny), BF16)],
-        compiler_params=pltpu.CompilerParams(vmem_limit_bytes=16 * 2**20),
-        cost_estimate=cost(10**9, 2**20),
-        name="answer",
-    )
+def look_up_all(table, lane, row, rows, width, store):
+    for j in range(0, lane.shape[0], 2):
+        pair = [jnp.concatenate([v[j : j + 1], v[j + 1 : j + 2]], axis=1) for v in (lane, row)]
+        values = look_up(table, pair[0], pair[1], rows, width)
+        for i in range(2):
+            store(j + i, [v[:, i * LANES : (i + 1) * LANES] for v in values])
 
 
 def llb(m, field, target):
@@ -439,54 +447,57 @@
         flat[pl.ds(8 + c, n_tiles, stride=8), :] = m_ref[pl.ds(c * n_tiles, n_tiles), :]
 
 
-def exchange(tiles_ref, pair_hi, pair_lo, out_ref, k, n_tiles, at):
-    mid = both(tiles_ref[k + 1])
-    low = both(tiles_ref[k])
+def exchange(tiles_ref, own, nxt, k):
+    here = jnp.concatenate([both(tiles_ref[k + 1]), both(tiles_ref[k])], axis=1)
     high = both(tiles_ref[k + 2])
-    here = jnp.concatenate([mid, low], axis=1)
-    hi = pair_hi[at]
-    lo = pair_lo[at]
-    field = fold(mm_nt(here, hi), mm_nt(here, lo))
-    field = field + fold(mm(high, hi[:, LANES:]), mm(high, lo[:, LANES:]))
-    for c in range(3):
-        out_ref[pl.ds(c * n_tiles + k, 1), :] = field[c : c + 1]
-
-
-def first_call(n_tiles, ny):
-    step = 8
-
-    def kernel(flags, own, nxt, m_ref, below, above, pair_hi, pair_lo, ex, tiles):
-        i = pl.program_id(0)
-
-        @pl.when(i == 0)
-        def _():
-            tile_major(m_ref, tiles, n_tiles)
-            tiles[0] = jnp.where(flags[0] > 0, below[pl.ds(3 * ny, 8), :], 0.0)
-            tiles[n_tiles + 1] = jnp.where(flags[1] > 0, above[pl.ds(3 * ny, 8), :], 0.0)
-
-        for j in range(step):
-            for ref, lanes in ((own, pl.ds(0, LANES)), (nxt, pl.ds(LANES, LANES))):
-                hi, lo = split(ref[j])
-                pair_hi[j, :, lanes] = hi
-                pair_lo[j, :, lanes] = lo
-        for j in range(step):
-            exchange(tiles, pair_hi, pair_lo, ex, i * step + j, n_tiles, j)
-
-    tile = pl.BlockSpec((step, LANES, LANES), lambda i: (i, 0, 0))
-    pair = pl.BlockSpec((step, LANES, 2 * LANES), lambda i: (i, 0, 0))
+    own_hi, own_lo = split(own)
+    nxt_hi, nxt_lo = split(nxt)
+    field = fold(
+        mm_nt(here, jnp.concatenate([own_hi, nxt_hi], axis=1)),
+        mm_nt(here, jnp.concatenate([own_lo, nxt_lo], axis=1)),
+    )
+    return field + fold(mm(high, nxt_hi), mm(high, nxt_lo))
+
+
+def first_call(n_tiles, ny, start, count):
+    step = 4
+    chunks = count // step
+
+    def kernel(flags, own_hbm, nxt_hbm, m_ref, below, above, ex, own, nxt, tiles, sem):
+        def copies(c):
+            part = pl.ds(c * step, step)
+            return [
+                pltpu.make_async_copy(own_hbm.at[pl.ds(start + c * step, step)], own.at[part], sem.at[0, c]),
+                pltpu.make_async_copy(nxt_hbm.at[pl.ds(start + c * step, step)], nxt.at[part], sem.at[1, c]),
+            ]
+
+        for c in range(chunks):
+            for copy in copies(c):
+                copy.start()
+        tile_major(m_ref, tiles, n_tiles)
+        tiles[0] = jnp.where(flags[0] > 0, below[pl.ds(3 * ny, 8), :], 0.0)
+        tiles[n_tiles + 1] = jnp.where(flags[1] > 0, above[pl.ds(3 * ny, 8), :], 0.0)
+        for c in range(chunks):
+            for copy in copies(c):
+                copy.wait()
+            for k in range(c * step, (c + 1) * step):
+                field = exchange(tiles, own[k], nxt[k], start + k)
+                for n in range(3):
+                    ex[pl.ds(n * count + k, 1), :] = field[n : n + 1]
+
     return pl.pallas_call(
         kernel,
-        grid=(n_tiles // step,),
-        out_shape=(
-            jax.ShapeDtypeStruct((n_tiles, LANES, 2 * LANES), BF16),
-            jax.ShapeDtypeStruct((n_tiles, LANES, 2 * LANES), BF16),
-            jax.ShapeDtypeStruct((3 * n_tiles, LANES), F32),
-        ),
-        in_specs=[SM, tile, tile, VM, VM, VM],
-        out_specs=(pair, pair, VM),
-        scratch_shapes=[pltpu.VMEM((n_tiles + 2, 8, LANES), F32)],
-        compiler_params=pltpu.CompilerParams(vmem_limit_bytes=24 * 2**20),
-        cost_estimate=cost(10**9, 8 * 2**20),
+        out_shape=jax.ShapeDtypeStruct((3 * count, LANES), F32),
+        in_specs=[SM, HBM, HBM, VM, VM, VM],
+        out_specs=VM,
+        scratch_shapes=[
+            pltpu.VMEM((count, LANES, LANES), F32),
+            pltpu.VMEM((count, LANES, LANES), F32),
+            pltpu.VMEM((n_tiles + 2, 8, LANES), F32),
+            pltpu.SemaphoreType.DMA((2, chunks)),
+        ],
+        compiler_params=pltpu.CompilerParams(vmem_limit_bytes=LARGE),
+        cost_estimate=cost(10**9, 4 * 2**20),
         name="couple_first",
     )
 
@@ -495,7 +506,7 @@
     per = cap // LANES
     slot_rows = n_track * per
 
-    def kernel(answers, slots, m_ref, ex, target, applied, m_out, edge_lo, edge_hi, parts):
+    def kernel(answers, slots, m_ref, ex_a, ex_b, target, applied, m_out, edge_lo, edge_hi, parts):
         for c in range(3):
             rows = jnp.concatenate([answers[o, pl.ds(c * per, per), :] for o in range(n_track)], axis=0)
             hi, lo = split(rows)
@@ -505,13 +516,19 @@
         slot = slots[...]
         at_row = lax.shift_right_logical(slot, int(math.log2(LANES)))
         at_lane = slot & (LANES - 1)
-        for k in range(n_tiles):
-            values = look_up(table, at_lane[k : k + 1], at_row[k : k + 1], slot_rows, LANES)
+
+        def store(k, values):
             for c in range(3):
                 applied[pl.ds(c * n_tiles + k, 1), :] = values[c]
+
+        look_up_all(table, at_lane, at_row, slot_rows, LANES, store)
         part = [pl.ds(c * n_tiles, n_tiles) for c in range(3)]
         m = [m_ref[part[c], :] for c in range(3)]
-        m = llb(m, [applied[part[c], :] + ex[part[c], :] for c in range(3)], target[...])
+        half = n_tiles // 2
+        ex = [
+            jnp.concatenate([ref[pl.ds(c * half, half), :] for ref in (ex_a, ex_b)], axis=0) for c in range(3)
+        ]
+        m = llb(m, [applied[part[c], :] + ex[c] for c in range(3)], target[...])
         edge_lo[...] = jnp.zeros((8, LANES), F32)
         edge_hi[...] = jnp.zeros((8, LANES), F32)
         for c in range(3):
@@ -524,20 +541,22 @@
     return pl.pallas_call(
         kernel,
         out_shape=(grains, grains, edge, edge),
-        in_specs=[VM] * 5,
+        in_specs=[VM] * 6,
         out_specs=(VM,) * 4,
         scratch_shapes=[pltpu.VMEM((3 * slot_rows, 2 * LANES), BF16)],
-        compiler_params=pltpu.CompilerParams(vmem_limit_bytes=16 * 2**20),
+        compiler_params=pltpu.CompilerParams(vmem_limit_bytes=SMALL),
         cost_estimate=cost(10**9, 2**20),
         name="section_first",
     )
 
 
 def second_call(n_tiles):
-    def kernel(pair_hi, pair_lo, m_ref, ex, tiles):
+    def kernel(own, nxt, m_ref, ex, tiles):
         tile_major(m_ref, tiles, n_tiles)
         for k in range(n_tiles):
-            exchange(tiles, pair_hi, pair_lo, ex, k, n_tiles, k)
+            field = exchange(tiles, own[k], nxt[k], k)
+            for n in range(3):
+                ex[pl.ds(n * n_tiles + k, 1), :] = field[n : n + 1]
 
     return pl.pallas_call(
         kernel,
@@ -545,19 +564,20 @@
         in_specs=[VM] * 3,
         out_specs=VM,
         scratch_shapes=[pltpu.VMEM((n_tiles + 2, 8, LANES), F32)],
-        compiler_params=pltpu.CompilerParams(vmem_limit_bytes=24 * 2**20),
+        compiler_params=pltpu.CompilerParams(vmem_limit_bytes=SMALL),
         cost_estimate=cost(10**9, 4 * 2**20),
         name="couple_second",
     )
 
 
 def last_call(n_tiles):
-    def kernel(flags, m_ref, ex, applied, target, below, above, hi_first, lo_first, hi_last, lo_last, out):
+    def kernel(flags, m_ref, ex, applied, target, below, above, nxt, out):
         low = both(jnp.where(flags[0] > 0, below[...], 0.0))
         high = both(jnp.where(flags[1] > 0, above[...], 0.0))
-        beside = slice(LANES, 2 * LANES)
-        first = fold(mm_nt(low, hi_first[0][:, beside]), mm_nt(low, lo_first[0][:, beside]))
-        last = fold(mm(high, hi_last[0][:, beside]), mm(high, lo_last[0][:, beside]))
+        hi, lo = split(nxt[0])
+        first = fold(mm_nt(low, hi), mm_nt(low, lo))
+        hi, lo = split(nxt[n_tiles - 1])
+        last = fold(mm(high, hi), mm(high, lo))
         at = lax.broadcasted_iota(jnp.int32, (n_tiles, LANES), 0)
         field = []
         m = []
@@ -570,22 +590,12 @@
         for c in range(3):
             out[pl.ds(c * n_tiles, n_tiles), :] = m[c]
 
-    def at(k):
-        return pl.BlockSpec((1, LANES, 2 * LANES), lambda i: (k, 0, 0))
-
-    def full(shape):
-        return pl.BlockSpec(shape, lambda i: (0, 0))
-
-    grains = full((3 * n_tiles, LANES))
-    edge = full((8, LANES))
     return pl.pallas_call(
         kernel,
-        grid=(1,),
         out_shape=jax.ShapeDtypeStruct((3 * n_tiles, LANES), F32),
-        in_specs=[SM, grains, grains, grains, full((n_tiles, LANES)), edge, edge,
-                  at(0), at(0), at(n_tiles - 1), at(n_tiles - 1)],
-        out_specs=grains,
-        compiler_params=pltpu.CompilerParams(vmem_limit_bytes=16 * 2**20),
+        in_specs=[SM] + [VM] * 7,
+        out_specs=VM,
+        compiler_params=pltpu.CompilerParams(vmem_limit_bytes=SMALL),
         cost_estimate=cost(10**7, 2**20),
         name="section_last",
     )
@@ -621,19 +631,23 @@
     asked = lax.all_to_all(requests.reshape(n_track, cap // LANES, LANES), "track", 0, 0)
 
     kern = jnp.pad(depth_kernel, ((0, 5), (0, 0)))
-    relaxed, surface = relax_call(nx, ny, nz)(
-        flags, potential, source, below, above, left, right, track_lo, track_hi, kern
-    )
-    reply = answer_call(n_track, cap, nx, ny)(asked.reshape(n_track * cap // LANES, LANES), surface)
+    half = n_tiles // 2
+    couplings = (flags, self_tiles[0], next_tiles[0], state, below, above)
+    ex_a = first_call(n_tiles, ny, 0, half)(*couplings)
+    relaxed, reply = relax_call(nx, ny, nz, n_track, cap)(
+        flags, potential, source, below, above, left, right, track_lo, track_hi, kern,
+        asked.reshape(n_track * cap // LANES, LANES), ex_a,
+    )
     answers = lax.all_to_all(reply, "track", 0, 0)
-
-    pair_hi, pair_lo, ex = first_call(n_tiles, ny)(flags, self_tiles[0], next_tiles[0], state, below, above)
-    applied, state, edge_lo, edge_hi = section_call(n_tiles, n_track, cap)(answers, slots, state, ex, target)
+    ex_b = first_call(n_tiles, ny, half, n_tiles - half)(*couplings)
+    applied, state, edge_lo, edge_hi = section_call(n_tiles, n_track, cap)(
+        answers, slots, state, ex_a, ex_b, target
+    )
     tile_below = shifted(edge_hi, "head", 1)
     tile_above = shifted(edge_lo, "head", -1)
-    ex = second_call(n_tiles)(pair_hi, pair_lo, state)
+    ex = second_call(n_tiles)(self_tiles[0], next_tiles[0], state)
     state = last_call(n_tiles)(
-        flags, state, ex, applied, target, tile_below, tile_above, pair_hi, pair_lo, pair_hi, pair_lo
+        flags, state, ex, applied, target, tile_below, tile_above, next_tiles[0]
     )
     return relaxed, state.reshape(3, 1, grains)
 

time: 70.8 us -> 60.1 us (0.85)
  local copies, waits for them, and re-layouts: 14.1 us -> 0.82 us
  Pallas kernels: 30.4 us -> 32.2 us
  waiting for transfers between devices: 3.8 us -> 4.81 us
    unnamed x28 -> x16, local copies, waits for them, and re-layouts: 14.1 us -> 0.82 us
    all_to_all x1, waiting for transfers between devices: 0.01 us -> 4.04 us  [per_device(): answers = lax.all_to_all(reply, 'track', 0, 0)]
    ppermute x6, waiting for transfers between devices: 3.79 us -> 0.76 us  [shifted(): return lax.ppermute(v, axis, [(i, (i + by) % n) for i in range(n)])]
    pallas_call x5, Pallas kernels: 26.5 us -> 27.4 us  [the longest x1 18.8 us: per_device(): relax_call(nx, ny, nz, n_track, cap)]
    pallas_call x1, Pallas kernels: 0.8 us -> 1.65 us  [per_device(): pack_call(nx, ny, nz, n_tiles)(potential, source, state)]
  transfers between devices with their start and end apart: 8 -> 8, of which waited for: 2 -> 2; matrix products, arithmetic and copies ran while one was open for 0% -> 0% of each run, Pallas kernels for 34% -> 16%
where the time goes in v2:
time: 60.1 us; the launch traced here: 59.1 us
  Pallas kernels  32.2 us (54%)
  starting transfers between devices  20.5 us (34%)
  waiting for transfers between devices  4.81 us (8%)
  local copies, waits for them, and re-layouts  0.82 us (1%)
  between operations  0.77 us (1%)
    pallas_call x1, Pallas kernels, per_device(): relax_call(nx, ny, nz, n_track, cap)  18.8 us
    ppermute x6, starting transfers between devices, shifted(): return lax.ppermute(v, axis, [(i, (i + by) % n) for i in range(n)])  9.11 us
    all_to_all x1, starting transfers between devices, per_device(): lax.all_to_all(requests.reshape(n_track, cap // LANES, LANES), 'track', 0...  6.59 us
    all_to_all x1, starting transfers between devices, per_device(): answers = lax.all_to_all(reply, 'track', 0, 0)  4.79 us
    all_to_all x1, waiting for transfers between devices, per_device(): answers = lax.all_to_all(reply, 'track', 0, 0)  4.04 us
    pallas_call x1, Pallas kernels, per_device(): ex_b = first_call(n_tiles, ny, half, n_tiles - half)(*couplings)  3.07 us
    pallas_call x1, Pallas kernels, per_device(): ex_a = first_call(n_tiles, ny, 0, half)(*couplings)  2.98 us
    pallas_call x1, Pallas kernels, per_device(): ex = second_call(n_tiles)(self_tiles[0], next_tiles[0], state)  1.83 us
  transfers between devices with their start and end apart: 8, of which 2 were waited for; matrix products, arithmetic and copies ran while one was open for 0% of the time, Pallas kernels for 16%

profile of v2, /device:TPU:0, one launch (start us, length us, event | category | flops | bytes accessed | tf_op | source)
XLA Modules:
  0.0 59.1 jit_solution(10843297489425289333)
XLA Ops:
  0.6 0.8 %copy-done.2 = f32[3,1,4096]{2,1,0:T(1,128)S(1)} copy-done((f32[3,1,4096]{2,1,0:T(1,128)S(1)}, f32[3,1,4096]{2,1,0:T(1,128)}, u32[]{:S(2)}) %copy-start.2) | copy-done | bytes 49176
  1.5 1.7 %pack.1 = (f32[392,128]{1,0:T(8,128)S(1)}, f32[392,128]{1,0:T(8,128)S(1)}, f32[200,128]{1,0:T(8,128)S(1)}, f32[200,128]{1,0:T(8,128)S(1)}) custom-call(f32[64,128,128]{2,1,0:T(8,128)} %p_hbm.3, f32[64,128,128]{2,1,0:T(8,128)} %s_hbm.3, f32[96,128]{1,0:T(8,128)S(1)} %bitcast.20), custom_call_target="tpu_custom_call" | custom-call | flops 1000000 | bytes 4194304 | tf_op jit(solution)/shard_map/pack/pallas_call | solution.py:622
  3.1 0.5 collective-permute-start
  3.6 2.0 %collective-permute-start.1 = (f32[392,128]{1,0:T(8,128)S(1)}, f32[392,128]{1,0:T(8,128)S(1)}, u32[]{:S(2)}, u32[]{:S(2)}) collective-permute-start(f32[392,128]{1,0:T(8,128)S(1)} %get-tuple-element.18), channel_id=1, source_target_pairs={{0,24},{8,0},{16,8},{24,16},{1,25},{9,1},{17,9},{25,17},{2,26},{10... | collective-permute-start | bytes 602120 | tf_op jit(solution)/shard_map/ppermute | solution.py:606
  5.6 1.8 %requests.1 = (f32[64,128]{1,0:T(8,128)}, s32[32,128]{1,0:T(8,128)S(1)}, f32[32,128]{1,0:T(8,128)S(1)}) custom-call(s32[32,128]{1,0:T(8,128)S(1)} %bitcast.25, s32[32,128]{1,0:T(8,128)S(1)} %bitcast.26, f32[1,128]{1,0:T(1,128)S(1)} %bitcast.27), custom_call_target="tpu_custom_call" | custom-call | flops 100000000 | bytes 1048576 | tf_op jit(solution)/shard_map/requests/pallas_call | solution.py:625
  7.4 6.6 %all-to-all-start = ((f32[8,8,128]{2,1,0:T(8,128)}), f32[8,8,128]{2,1,0:T(8,128)S(1)}, u32[]{:S(2)}, u32[]{:S(2)}) async-start(f32[8,8,128]{2,1,0:T(8,128)} %bitcast.8), calls=%async_computation | async-start | bytes 65536 | tf_op jit(solution)/shard_map/all_to_all | solution.py:631
  14.0 0.0 collective-permute-done.1.above.hhi
  14.0 2.1 %collective-permute-start.2 = (f32[200,128]{1,0:T(8,128)S(1)}, f32[200,128]{1,0:T(8,128)S(1)}, u32[]{:S(2)}, u32[]{:S(2)}) collective-permute-start(f32[200,128]{1,0:T(8,128)S(1)} %get-tuple-element.21.own_hi), channel_id=1, source_target_pairs={{0,1},{1,2},{2,3},{3,4},{4,5},{5,6},{6,7},{7,0},{8,9},{9,10},{10,1... | collective-permute-start | bytes 307208 | tf_op jit(solution)/shard_map/ppermute | solution.py:606
  16.1 2.8 %collective-permute-start.3 = (f32[200,128]{1,0:T(8,128)S(1)}, f32[200,128]{1,0:T(8,128)S(1)}, u32[]{:S(2)}, u32[]{:S(2)}) collective-permute-start(f32[200,128]{1,0:T(8,128)S(1)} %get-tuple-element.22.own_lo), channel_id=1, source_target_pairs={{0,7},{1,0},{2,1},{3,2},{4,3},{5,4},{6,5},{7,6},{8,15},{9,8},{10,9... | collective-permute-start | bytes 307208 | tf_op jit(solution)/shard_map/ppermute | solution.py:606
  18.9 0.1 add_convert_fusion.flags
  19.0 3.0 %couple_first.2.ex_hbm.ex_a = f32[48,128]{1,0:T(8,128)S(1)} custom-call(s32[4]{0:T(128)S(1)} %add_convert_fusion.flags, f32[32,128,128]{2,1,0:T(8,128)} %bitcast.17, f32[32,128,128]{2,1,0:T(8,128)} %bitcast.13, f32[96,128]{1,0:T(8,128)S(1)} %bitcast.21, f32[392,128]{1,0:T(8,128)S(1)} %collective-permute-done.below.hlo, ...), custom_call_target="tpu_custom_call" | custom-call | flops 1000000000 | bytes 4194304 | tf_op jit(solution)/shard_map/couple_first/pallas_call | solution.py:636
  22.0 0.0 all-to-all-done
  22.0 0.7 %collective-permute-done.3.thi = f32[200,128]{1,0:T(8,128)S(1)} collective-permute-done((f32[200,128]{1,0:T(8,128)S(1)}, f32[200,128]{1,0:T(8,128)S(1)}, u32[]{:S(2)}, u32[]{:S(2)}) %collective-permute-start.3) | collective-permute-done | bytes 102432 | tf_op jit(solution)/shard_map/ppermute | solution.py:606
  22.7 18.8 %relax.1 = (f32[64,128,128]{2,1,0:T(8,128)}, f32[8,24,128]{2,1,0:T(8,128)}) custom-call(s32[4]{0:T(128)S(1)} %add_convert_fusion.flags, f32[64,128,128]{2,1,0:T(8,128)} %p_hbm.3, f32[64,128,128]{2,1,0:T(8,128)} %s_hbm.3, f32[392,128]{1,0:T(8,128)S(1)} %collective-permute-done.below.hlo, f32[392,128]{1,0:T(8,128)S(1)} %collective-permute-done.1.above.hhi, ...), custom_call_target="tpu_custom_call" | custom-call | flops 104857600 | bytes 12582912 | tf_op jit(solution)/shard_map/relax/pallas_call | solution.py:637
  41.5 4.8 %all-to-all-start.1 = ((f32[8,24,128]{2,1,0:T(8,128)}), f32[8,24,128]{2,1,0:T(8,128)S(1)}, u32[]{:S(2)}, u32[]{:S(2)}) async-start(f32[8,24,128]{2,1,0:T(8,128)} %get-tuple-element.25), calls=%async_computation.1 | async-start | bytes 196608 | tf_op jit(solution)/shard_map/all_to_all | solution.py:641
  46.3 3.1 %couple_first.3.ex_b = f32[48,128]{1,0:T(8,128)S(1)} custom-call(s32[4]{0:T(128)S(1)} %add_convert_fusion.flags, f32[32,128,128]{2,1,0:T(8,128)} %bitcast.18, f32[32,128,128]{2,1,0:T(8,128)} %bitcast.14, f32[96,128]{1,0:T(8,128)S(1)} %bitcast.22, f32[392,128]{1,0:T(8,128)S(1)} %collective-permute-done.below.hlo, f32[392,128]{1,0:T(8,128)S(1)} %collective-permute-done.1.above.hhi), custom_call_target="tpu_custom_call" | custom-call | flops 1000000000 | bytes 4194304 | tf_op jit(solution)/shard_map/couple_first/pallas_call | solution.py:642
  49.4 4.0 %all-to-all-done.1.answers = f32[8,24,128]{2,1,0:T(8,128)S(1)} async-done(((f32[8,24,128]{2,1,0:T(8,128)}), f32[8,24,128]{2,1,0:T(8,128)S(1)}, u32[]{:S(2)}, u32[]{:S(2)}) %all-to-all-start.1) | async-done | bytes 98336 | tf_op jit(solution)/shard_map/all_to_all | solution.py:641
  53.4 0.7 %section_first.1 = (f32[96,128]{1,0:T(8,128)S(1)}, f32[96,128]{1,0:T(8,128)S(1)}, f32[8,128]{1,0:T(8,128)S(1)}, f32[8,128]{1,0:T(8,128)S(1)}) custom-call(f32[8,24,128]{2,1,0:T(8,128)S(1)} %all-to-all-done.1.answers, s32[32,128]{1,0:T(8,128)S(1)} %get-tuple-element.26.slots, f32[96,128]{1,0:T(8,128)S(1)} %bitcast.23, f32[48,128]{1,0:T(8,128)S(1)} %couple_first.2.ex_hbm.ex_a, ...), custom_call_target="tpu_custom_call" | custom-call | flops 1000000000 | bytes 1048576 | tf_op jit(solution)/shard_map/section_first/pallas_call | solution.py:643
  54.1 0.1 collective-permute-start.4
  54.2 1.7 %collective-permute-start.5 = (f32[8,128]{1,0:T(8,128)S(1)}, f32[8,128]{1,0:T(8,128)S(1)}, u32[]{:S(2)}, u32[]{:S(2)}) collective-permute-start(f32[8,128]{1,0:T(8,128)S(1)} %get-tuple-element.31), channel_id=1, source_target_pairs={{0,24},{8,0},{16,8},{24,16},{1,25},{9,1},{17,9},{25,17},{2,26},{10... | collective-permute-start | bytes 12296 | tf_op jit(solution)/shard_map/ppermute | solution.py:606
  55.9 1.8 %couple_second.1.ex = f32[96,128]{1,0:T(8,128)S(1)} custom-call(f32[32,128,128]{2,1,0:T(8,128)S(1)} %bitcast.19, f32[32,128,128]{2,1,0:T(8,128)S(1)} %bitcast.15, f32[96,128]{1,0:T(8,128)S(1)} %get-tuple-element.28.m_ref), custom_call_target="tpu_custom_call" | custom-call | flops 1000000000 | bytes 4194304 | tf_op jit(solution)/shard_map/couple_second/pallas_call | solution.py:648
  57.8 0.0 collective-permute-done.4.below
  57.8 0.0 collective-permute-done.5.above
  57.8 1.3 %section_last.1 = f32[96,128]{1,0:T(8,128)} custom-call(s32[4]{0:T(128)S(1)} %add_convert_fusion.flags, f32[96,128]{1,0:T(8,128)S(1)} %get-tuple-element.28.m_ref, f32[96,128]{1,0:T(8,128)S(1)} %couple_second.1.ex, f32[96,128]{1,0:T(8,128)S(1)} %get-tuple-element.29.applied, f32[32,128]{1,0:T(8,128)S(1)} %get-tuple-element.27.target, ...), custom_call_target="tpu_custom_call" | custom-call | flops 10000000 | bytes 1048576 | tf_op jit(solution)/shard_map/section_last/pallas_call | solution.py:649
  (19 shorter events, 0.1 us)
Async XLA Ops:
  0.6 0.8 %copy-start.2 = (f32[3,1,4096]{2,1,0:T(1,128)S(1)}, f32[3,1,4096]{2,1,0:T(1,128)}, u32[]{:S(2)}) copy-start(f32[3,1,4096]{2,1,0:T(1,128)} %param.12) | copy-start | bytes 147460
  1.4 4.2 %copy-start.4 = (s32[1,4096]{1,0:T(1,128)S(1)}, s32[1,4096]{1,0:T(1,128)}, u32[]{:S(2)}) copy-start(s32[1,4096]{1,0:T(1,128)} %param.13) | copy-start | bytes 49156
  1.4 4.2 %copy-start.5 = (s32[1,4096]{1,0:T(1,128)S(1)}, s32[1,4096]{1,0:T(1,128)}, u32[]{:S(2)}) copy-start(s32[1,4096]{1,0:T(1,128)} %param.14) | copy-start | bytes 49156
  1.4 4.2 %copy-start.6 = (f32[128]{0:T(128)S(1)}, f32[128]{0:T(128)}, u32[]{:S(2)}) copy-start(f32[128]{0:T(128)} %param.15) | copy-start | bytes 1540
  1.4 17.5 %copy-start.7 = (f32[3,128]{1,0:T(4,128)S(1)}, f32[3,128]{1,0:T(4,128)}, u32[]{:S(2)}) copy-start(f32[3,128]{1,0:T(4,128)} %param.11) | copy-start | bytes 4612
  1.4 17.5 %copy-start.3 = (f32[3,1,4096]{2,1,0:T(1,128)S(1)}, f32[3,1,4096]{2,1,0:T(1,128)}, u32[]{:S(2)}) copy-start(f32[3,1,4096]{2,1,0:T(1,128)} %param.12) | copy-start | bytes 147460
  3.1 10.9 %collective-permute-start = (f32[392,128]{1,0:T(8,128)S(1)}, f32[392,128]{1,0:T(8,128)S(1)}, u32[]{:S(2)}, u32[]{:S(2)}) collective-permute-start(f32[392,128]{1,0:T(8,128)S(1)} %get-tuple-element.17), channel_id=1, source_target_pairs={{0,8},{8,16},{16,24},{24,0},{1,9},{9,17},{17,25},{25,1},{2,10},{10... | collective-permute-start | bytes 602120 | tf_op jit(solution)/shard_map/ppermute | solution.py:606
  3.6 10.4 %collective-permute-start.1 = (f32[392,128]{1,0:T(8,128)S(1)}, f32[392,128]{1,0:T(8,128)S(1)}, u32[]{:S(2)}, u32[]{:S(2)}) collective-permute-start(f32[392,128]{1,0:T(8,128)S(1)} %get-tuple-element.18), channel_id=1, source_target_pairs={{0,24},{8,0},{16,8},{24,16},{1,25},{9,1},{17,9},{25,17},{2,26},{10... | collective-permute-start | bytes 602120 | tf_op jit(solution)/shard_map/ppermute | solution.py:606
  7.4 14.6 %all-to-all-start = ((f32[8,8,128]{2,1,0:T(8,128)}), f32[8,8,128]{2,1,0:T(8,128)S(1)}, u32[]{:S(2)}, u32[]{:S(2)}) async-start(f32[8,8,128]{2,1,0:T(8,128)} %bitcast.8), calls=%async_computation | async-start | bytes 65536 | tf_op jit(solution)/shard_map/all_to_all | solution.py:631
  14.0 7.9 %collective-permute-start.2 = (f32[200,128]{1,0:T(8,128)S(1)}, f32[200,128]{1,0:T(8,128)S(1)}, u32[]{:S(2)}, u32[]{:S(2)}) collective-permute-start(f32[200,128]{1,0:T(8,128)S(1)} %get-tuple-element.21.own_hi), channel_id=1, source_target_pairs={{0,1},{1,2},{2,3},{3,4},{4,5},{5,6},{6,7},{7,0},{8,9},{9,10},{10,1... | collective-permute-start | bytes 307208 | tf_op jit(solution)/shard_map/ppermute | solution.py:606
  16.1 6.6 %collective-permute-start.3 = (f32[200,128]{1,0:T(8,128)S(1)}, f32[200,128]{1,0:T(8,128)S(1)}, u32[]{:S(2)}, u32[]{:S(2)}) collective-permute-start(f32[200,128]{1,0:T(8,128)S(1)} %get-tuple-element.22.own_lo), channel_id=1, source_target_pairs={{0,7},{1,0},{2,1},{3,2},{4,3},{5,4},{6,5},{7,6},{8,15},{9,8},{10,9... | collective-permute-start | bytes 307208 | tf_op jit(solution)/shard_map/ppermute | solution.py:606
  41.5 11.9 %all-to-all-start.1 = ((f32[8,24,128]{2,1,0:T(8,128)}), f32[8,24,128]{2,1,0:T(8,128)S(1)}, u32[]{:S(2)}, u32[]{:S(2)}) async-start(f32[8,24,128]{2,1,0:T(8,128)} %get-tuple-element.25), calls=%async_computation.1 | async-start | bytes 196608 | tf_op jit(solution)/shard_map/all_to_all | solution.py:641
  46.3 9.7 %copy-start = (f32[1,32,128,128]{3,2,1,0:T(8,128)S(1)}, f32[1,32,128,128]{3,2,1,0:T(8,128)}, u32[]{:S(2)}) copy-start(f32[1,32,128,128]{3,2,1,0:T(8,128)} %param.17) | copy-start | bytes 6291460
  53.4 2.5 %copy-start.1 = (f32[1,32,128,128]{3,2,1,0:T(8,128)S(1)}, f32[1,32,128,128]{3,2,1,0:T(8,128)}, u32[]{:S(2)}) copy-start(f32[1,32,128,128]{3,2,1,0:T(8,128)} %param.16) | copy-start | bytes 6291460
  54.1 3.6 %collective-permute-start.4 = (f32[8,128]{1,0:T(8,128)S(1)}, f32[8,128]{1,0:T(8,128)S(1)}, u32[]{:S(2)}, u32[]{:S(2)}) collective-permute-start(f32[8,128]{1,0:T(8,128)S(1)} %get-tuple-element.30), channel_id=1, source_target_pairs={{0,8},{8,16},{16,24},{24,0},{1,9},{9,17},{17,25},{25,1},{2,10},{10... | collective-permute-start | bytes 12296 | tf_op jit(solution)/shard_map/ppermute | solution.py:606
  54.2 3.6 %collective-permute-start.5 = (f32[8,128]{1,0:T(8,128)S(1)}, f32[8,128]{1,0:T(8,128)S(1)}, u32[]{:S(2)}, u32[]{:S(2)}) collective-permute-start(f32[8,128]{1,0:T(8,128)S(1)} %get-tuple-element.31), channel_id=1, source_target_pairs={{0,24},{8,0},{16,8},{24,16},{1,25},{9,1},{17,9},{25,17},{2,26},{10... | collective-permute-start | bytes 12296 | tf_op jit(solution)/shard_map/ppermute | solution.py:606

commit v3 on v2

--- a/solution.py
+++ b/solution.py
@@ -20,6 +20,7 @@
 VM = pl.BlockSpec(memory_space=pltpu.VMEM)
 SM = pl.BlockSpec(memory_space=pltpu.SMEM)
 HBM = pl.BlockSpec(memory_space=pltpu.HBM)
+ANY = pl.BlockSpec(memory_space=pl.ANY)
 
 
 def mm(a, b):
@@ -33,6 +34,13 @@
 def split(v):
     hi = v.astype(BF16)
     return hi, (v - hi.astype(F32)).astype(BF16)
+
+
+def place():
+    h = lax.axis_index("head")
+    t = lax.axis_index("track")
+    flags = (h > 0, h < lax.axis_size("head") - 1, t > 0, t < lax.axis_size("track") - 1, h % 2 == 1)
+    return [flag.astype(jnp.int32) for flag in flags]
 
 
 def cost(flops, moved):
@@ -72,7 +80,7 @@
     per = cap // LANES
     rows = ny + 2 * TOP
 
-    def kernel(flags, p_hbm, s_hbm, hlo, hhi, tlo, thi, own_lo, own_hi, kern, requests, ex_hbm, o_hbm, reply,
+    def kernel(p_hbm, s_hbm, from_a, from_b, tlo, thi, own_lo, own_hi, kern, requests, ex_hbm, o_hbm, reply,
                table, parts, pe, q, sb, ob, fx1, mx1, fx2, mx2, fy1, my1, fy2, my2, psem, ssem, osem):
         n_chunk = nx // chunk
 
@@ -95,16 +103,22 @@
         for c in range(AHEAD):
             fetch(c)
 
+        flags = place()
         has = [flags[n] > 0 for n in range(4)]
 
         def keep(flag, v):
             return jnp.where(flag, v, 0.0)
 
         main = pl.ds(TOP, ny)
-        for at, ref, first in ((0, hlo, 0), (1, hlo, ny), (nx + 2, hhi, 0), (nx + 3, hhi, ny)):
-            pe[at, main, :] = keep(has[0 if at < 2 else 1], ref[pl.ds(first, ny), :])
-        sb[0, :, :] = hlo[pl.ds(2 * ny, ny), :]
-        sb[nx + 1, :, :] = hhi[pl.ds(2 * ny, ny), :]
+        odd = flags[4] > 0
+        for side, (at, to) in enumerate((((0, 1), 0), ((nx + 2, nx + 3), nx + 1))):
+            swap = odd if side == 0 else jnp.logical_not(odd)
+            planes = [
+                jnp.where(swap, from_a[pl.ds(n * ny, ny), :], from_b[pl.ds(n * ny, ny), :]) for n in range(3)
+            ]
+            pe[at[0], main, :] = keep(has[side], planes[0])
+            pe[at[1], main, :] = keep(has[side], planes[1])
+            sb[to, :, :] = planes[2]
         pe2 = pe.reshape((nx + 4) * rows, nz)
         q2 = q.reshape((nx + 2) * rows, nz)
         for side, (ref, own, row) in enumerate(((tlo, own_lo, TOP - 1), (thi, own_hi, TOP + ny))):
@@ -259,7 +273,7 @@
             jax.ShapeDtypeStruct((nx, ny, nz), f32),
             jax.ShapeDtypeStruct((n_track, 3 * per, 128), f32),
         ),
-        in_specs=[pl.BlockSpec(memory_space=pltpu.SMEM), hbm, hbm] + [vm] * 8 + [pl.BlockSpec(memory_space=pl.ANY)],
+        in_specs=[hbm, hbm] + [vm] * 8 + [pl.BlockSpec(memory_space=pl.ANY)],
         out_specs=(hbm, vm),
         scratch_shapes=[
             pltpu.VMEM((nx + UNIT, 8, ny), f32), pltpu.VMEM((3 * nx, 2 * ny), jnp.bfloat16),
@@ -275,37 +289,29 @@
     )
 
 
-def pack_call(nx, ny, nz, n_tiles):
-    def kernel(p_hbm, s_hbm, m_hbm, head_lo, head_hi, track_lo, track_hi, p_lo, p_hi, s_lo, s_hi, m_ends, sem):
-        planes = [
-            (p_hbm, 0, head_lo, 0), (p_hbm, 1, head_lo, 1), (s_hbm, 0, head_lo, 2),
-            (p_hbm, nx - 2, head_hi, 0), (p_hbm, nx - 1, head_hi, 1), (s_hbm, nx - 1, head_hi, 2),
-        ]
-        copies = [
-            pltpu.make_async_copy(src.at[at], dst.at[pl.ds(n * ny, ny)], sem.at[i])
-            for i, (src, at, dst, n) in enumerate(planes)
-        ]
+def pack_call(nx, ny, nz):
+    def kernel(p_hbm, s_hbm, head_a, head_b, track_lo, track_hi, p_lo, p_hi, s_lo, s_hi, sem):
+        odd = place()[4]
+        copies = []
+        for i, (out, low) in enumerate(((head_a, odd), (head_b, 1 - odd))):
+            at_p = jnp.where(low > 0, 0, nx - 2)
+            at_s = jnp.where(low > 0, 0, nx - 1)
+            copies += [
+                pltpu.make_async_copy(p_hbm.at[at_p], out.at[pl.ds(0, ny)], sem.at[3 * i]),
+                pltpu.make_async_copy(p_hbm.at[at_p + 1], out.at[pl.ds(ny, ny)], sem.at[3 * i + 1]),
+                pltpu.make_async_copy(s_hbm.at[at_s], out.at[pl.ds(2 * ny, ny)], sem.at[3 * i + 2]),
+            ]
         rows = [(p_hbm, 0, p_lo), (p_hbm, ny - 8, p_hi), (s_hbm, 0, s_lo), (s_hbm, ny - 8, s_hi)]
         copies += [
             pltpu.make_async_copy(src.at[:, pl.ds(at, 8)], dst, sem.at[6 + i])
             for i, (src, at, dst) in enumerate(rows)
         ]
-        copies += [
-            pltpu.make_async_copy(
-                m_hbm.at[pl.ds(c * n_tiles + side * (n_tiles - 8), 8)], m_ends.at[2 * c + side], sem.at[10 + 2 * c + side]
-            )
-            for c in range(3)
-            for side in range(2)
-        ]
         for copy in copies:
             copy.start()
-        head_lo[pl.ds(3 * ny, 8), :] = jnp.zeros((8, nz), F32)
-        head_hi[pl.ds(3 * ny, 8), :] = jnp.zeros((8, nz), F32)
+        head_a[pl.ds(3 * ny, 8), :] = jnp.zeros((8, nz), F32)
+        head_b[pl.ds(3 * ny, 8), :] = jnp.zeros((8, nz), F32)
         for copy in copies[6:]:
             copy.wait()
-        for c in range(3):
-            head_lo[pl.ds(3 * ny + c, 1), :] = m_ends[2 * c, pl.ds(0, 1), :]
-            head_hi[pl.ds(3 * ny + c, 1), :] = m_ends[2 * c + 1, pl.ds(7, 1), :]
         for out, p_ref, s_ref, order in ((track_lo, p_lo, s_lo, (0, 1)), (track_hi, p_hi, s_hi, (7, 6))):
             p2 = p_ref.reshape(nx * 8, nz)
             s2 = s_ref.reshape(nx * 8, nz)
@@ -322,22 +328,43 @@
     return pl.pallas_call(
         kernel,
         out_shape=(head, head, track, track),
-        in_specs=[HBM] * 3,
+        in_specs=[HBM, HBM],
         out_specs=(VM,) * 4,
-        scratch_shapes=[eight] * 4 + [pltpu.VMEM((6, 8, LANES), F32), pltpu.SemaphoreType.DMA((16,))],
+        scratch_shapes=[eight] * 4 + [pltpu.SemaphoreType.DMA((10,))],
         compiler_params=pltpu.CompilerParams(vmem_limit_bytes=LARGE),
         cost_estimate=cost(10**6, 4 * 2**20),
         name="pack",
     )
 
 
+def ends_call(ny, n_tiles):
+    def kernel(m_ref, a_in, b_in, head_a, head_b):
+        flags = place()
+        for out, low in ((head_a, flags[4]), (head_b, 1 - flags[4])):
+            for c in range(3):
+                first = m_ref[pl.ds(c * n_tiles, 1), :]
+                last = m_ref[pl.ds((c + 1) * n_tiles - 1, 1), :]
+                out[pl.ds(3 * ny + c, 1), :] = jnp.where(low > 0, first, last)
+
+    head = jax.ShapeDtypeStruct((3 * ny + 8, LANES), F32)
+    return pl.pallas_call(
+        kernel, out_shape=(head, head), in_specs=[VM, VM, VM], out_specs=(VM, VM),
+        input_output_aliases={1: 0, 2: 1},
+        compiler_params=pltpu.CompilerParams(vmem_limit_bytes=SMALL),
+        cost_estimate=cost(10**5, 10**5), name="ends",
+    )
+
+
 def corner_call(nx, ny, nz):
-    def kernel(lo_in, hi_in, below, above, lo, hi):
+    def kernel(lo_in, hi_in, from_a, from_b, lo, hi):
+        odd = place()[4] > 0
         for src, dst, row in ((lo_in, lo, 0), (hi_in, hi, ny - 1)):
             dst[pl.ds(0, 3 * nx), :] = src[pl.ds(0, 3 * nx), :]
             dst[pl.ds(3 * nx, 8), :] = jnp.zeros((8, nz), F32)
-            dst[pl.ds(3 * nx, 1), :] = below[pl.ds(ny + row, 1), :]
-            dst[pl.ds(3 * nx + 1, 1), :] = above[pl.ds(row, 1), :]
+            below = pl.ds(ny + row, 1)
+            above = pl.ds(row, 1)
+            dst[pl.ds(3 * nx, 1), :] = jnp.where(odd, from_a[below, :], from_b[below, :])
+            dst[pl.ds(3 * nx + 1, 1), :] = jnp.where(odd, from_b[above, :], from_a[above, :])
 
     track = jax.ShapeDtypeStruct((3 * nx + 8, nz), F32)
     return pl.pallas_call(
@@ -463,7 +490,7 @@
     step = 4
     chunks = count // step
 
-    def kernel(flags, own_hbm, nxt_hbm, m_ref, below, above, ex, own, nxt, tiles, sem):
+    def kernel(own_hbm, nxt_hbm, m_ref, from_a, from_b, after, ex, own, nxt, tiles, sem):
         def copies(c):
             part = pl.ds(c * step, step)
             return [
@@ -475,8 +502,12 @@
             for copy in copies(c):
                 copy.start()
         tile_major(m_ref, tiles, n_tiles)
-        tiles[0] = jnp.where(flags[0] > 0, below[pl.ds(3 * ny, 8), :], 0.0)
-        tiles[n_tiles + 1] = jnp.where(flags[1] > 0, above[pl.ds(3 * ny, 8), :], 0.0)
+        flags = place()
+        odd = flags[4] > 0
+        by_a = from_a[pl.ds(3 * ny, 8), :]
+        by_b = from_b[pl.ds(3 * ny, 8), :]
+        tiles[0] = jnp.where(flags[0] > 0, jnp.where(odd, by_a, by_b), 0.0)
+        tiles[n_tiles + 1] = jnp.where(flags[1] > 0, jnp.where(odd, by_b, by_a), 0.0)
         for c in range(chunks):
             for copy in copies(c):
                 copy.wait()
@@ -488,7 +519,7 @@
     return pl.pallas_call(
         kernel,
         out_shape=jax.ShapeDtypeStruct((3 * count, LANES), F32),
-        in_specs=[SM, HBM, HBM, VM, VM, VM],
+        in_specs=[HBM, HBM, VM, VM, VM, ANY],
         out_specs=VM,
         scratch_shapes=[
             pltpu.VMEM((count, LANES, LANES), F32),
@@ -506,7 +537,7 @@
     per = cap // LANES
     slot_rows = n_track * per
 
-    def kernel(answers, slots, m_ref, ex_a, ex_b, target, applied, m_out, edge_lo, edge_hi, parts):
+    def kernel(answers, slots, m_ref, ex_a, ex_b, target, applied, m_out, edge_a, edge_b, parts):
         for c in range(3):
             rows = jnp.concatenate([answers[o, pl.ds(c * per, per), :] for o in range(n_track)], axis=0)
             hi, lo = split(rows)
@@ -529,12 +560,13 @@
             jnp.concatenate([ref[pl.ds(c * half, half), :] for ref in (ex_a, ex_b)], axis=0) for c in range(3)
         ]
         m = llb(m, [applied[part[c], :] + ex[c] for c in range(3)], target[...])
-        edge_lo[...] = jnp.zeros((8, LANES), F32)
-        edge_hi[...] = jnp.zeros((8, LANES), F32)
+        odd = place()[4] > 0
+        edge_a[...] = jnp.zeros((8, LANES), F32)
+        edge_b[...] = jnp.zeros((8, LANES), F32)
         for c in range(3):
             m_out[part[c], :] = m[c]
-            edge_lo[pl.ds(c, 1), :] = m[c][0:1]
-            edge_hi[pl.ds(c, 1), :] = m[c][n_tiles - 1 :]
+            edge_a[pl.ds(c, 1), :] = jnp.where(odd, m[c][0:1], m[c][n_tiles - 1 :])
+            edge_b[pl.ds(c, 1), :] = jnp.where(odd, m[c][n_tiles - 1 :], m[c][0:1])
 
     grains = jax.ShapeDtypeStruct((3 * n_tiles, LANES), F32)
     edge = jax.ShapeDtypeStruct((8, LANES), F32)
@@ -571,9 +603,13 @@
 
 
 def last_call(n_tiles):
-    def kernel(flags, m_ref, ex, applied, target, below, above, nxt, out):
-        low = both(jnp.where(flags[0] > 0, below[...], 0.0))
-        high = both(jnp.where(flags[1] > 0, above[...], 0.0))
+    def kernel(m_ref, ex, applied, target, from_a, from_b, nxt, out):
+        flags = place()
+        odd = flags[4] > 0
+        below = jnp.where(odd, from_a[...], from_b[...])
+        above = jnp.where(odd, from_b[...], from_a[...])
+        low = both(jnp.where(flags[0] > 0, below, 0.0))
+        high = both(jnp.where(flags[1] > 0, above, 0.0))
         hi, lo = split(nxt[0])
         first = fold(mm_nt(low, hi), mm_nt(low, lo))
         hi, lo = split(nxt[n_tiles - 1])
@@ -593,7 +629,7 @@
     return pl.pallas_call(
         kernel,
         out_shape=jax.ShapeDtypeStruct((3 * n_tiles, LANES), F32),
-        in_specs=[SM] + [VM] * 7,
+        in_specs=[VM] * 7,
         out_specs=VM,
         compiler_params=pltpu.CompilerParams(vmem_limit_bytes=SMALL),
         cost_estimate=cost(10**7, 2**20),
@@ -604,6 +640,13 @@
 def shifted(v, axis, by):
     n = lax.axis_size(axis)
     return lax.ppermute(v, axis, [(i, (i + by) % n) for i in range(n)])
+
+
+def traded(to_a, to_b, axis):
+    n = lax.axis_size(axis)
+    first = [(i, i ^ 1) for i in range(n)]
+    second = [(i, (i + 1) % n if i % 2 else (i - 1) % n) for i in range(n)]
+    return lax.ppermute(to_a, axis, first), lax.ppermute(to_b, axis, second)
 
 
 def per_device(
@@ -614,40 +657,36 @@
     n_tiles = self_tiles.shape[1]
     grains = footprint.shape[1]
     cap = 2 * grains // n_track
-    h = lax.axis_index("head")
-    t = lax.axis_index("track")
-    flags = jnp.stack([h > 0, h < lax.axis_size("head") - 1, t > 0, t < n_track - 1]).astype(jnp.int32)
     state = magnet.reshape(3 * n_tiles, LANES)
 
-    head_lo, head_hi, track_lo, track_hi = pack_call(nx, ny, nz, n_tiles)(potential, source, state)
-    below = shifted(head_hi, "head", 1)
-    above = shifted(head_lo, "head", -1)
+    head_a, head_b, track_lo, track_hi = pack_call(nx, ny, nz)(potential, source)
+    head_a, head_b = ends_call(ny, n_tiles)(state, head_a, head_b)
+    from_a, from_b = traded(head_a, head_b, "head")
     requests, slots, target = request_call(n_track, n_tiles, nx * ny, ny, cap)(
         footprint.reshape(n_tiles, LANES), temp_index.reshape(n_tiles, LANES), temp_profile[None, :]
     )
-    track_lo, track_hi = corner_call(nx, ny, nz)(track_lo, track_hi, below, above)
+    track_lo, track_hi = corner_call(nx, ny, nz)(track_lo, track_hi, from_a, from_b)
     left = shifted(track_hi, "track", 1)
     right = shifted(track_lo, "track", -1)
     asked = lax.all_to_all(requests.reshape(n_track, cap // LANES, LANES), "track", 0, 0)
 
     kern = jnp.pad(depth_kernel, ((0, 5), (0, 0)))
     half = n_tiles // 2
-    couplings = (flags, self_tiles[0], next_tiles[0], state, below, above)
+    couplings = (self_tiles[0], next_tiles[0], state, from_a, from_b, asked)
     ex_a = first_call(n_tiles, ny, 0, half)(*couplings)
     relaxed, reply = relax_call(nx, ny, nz, n_track, cap)(
-        flags, potential, source, below, above, left, right, track_lo, track_hi, kern,
+        potential, source, from_a, from_b, left, right, track_lo, track_hi, kern,
         asked.reshape(n_track * cap // LANES, LANES), ex_a,
     )
     answers = lax.all_to_all(reply, "track", 0, 0)
     ex_b = first_call(n_tiles, ny, half, n_tiles - half)(*couplings)
-    applied, state, edge_lo, edge_hi = section_call(n_tiles, n_track, cap)(
+    applied, state, edge_a, edge_b = section_call(n_tiles, n_track, cap)(
         answers, slots, state, ex_a, ex_b, target
     )
-    tile_below = shifted(edge_hi, "head", 1)
-    tile_above = shifted(edge_lo, "head", -1)
+    tile_a, tile_b = traded(edge_a, edge_b, "head")
     ex = second_call(n_tiles)(self_tiles[0], next_tiles[0], state)
     state = last_call(n_tiles)(
-        flags, state, ex, applied, target, tile_below, tile_above, next_tiles[0]
+        state, ex, applied, target, tile_a, tile_b, next_tiles[0]
     )
     return relaxed, state.reshape(3, 1, grains)
 

time: 60.1 us -> 57.1 us (0.950)
  waiting for transfers between devices: 4.81 us -> 6.99 us
  Pallas kernels: 32.2 us -> 30.1 us
  starting transfers between devices: 20.5 us -> 18.7 us
  local copies, waits for them, and re-layouts: 0.82 us -> 0.16 us
    ppermute x6 -> x2, starting transfers between devices: 9.11 us -> 4.83 us  [shifted(): return lax.ppermute(v, axis, [(i, (i + by) % n) for i in range(n)])]
    ppermute x0 -> x4, starting transfers between devices: none -> 3.86 us  [traded(): return (lax.ppermute(to_a, axis, first), lax.ppermute(to_b, axis, second))]
    all_to_all x1, waiting for transfers between devices: 0.01 us -> 1.99 us  [per_device(): lax.all_to_all(requests.reshape(n_track, cap // LANES, LANES), 'track', 0...]
    ppermute x6 -> x2, waiting for transfers between devices: 0.76 us -> 0.01 us  [shifted(): return lax.ppermute(v, axis, [(i, (i + by) % n) for i in range(n)])]
    all_to_all x1, starting transfers between devices: 6.59 us -> 5.84 us  [per_device(): lax.all_to_all(requests.reshape(n_track, cap // LANES, LANES), 'track', 0...]
    unnamed x16 -> x14, local copies, waits for them, and re-layouts: 0.82 us -> 0.15 us
    all_to_all x1, starting transfers between devices: 4.79 us -> 4.16 us  [per_device(): answers = lax.all_to_all(reply, 'track', 0, 0)]
    pallas_call x2 -> x3, Pallas kernels: 1.67 us -> 1.61 us  [the longest x1 1.57 us: per_device(): pack_call(nx, ny, nz)(potential, source)]
  transfers between devices with their start and end apart: 8 -> 8, of which waited for: 2 -> 3; matrix products, arithmetic and copies ran while one was open for 0% -> 0% of each run, Pallas kernels for 16% -> 15%
where the time goes in v3:
time: 57.1 us; the launch traced here: 56.7 us
  Pallas kernels  30.1 us (53%)
  starting transfers between devices  18.7 us (33%)
  waiting for transfers between devices  6.99 us (12%)
  between operations  0.79 us (1%)
    pallas_call x1, Pallas kernels, per_device(): relax_call(nx, ny, nz, n_track, cap)  18.3 us
    all_to_all x1, starting transfers between devices, per_device(): lax.all_to_all(requests.reshape(n_track, cap // LANES, LANES), 'track', 0...  5.84 us
    ppermute x2, starting transfers between devices, shifted(): return lax.ppermute(v, axis, [(i, (i + by) % n) for i in range(n)])  4.83 us
    all_to_all x1, waiting for transfers between devices, per_device(): answers = lax.all_to_all(reply, 'track', 0, 0)  4.52 us
    all_to_all x1, starting transfers between devices, per_device(): answers = lax.all_to_all(reply, 'track', 0, 0)  4.16 us
    ppermute x4, starting transfers between devices, traded(): return (lax.ppermute(to_a, axis, first), lax.ppermute(to_b, axis, second))  3.86 us
    pallas_call x1, Pallas kernels, per_device(): ex_b = first_call(n_tiles, ny, half, n_tiles - half)(*couplings)  2.59 us
    pallas_call x1, Pallas kernels, per_device(): ex_a = first_call(n_tiles, ny, 0, half)(*couplings)  2.44 us
  transfers between devices with their start and end apart: 8, of which 3 were waited for; matrix products, arithmetic and copies ran while one was open for 0% of the time, Pallas kernels for 15%

profile of v3, /device:TPU:0, one launch (start us, length us, event | category | flops | bytes accessed | tf_op | source)
XLA Modules:
  0.0 56.7 jit_solution(11370336914980339091)
XLA Ops:
  0.7 1.6 %pack.1 = (f32[392,128]{1,0:T(8,128)S(1)}, f32[392,128]{1,0:T(8,128)S(1)}, f32[200,128]{1,0:T(8,128)S(1)}, f32[200,128]{1,0:T(8,128)S(1)}) custom-call(f32[64,128,128]{2,1,0:T(8,128)} %p_hbm.3, f32[64,128,128]{2,1,0:T(8,128)} %s_hbm.3), custom_call_target="tpu_custom_call" | custom-call | flops 1000000 | bytes 4194304 | tf_op jit(solution)/shard_map/pack/pallas_call | solution.py:662
  2.3 0.5 collective-permute-start
  2.8 2.6 %collective-permute-start.1 = (f32[392,128]{1,0:T(8,128)S(1)}, f32[392,128]{1,0:T(8,128)S(1)}, u32[]{:S(2)}, u32[]{:S(2)}) collective-permute-start(f32[392,128]{1,0:T(8,128)S(1)} %get-tuple-element.22), channel_id=1, source_target_pairs={{0,24},{8,16},{16,8},{24,0},{1,25},{9,17},{17,9},{25,1},{2,26},{10... | collective-permute-start | bytes 602120 | tf_op jit(solution)/shard_map/ppermute | solution.py:649
  5.4 1.8 %requests.1 = (f32[64,128]{1,0:T(8,128)}, s32[32,128]{1,0:T(8,128)S(1)}, f32[32,128]{1,0:T(8,128)S(1)}) custom-call(s32[32,128]{1,0:T(8,128)S(1)} %bitcast.21, s32[32,128]{1,0:T(8,128)S(1)} %bitcast.22, f32[1,128]{1,0:T(1,128)S(1)} %bitcast.23), custom_call_target="tpu_custom_call" | custom-call | flops 100000000 | bytes 1048576 | tf_op jit(solution)/shard_map/requests/pallas_call | solution.py:665
  7.2 5.8 %all-to-all-start = ((f32[8,8,128]{2,1,0:T(8,128)}), f32[8,8,128]{2,1,0:T(8,128)S(1)}, u32[]{:S(2)}, u32[]{:S(2)}) async-start(f32[8,8,128]{2,1,0:T(8,128)} %bitcast.4), calls=%async_computation | async-start | bytes 65536 | tf_op jit(solution)/shard_map/all_to_all | solution.py:671
  13.1 0.0 collective-permute-done.from_a
  13.1 0.0 collective-permute-done.1.from_b
  13.1 2.1 %collective-permute-start.2 = (f32[200,128]{1,0:T(8,128)S(1)}, f32[200,128]{1,0:T(8,128)S(1)}, u32[]{:S(2)}, u32[]{:S(2)}) collective-permute-start(f32[200,128]{1,0:T(8,128)S(1)} %get-tuple-element.25.own_hi), channel_id=1, source_target_pairs={{0,1},{1,2},{2,3},{3,4},{4,5},{5,6},{6,7},{7,0},{8,9},{9,10},{10,1... | collective-permute-start | bytes 307208 | tf_op jit(solution)/shard_map/ppermute | solution.py:642
  15.2 2.8 %collective-permute-start.3 = (f32[200,128]{1,0:T(8,128)S(1)}, f32[200,128]{1,0:T(8,128)S(1)}, u32[]{:S(2)}, u32[]{:S(2)}) collective-permute-start(f32[200,128]{1,0:T(8,128)S(1)} %get-tuple-element.26.own_lo), channel_id=1, source_target_pairs={{0,7},{1,0},{2,1},{3,2},{4,3},{5,4},{6,5},{7,6},{8,15},{9,8},{10,9... | collective-permute-start | bytes 307208 | tf_op jit(solution)/shard_map/ppermute | solution.py:642
  18.0 2.0 %all-to-all-done.after = f32[8,8,128]{2,1,0:T(8,128)S(1)} async-done(((f32[8,8,128]{2,1,0:T(8,128)}), f32[8,8,128]{2,1,0:T(8,128)S(1)}, u32[]{:S(2)}, u32[]{:S(2)}) %all-to-all-start) | async-done | bytes 32800 | tf_op jit(solution)/shard_map/all_to_all | solution.py:671
  19.9 2.4 %couple_first.2.ex_hbm.ex_a = f32[48,128]{1,0:T(8,128)S(1)} custom-call(f32[32,128,128]{2,1,0:T(8,128)} %bitcast.13, f32[32,128,128]{2,1,0:T(8,128)} %bitcast.9, f32[96,128]{1,0:T(8,128)S(1)} %bitcast.17, f32[392,128]{1,0:T(8,128)S(1)} %collective-permute-done.from_a, f32[392,128]{1,0:T(8,128)S(1)} %collective-permute-done.1.from_b, ...), custom_call_target="tpu_custom_call" | custom-call | flops 1000000000 | bytes 4194304 | tf_op jit(solution)/shard_map/couple_first/pallas_call | solution.py:676
  22.4 0.0 collective-permute-done.2.tlo
  22.4 0.0 collective-permute-done.3.thi
  22.4 18.3 %relax.1 = (f32[64,128,128]{2,1,0:T(8,128)}, f32[8,24,128]{2,1,0:T(8,128)}) custom-call(f32[64,128,128]{2,1,0:T(8,128)} %p_hbm.3, f32[64,128,128]{2,1,0:T(8,128)} %s_hbm.3, f32[392,128]{1,0:T(8,128)S(1)} %collective-permute-done.from_a, f32[392,128]{1,0:T(8,128)S(1)} %collective-permute-done.1.from_b, f32[200,128]{1,0:T(8,128)S(1)} %collective-permute-done.2.tlo, ...), custom_call_target="tpu_custom_call" | custom-call | flops 104857600 | bytes 12582912 | tf_op jit(solution)/shard_map/relax/pallas_call | solution.py:677
  40.7 4.2 %all-to-all-start.1 = ((f32[8,24,128]{2,1,0:T(8,128)}), f32[8,24,128]{2,1,0:T(8,128)S(1)}, u32[]{:S(2)}, u32[]{:S(2)}) async-start(f32[8,24,128]{2,1,0:T(8,128)} %get-tuple-element.29), calls=%async_computation.1 | async-start | bytes 196608 | tf_op jit(solution)/shard_map/all_to_all | solution.py:681
  44.9 2.6 %couple_first.3.ex_b = f32[48,128]{1,0:T(8,128)S(1)} custom-call(f32[32,128,128]{2,1,0:T(8,128)} %bitcast.14, f32[32,128,128]{2,1,0:T(8,128)} %bitcast.10, f32[96,128]{1,0:T(8,128)S(1)} %bitcast.18, f32[392,128]{1,0:T(8,128)S(1)} %collective-permute-done.from_a, f32[392,128]{1,0:T(8,128)S(1)} %collective-permute-done.1.from_b, ...), custom_call_target="tpu_custom_call" | custom-call | flops 1000000000 | bytes 4194304 | tf_op jit(solution)/shard_map/couple_first/pallas_call | solution.py:682
  47.5 4.5 %all-to-all-done.1.answers = f32[8,24,128]{2,1,0:T(8,128)S(1)} async-done(((f32[8,24,128]{2,1,0:T(8,128)}), f32[8,24,128]{2,1,0:T(8,128)S(1)}, u32[]{:S(2)}, u32[]{:S(2)}) %all-to-all-start.1) | async-done | bytes 98336 | tf_op jit(solution)/shard_map/all_to_all | solution.py:681
  52.0 0.7 %section_first.1 = (f32[96,128]{1,0:T(8,128)S(1)}, f32[96,128]{1,0:T(8,128)S(1)}, f32[8,128]{1,0:T(8,128)S(1)}, f32[8,128]{1,0:T(8,128)S(1)}) custom-call(f32[8,24,128]{2,1,0:T(8,128)S(1)} %all-to-all-done.1.answers, s32[32,128]{1,0:T(8,128)S(1)} %get-tuple-element.30.slots, f32[96,128]{1,0:T(8,128)S(1)} %bitcast.19, f32[48,128]{1,0:T(8,128)S(1)} %couple_first.2.ex_hbm.ex_a, ...), custom_call_target="tpu_custom_call" | custom-call | flops 1000000000 | bytes 1048576 | tf_op jit(solution)/shard_map/section_first/pallas_call | solution.py:683
  52.8 0.1 collective-permute-start.4
  52.8 0.7 %collective-permute-start.5 = (f32[8,128]{1,0:T(8,128)S(1)}, f32[8,128]{1,0:T(8,128)S(1)}, u32[]{:S(2)}, u32[]{:S(2)}) collective-permute-start(f32[8,128]{1,0:T(8,128)S(1)} %get-tuple-element.35), channel_id=1, source_target_pairs={{0,24},{8,16},{16,8},{24,0},{1,25},{9,17},{17,9},{25,1},{2,26},{10... | collective-permute-start | bytes 12296 | tf_op jit(solution)/shard_map/ppermute | solution.py:649
  53.5 0.1 copy-done.1
  53.6 1.8 %couple_second.1.ex = f32[96,128]{1,0:T(8,128)S(1)} custom-call(f32[32,128,128]{2,1,0:T(8,128)S(1)} %bitcast.15, f32[32,128,128]{2,1,0:T(8,128)S(1)} %bitcast.11, f32[96,128]{1,0:T(8,128)S(1)} %get-tuple-element.32.m_ref), custom_call_target="tpu_custom_call" | custom-call | flops 1000000000 | bytes 4194304 | tf_op jit(solution)/shard_map/couple_second/pallas_call | solution.py:687
  55.5 0.5 collective-permute-done.5.from_b
  55.9 0.8 %section_last.1 = f32[96,128]{1,0:T(8,128)} custom-call(f32[96,128]{1,0:T(8,128)S(1)} %get-tuple-element.32.m_ref, f32[96,128]{1,0:T(8,128)S(1)} %couple_second.1.ex, f32[96,128]{1,0:T(8,128)S(1)} %get-tuple-element.33.applied, f32[32,128]{1,0:T(8,128)S(1)} %get-tuple-element.31.target, f32[8,128]{1,0:T(8,128)S(1)} %collective-permute-done.4.from_a, ...), custom_call_target="tpu_custom_call" | custom-call | flops 10000000 | bytes 1048576 | tf_op jit(solution)/shard_map/section_last/pallas_call | solution.py:688
  (17 shorter events, 0.1 us)
Async XLA Ops:
  0.6 1.6 %copy-start.2 = (f32[3,1,4096]{2,1,0:T(1,128)S(1)}, f32[3,1,4096]{2,1,0:T(1,128)}, u32[]{:S(2)}) copy-start(f32[3,1,4096]{2,1,0:T(1,128)} %param.12) | copy-start | bytes 147460
  0.6 4.8 %copy-start.3 = (s32[1,4096]{1,0:T(1,128)S(1)}, s32[1,4096]{1,0:T(1,128)}, u32[]{:S(2)}) copy-start(s32[1,4096]{1,0:T(1,128)} %param.13) | copy-start | bytes 49156
  0.7 4.8 %copy-start.4 = (s32[1,4096]{1,0:T(1,128)S(1)}, s32[1,4096]{1,0:T(1,128)}, u32[]{:S(2)}) copy-start(s32[1,4096]{1,0:T(1,128)} %param.14) | copy-start | bytes 49156
  0.7 4.8 %copy-start.5 = (f32[128]{0:T(128)S(1)}, f32[128]{0:T(128)}, u32[]{:S(2)}) copy-start(f32[128]{0:T(128)} %param.15) | copy-start | bytes 1540
  0.7 17.3 %copy-start.6 = (f32[3,128]{1,0:T(4,128)S(1)}, f32[3,128]{1,0:T(4,128)}, u32[]{:S(2)}) copy-start(f32[3,128]{1,0:T(4,128)} %param.11) | copy-start | bytes 4612
  2.3 10.8 %collective-permute-start = (f32[392,128]{1,0:T(8,128)S(1)}, f32[392,128]{1,0:T(8,128)S(1)}, u32[]{:S(2)}, u32[]{:S(2)}) collective-permute-start(f32[392,128]{1,0:T(8,128)S(1)} %get-tuple-element.21), channel_id=1, source_target_pairs={{0,8},{8,0},{16,24},{24,16},{1,9},{9,1},{17,25},{25,17},{2,10},{10... | collective-permute-start | bytes 602120 | tf_op jit(solution)/shard_map/ppermute | solution.py:649
  2.8 10.3 %collective-permute-start.1 = (f32[392,128]{1,0:T(8,128)S(1)}, f32[392,128]{1,0:T(8,128)S(1)}, u32[]{:S(2)}, u32[]{:S(2)}) collective-permute-start(f32[392,128]{1,0:T(8,128)S(1)} %get-tuple-element.22), channel_id=1, source_target_pairs={{0,24},{8,16},{16,8},{24,0},{1,25},{9,17},{17,9},{25,1},{2,26},{10... | collective-permute-start | bytes 602120 | tf_op jit(solution)/shard_map/ppermute | solution.py:649
  7.2 12.7 %all-to-all-start = ((f32[8,8,128]{2,1,0:T(8,128)}), f32[8,8,128]{2,1,0:T(8,128)S(1)}, u32[]{:S(2)}, u32[]{:S(2)}) async-start(f32[8,8,128]{2,1,0:T(8,128)} %bitcast.4), calls=%async_computation | async-start | bytes 65536 | tf_op jit(solution)/shard_map/all_to_all | solution.py:671
  13.1 9.3 %collective-permute-start.2 = (f32[200,128]{1,0:T(8,128)S(1)}, f32[200,128]{1,0:T(8,128)S(1)}, u32[]{:S(2)}, u32[]{:S(2)}) collective-permute-start(f32[200,128]{1,0:T(8,128)S(1)} %get-tuple-element.25.own_hi), channel_id=1, source_target_pairs={{0,1},{1,2},{2,3},{3,4},{4,5},{5,6},{6,7},{7,0},{8,9},{9,10},{10,1... | collective-permute-start | bytes 307208 | tf_op jit(solution)/shard_map/ppermute | solution.py:642
  15.2 7.2 %collective-permute-start.3 = (f32[200,128]{1,0:T(8,128)S(1)}, f32[200,128]{1,0:T(8,128)S(1)}, u32[]{:S(2)}, u32[]{:S(2)}) collective-permute-start(f32[200,128]{1,0:T(8,128)S(1)} %get-tuple-element.26.own_lo), channel_id=1, source_target_pairs={{0,7},{1,0},{2,1},{3,2},{4,3},{5,4},{6,5},{7,6},{8,15},{9,8},{10,9... | collective-permute-start | bytes 307208 | tf_op jit(solution)/shard_map/ppermute | solution.py:642
  40.7 11.3 %all-to-all-start.1 = ((f32[8,24,128]{2,1,0:T(8,128)}), f32[8,24,128]{2,1,0:T(8,128)S(1)}, u32[]{:S(2)}, u32[]{:S(2)}) async-start(f32[8,24,128]{2,1,0:T(8,128)} %get-tuple-element.29), calls=%async_computation.1 | async-start | bytes 196608 | tf_op jit(solution)/shard_map/all_to_all | solution.py:681
  44.9 8.6 %copy-start = (f32[1,32,128,128]{3,2,1,0:T(8,128)S(1)}, f32[1,32,128,128]{3,2,1,0:T(8,128)}, u32[]{:S(2)}) copy-start(f32[1,32,128,128]{3,2,1,0:T(8,128)} %param.17) | copy-start | bytes 6291460
  52.0 1.6 %copy-start.1 = (f32[1,32,128,128]{3,2,1,0:T(8,128)S(1)}, f32[1,32,128,128]{3,2,1,0:T(8,128)}, u32[]{:S(2)}) copy-start(f32[1,32,128,128]{3,2,1,0:T(8,128)} %param.16) | copy-start | bytes 6291460
  52.8 2.7 %collective-permute-start.4 = (f32[8,128]{1,0:T(8,128)S(1)}, f32[8,128]{1,0:T(8,128)S(1)}, u32[]{:S(2)}, u32[]{:S(2)}) collective-permute-start(f32[8,128]{1,0:T(8,128)S(1)} %get-tuple-element.34), channel_id=1, source_target_pairs={{0,8},{8,0},{16,24},{24,16},{1,9},{9,1},{17,25},{25,17},{2,10},{10... | collective-permute-start | bytes 12296 | tf_op jit(solution)/shard_map/ppermute | solution.py:649
  52.8 3.1 %collective-permute-start.5 = (f32[8,128]{1,0:T(8,128)S(1)}, f32[8,128]{1,0:T(8,128)S(1)}, u32[]{:S(2)}, u32[]{:S(2)}) collective-permute-start(f32[8,128]{1,0:T(8,128)S(1)} %get-tuple-element.35), channel_id=1, source_target_pairs={{0,24},{8,16},{16,8},{24,0},{1,25},{9,17},{17,9},{25,1},{2,26},{10... | collective-permute-start | bytes 12296 | tf_op jit(solution)/shard_map/ppermute | solution.py:649

commit v4 on v3

--- a/solution.py
+++ b/solution.py
@@ -80,8 +80,8 @@
     per = cap // LANES
     rows = ny + 2 * TOP
 
-    def kernel(p_hbm, s_hbm, from_a, from_b, tlo, thi, own_lo, own_hi, kern, requests, ex_hbm, o_hbm, reply,
-               table, parts, pe, q, sb, ob, fx1, mx1, fx2, mx2, fy1, my1, fy2, my2, psem, ssem, osem):
+    def kernel(p_hbm, s_hbm, from_a, from_b, tlo, thi, own_lo, own_hi, kern, requests, ex_hbm, o_hbm, reply_out,
+               reply, rsem, table, parts, pe, q, sb, ob, fx1, mx1, fx2, mx2, fy1, my1, fy2, my2, psem, ssem, osem):
         n_chunk = nx // chunk
 
         def pcopy(c):
@@ -252,13 +252,23 @@
             hi, lo = split(flat[pl.ds(UNIT * 8 + c, nx, stride=8), :])
             parts[pl.ds(c * nx, nx), pl.ds(0, ny)] = hi
             parts[pl.ds(c * nx, nx), pl.ds(ny, ny)] = lo
-        asked = requests[...].astype(jnp.int32)
+        asked = requests[...]
+
+        share = n_track // 4
+
+        def rcopy(n):
+            part = pl.ds(n * share, share)
+            return pltpu.make_async_copy(reply.at[part], reply_out.at[part], rsem.at[n])
 
         def answer(j, values):
             for c in range(3):
                 reply[j // per, pl.ds(c * per + j % per, 1), :] = values[c]
+            if (j + 1) % (share * per) == 0:
+                rcopy(j // (share * per)).start()
 
         look_up_all(parts[...], asked & (ny - 1), lax.shift_right_logical(asked, int(math.log2(ny))), nx, ny, answer)
+        for n in range(4):
+            rcopy(n).wait()
         for c in range(n_chunk):
             ocopy(c).wait()
 
@@ -274,8 +284,9 @@
             jax.ShapeDtypeStruct((n_track, 3 * per, 128), f32),
         ),
         in_specs=[hbm, hbm] + [vm] * 8 + [pl.BlockSpec(memory_space=pl.ANY)],
-        out_specs=(hbm, vm),
+        out_specs=(hbm, hbm),
         scratch_shapes=[
+            pltpu.VMEM((n_track, 3 * per, 128), f32), pltpu.SemaphoreType.DMA((4,)),
             pltpu.VMEM((nx + UNIT, 8, ny), f32), pltpu.VMEM((3 * nx, 2 * ny), jnp.bfloat16),
             pltpu.VMEM((nx + 4, rows, nz), f32), pltpu.VMEM((nx + 2, rows, nz), f32),
             pltpu.VMEM((nx + 2, ny, nz), f32), pltpu.VMEM((nx + UNIT, ny, nz), f32),
@@ -402,13 +413,17 @@
         low = (cell & (width - 1)).astype(F32)
         rows = lax.broadcasted_iota(jnp.int32, (slot_rows, LANES), 0)
         found = jnp.zeros((2 * slot_rows, LANES), F32)
-        for k in range(n_tiles):
-            here = rows == at_row[k : k + 1]
-            values = jnp.concatenate(
-                [jnp.where(here, high[k : k + 1], 0.0), jnp.where(here, low[k : k + 1], 0.0)], axis=0
-            ).astype(BF16)
-            lanes = (row == at_lane[k : k + 1]).astype(F32).astype(BF16)
-            found = found + mm_nt(values, lanes)
+        row_b = row.astype(F32).astype(BF16)
+        lane_b = at_lane.astype(F32).astype(BF16)
+        for k in range(0, n_tiles, 2):
+            values = []
+            lanes = []
+            for i in (k, k + 1):
+                here = rows == at_row[i : i + 1]
+                parts = [jnp.where(here, v[i : i + 1], 0.0) for v in (high, low)]
+                values.append(jnp.concatenate(parts, axis=0).astype(BF16))
+                lanes.append(jnp.where(row_b == lane_b[i : i + 1], jnp.array(1, BF16), jnp.array(0, BF16)))
+            found = found + mm_nt(jnp.concatenate(values, axis=1), jnp.concatenate(lanes, axis=1))
         requests[...] = found[:slot_rows] * float(width) + found[slot_rows:]
         spread = jnp.broadcast_to(profile[...], (n_tiles, profile.shape[1]))
         temp = jnp.take_along_axis(spread, index[...], axis=1)
@@ -490,7 +505,7 @@
     step = 4
     chunks = count // step
 
-    def kernel(own_hbm, nxt_hbm, m_ref, from_a, from_b, after, ex, own, nxt, tiles, sem):
+    def kernel(own_hbm, nxt_hbm, m_ref, from_a, from_b, ex, own, nxt, tiles, sem):
         def copies(c):
             part = pl.ds(c * step, step)
             return [
@@ -519,7 +534,7 @@
     return pl.pallas_call(
         kernel,
         out_shape=jax.ShapeDtypeStruct((3 * count, LANES), F32),
-        in_specs=[HBM, HBM, VM, VM, VM, ANY],
+        in_specs=[HBM, HBM, VM, VM, VM],
         out_specs=VM,
         scratch_shapes=[
             pltpu.VMEM((count, LANES, LANES), F32),
@@ -528,7 +543,7 @@
             pltpu.SemaphoreType.DMA((2, chunks)),
         ],
         compiler_params=pltpu.CompilerParams(vmem_limit_bytes=LARGE),
-        cost_estimate=cost(10**9, 4 * 2**20),
+        cost_estimate=cost(1, 1),
         name="couple_first",
     )
 
@@ -649,6 +664,17 @@
     return lax.ppermute(to_a, axis, first), lax.ppermute(to_b, axis, second)
 
 
+def cells_call(rows):
+    def kernel(asked, ex, cells):
+        cells[...] = asked[...].astype(jnp.int32)
+
+    return pl.pallas_call(
+        kernel, out_shape=jax.ShapeDtypeStruct((rows, LANES), jnp.int32), in_specs=[VM, ANY], out_specs=VM,
+        compiler_params=pltpu.CompilerParams(vmem_limit_bytes=SMALL),
+        cost_estimate=cost(10**9, 4 * 2**20), name="cells",
+    )
+
+
 def per_device(
     potential, source, depth_kernel, magnet, footprint, temp_index, temp_profile, self_tiles, next_tiles
 ):
@@ -672,11 +698,12 @@
 
     kern = jnp.pad(depth_kernel, ((0, 5), (0, 0)))
     half = n_tiles // 2
-    couplings = (self_tiles[0], next_tiles[0], state, from_a, from_b, asked)
+    couplings = (self_tiles[0], next_tiles[0], state, from_a, from_b)
     ex_a = first_call(n_tiles, ny, 0, half)(*couplings)
+    asked = cells_call(n_track * cap // LANES)(asked.reshape(n_track * cap // LANES, LANES), ex_a)
     relaxed, reply = relax_call(nx, ny, nz, n_track, cap)(
         potential, source, from_a, from_b, left, right, track_lo, track_hi, kern,
-        asked.reshape(n_track * cap // LANES, LANES), ex_a,
+        asked, ex_a,
     )
     answers = lax.all_to_all(reply, "track", 0, 0)
     ex_b = first_call(n_tiles, ny, half, n_tiles - half)(*couplings)

time: 57.1 us -> 56.7 us (level)
    all_to_all x1, waiting for transfers between devices: 1.99 us -> 0.01 us  [per_device(): lax.all_to_all(requests.reshape(n_track, cap // LANES, LANES), 'track', 0...]
    ppermute x2, waiting for transfers between devices: 0.01 us -> 1.56 us  [shifted(): return lax.ppermute(v, axis, [(i, (i + by) % n) for i in range(n)])]
  transfers between devices with their start and end apart: 8 -> 8, of which waited for: 3 -> 4; matrix products, arithmetic and copies ran while one was open for 0% -> 0% of each run, Pallas kernels for 15% -> 15%
where the time goes in v4:
time: 56.7 us; the launch traced here: 56.3 us
  Pallas kernels  29.7 us (52%)
  starting transfers between devices  19.1 us (34%)
  waiting for transfers between devices  6.56 us (12%)
  between operations  0.79 us (1%)
    pallas_call x1, Pallas kernels, per_device(): relax_call(nx, ny, nz, n_track, cap)  18.2 us
    all_to_all x1, starting transfers between devices, per_device(): lax.all_to_all(requests.reshape(n_track, cap // LANES, LANES), 'track', 0...  5.83 us
    ppermute x2, starting transfers between devices, shifted(): return lax.ppermute(v, axis, [(i, (i + by) % n) for i in range(n)])  4.83 us
    all_to_all x1, starting transfers between devices, per_device(): answers = lax.all_to_all(reply, 'track', 0, 0)  4.6 us
    all_to_all x1, waiting for transfers between devices, per_device(): answers = lax.all_to_all(reply, 'track', 0, 0)  4.52 us
    ppermute x4, starting transfers between devices, traded(): return (lax.ppermute(to_a, axis, first), lax.ppermute(to_b, axis, second))  3.84 us
    pallas_call x1, Pallas kernels, per_device(): ex_b = first_call(n_tiles, ny, half, n_tiles - half)(*couplings)  2.59 us
    pallas_call x1, Pallas kernels, per_device(): ex_a = first_call(n_tiles, ny, 0, half)(*couplings)  2.44 us
  transfers between devices with their start and end apart: 8, of which 4 were waited for; matrix products, arithmetic and copies ran while one was open for 0% of the time, Pallas kernels for 15%

profile of v4, /device:TPU:0, one launch (start us, length us, event | category | flops | bytes accessed | tf_op | source)
XLA Modules:
  0.0 56.3 jit_solution(12410893042243530935)
XLA Ops:
  0.7 1.6 %pack.1 = (f32[392,128]{1,0:T(8,128)S(1)}, f32[392,128]{1,0:T(8,128)S(1)}, f32[200,128]{1,0:T(8,128)S(1)}, f32[200,128]{1,0:T(8,128)S(1)}) custom-call(f32[64,128,128]{2,1,0:T(8,128)} %p_hbm.3, f32[64,128,128]{2,1,0:T(8,128)} %s_hbm.3), custom_call_target="tpu_custom_call" | custom-call | flops 1000000 | bytes 4194304 | tf_op jit(solution)/shard_map/pack/pallas_call | solution.py:688
  2.3 0.5 collective-permute-start
  2.8 2.6 %collective-permute-start.1 = (f32[392,128]{1,0:T(8,128)S(1)}, f32[392,128]{1,0:T(8,128)S(1)}, u32[]{:S(2)}, u32[]{:S(2)}) collective-permute-start(f32[392,128]{1,0:T(8,128)S(1)} %get-tuple-element.22), channel_id=1, source_target_pairs={{0,24},{8,16},{16,8},{24,0},{1,25},{9,17},{17,9},{25,1},{2,26},{10... | collective-permute-start | bytes 602120 | tf_op jit(solution)/shard_map/ppermute | solution.py:664
  5.4 1.4 %requests.1 = (f32[64,128]{1,0:T(8,128)}, s32[32,128]{1,0:T(8,128)S(1)}, f32[32,128]{1,0:T(8,128)S(1)}) custom-call(s32[32,128]{1,0:T(8,128)S(1)} %bitcast.21, s32[32,128]{1,0:T(8,128)S(1)} %bitcast.22, f32[1,128]{1,0:T(1,128)S(1)} %bitcast.23), custom_call_target="tpu_custom_call" | custom-call | flops 100000000 | bytes 1048576 | tf_op jit(solution)/shard_map/requests/pallas_call | solution.py:691
  6.8 5.8 %all-to-all-start = ((f32[8,8,128]{2,1,0:T(8,128)}), f32[8,8,128]{2,1,0:T(8,128)S(1)}, u32[]{:S(2)}, u32[]{:S(2)}) async-start(f32[8,8,128]{2,1,0:T(8,128)} %bitcast.4), calls=%async_computation | async-start | bytes 65536 | tf_op jit(solution)/shard_map/all_to_all | solution.py:697
  12.7 0.0 collective-permute-done.from_a
  12.7 0.0 collective-permute-done.1.from_b
  12.7 2.1 %collective-permute-start.2 = (f32[200,128]{1,0:T(8,128)S(1)}, f32[200,128]{1,0:T(8,128)S(1)}, u32[]{:S(2)}, u32[]{:S(2)}) collective-permute-start(f32[200,128]{1,0:T(8,128)S(1)} %get-tuple-element.25.own_hi), channel_id=1, source_target_pairs={{0,1},{1,2},{2,3},{3,4},{4,5},{5,6},{6,7},{7,0},{8,9},{9,10},{10,1... | collective-permute-start | bytes 307208 | tf_op jit(solution)/shard_map/ppermute | solution.py:657
  14.8 2.8 %collective-permute-start.3 = (f32[200,128]{1,0:T(8,128)S(1)}, f32[200,128]{1,0:T(8,128)S(1)}, u32[]{:S(2)}, u32[]{:S(2)}) collective-permute-start(f32[200,128]{1,0:T(8,128)S(1)} %get-tuple-element.26.own_lo), channel_id=1, source_target_pairs={{0,7},{1,0},{2,1},{3,2},{4,3},{5,4},{6,5},{7,6},{8,15},{9,8},{10,9... | collective-permute-start | bytes 307208 | tf_op jit(solution)/shard_map/ppermute | solution.py:657
  17.6 2.4 %couple_first.2.ex.ex_hbm.ex_a = f32[48,128]{1,0:T(8,128)S(1)} custom-call(f32[32,128,128]{2,1,0:T(8,128)} %bitcast.13, f32[32,128,128]{2,1,0:T(8,128)} %bitcast.9, f32[96,128]{1,0:T(8,128)S(1)} %bitcast.17, f32[392,128]{1,0:T(8,128)S(1)} %collective-permute-done.from_a, f32[392,128]{1,0:T(8,128)S(1)} %collective-permute-done.1.from_b), custom_call_target="tpu_custom_call" | custom-call | flops 1 | bytes 1 | tf_op jit(solution)/shard_map/couple_first/pallas_call | solution.py:702
  20.0 0.7 %collective-permute-done.2.tlo = f32[200,128]{1,0:T(8,128)S(1)} collective-permute-done((f32[200,128]{1,0:T(8,128)S(1)}, f32[200,128]{1,0:T(8,128)S(1)}, u32[]{:S(2)}, u32[]{:S(2)}) %collective-permute-start.2) | collective-permute-done | bytes 102432 | tf_op jit(solution)/shard_map/ppermute | solution.py:657
  20.8 0.8 %collective-permute-done.3.thi = f32[200,128]{1,0:T(8,128)S(1)} collective-permute-done((f32[200,128]{1,0:T(8,128)S(1)}, f32[200,128]{1,0:T(8,128)S(1)}, u32[]{:S(2)}, u32[]{:S(2)}) %collective-permute-start.3) | collective-permute-done | bytes 102432 | tf_op jit(solution)/shard_map/ppermute | solution.py:657
  21.6 18.2 %relax.1 = (f32[64,128,128]{2,1,0:T(8,128)}, f32[8,24,128]{2,1,0:T(8,128)}) custom-call(f32[64,128,128]{2,1,0:T(8,128)} %p_hbm.3, f32[64,128,128]{2,1,0:T(8,128)} %s_hbm.3, f32[392,128]{1,0:T(8,128)S(1)} %collective-permute-done.from_a, f32[392,128]{1,0:T(8,128)S(1)} %collective-permute-done.1.from_b, f32[200,128]{1,0:T(8,128)S(1)} %collective-permute-done.2.tlo, ...), custom_call_target="tpu_custom_call" | custom-call | flops 104857600 | bytes 12582912 | tf_op jit(solution)/shard_map/relax/pallas_call | solution.py:704
  39.8 4.6 %all-to-all-start.1 = ((f32[8,24,128]{2,1,0:T(8,128)}), f32[8,24,128]{2,1,0:T(8,128)S(1)}, u32[]{:S(2)}, u32[]{:S(2)}) async-start(f32[8,24,128]{2,1,0:T(8,128)} %get-tuple-element.29), calls=%async_computation.1 | async-start | bytes 196608 | tf_op jit(solution)/shard_map/all_to_all | solution.py:708
  44.5 2.6 %couple_first.3.ex_b = f32[48,128]{1,0:T(8,128)S(1)} custom-call(f32[32,128,128]{2,1,0:T(8,128)} %bitcast.14, f32[32,128,128]{2,1,0:T(8,128)} %bitcast.10, f32[96,128]{1,0:T(8,128)S(1)} %bitcast.18, f32[392,128]{1,0:T(8,128)S(1)} %collective-permute-done.from_a, f32[392,128]{1,0:T(8,128)S(1)} %collective-permute-done.1.from_b), custom_call_target="tpu_custom_call" | custom-call | flops 1 | bytes 1 | tf_op jit(solution)/shard_map/couple_first/pallas_call | solution.py:709
  47.1 4.5 %all-to-all-done.1.answers = f32[8,24,128]{2,1,0:T(8,128)S(1)} async-done(((f32[8,24,128]{2,1,0:T(8,128)}), f32[8,24,128]{2,1,0:T(8,128)S(1)}, u32[]{:S(2)}, u32[]{:S(2)}) %all-to-all-start.1) | async-done | bytes 98336 | tf_op jit(solution)/shard_map/all_to_all | solution.py:708
  51.6 0.7 %section_first.1 = (f32[96,128]{1,0:T(8,128)S(1)}, f32[96,128]{1,0:T(8,128)S(1)}, f32[8,128]{1,0:T(8,128)S(1)}, f32[8,128]{1,0:T(8,128)S(1)}) custom-call(f32[8,24,128]{2,1,0:T(8,128)S(1)} %all-to-all-done.1.answers, s32[32,128]{1,0:T(8,128)S(1)} %get-tuple-element.30.slots, f32[96,128]{1,0:T(8,128)S(1)} %bitcast.19, ...), custom_call_target="tpu_custom_call" | custom-call | flops 1000000000 | bytes 1048576 | tf_op jit(solution)/shard_map/section_first/pallas_call | solution.py:710
  52.3 0.1 collective-permute-start.4
  52.4 0.6 %collective-permute-start.5 = (f32[8,128]{1,0:T(8,128)S(1)}, f32[8,128]{1,0:T(8,128)S(1)}, u32[]{:S(2)}, u32[]{:S(2)}) collective-permute-start(f32[8,128]{1,0:T(8,128)S(1)} %get-tuple-element.35), channel_id=1, source_target_pairs={{0,24},{8,16},{16,8},{24,0},{1,25},{9,17},{17,9},{25,1},{2,26},{10... | collective-permute-start | bytes 12296 | tf_op jit(solution)/shard_map/ppermute | solution.py:664
  53.0 0.1 copy-done.1
  53.2 1.8 %couple_second.1.ex = f32[96,128]{1,0:T(8,128)S(1)} custom-call(f32[32,128,128]{2,1,0:T(8,128)S(1)} %bitcast.15, f32[32,128,128]{2,1,0:T(8,128)S(1)} %bitcast.11, f32[96,128]{1,0:T(8,128)S(1)} %get-tuple-element.32.m_ref), custom_call_target="tpu_custom_call" | custom-call | flops 1000000000 | bytes 4194304 | tf_op jit(solution)/shard_map/couple_second/pallas_call | solution.py:714
  55.0 0.0 collective-permute-done.4.from_a
  55.0 0.5 collective-permute-done.5.from_b
  55.5 0.8 %section_last.1 = f32[96,128]{1,0:T(8,128)} custom-call(f32[96,128]{1,0:T(8,128)S(1)} %get-tuple-element.32.m_ref, f32[96,128]{1,0:T(8,128)S(1)} %couple_second.1.ex, f32[96,128]{1,0:T(8,128)S(1)} %get-tuple-element.33.applied, f32[32,128]{1,0:T(8,128)S(1)} %get-tuple-element.31.target, f32[8,128]{1,0:T(8,128)S(1)} %collective-permute-done.4.from_a, ...), custom_call_target="tpu_custom_call" | custom-call | flops 10000000 | bytes 1048576 | tf_op jit(solution)/shard_map/section_last/pallas_call | solution.py:715
  (18 shorter events, 0.1 us)
Async XLA Ops:
  0.6 1.6 %copy-start.2 = (f32[3,1,4096]{2,1,0:T(1,128)S(1)}, f32[3,1,4096]{2,1,0:T(1,128)}, u32[]{:S(2)}) copy-start(f32[3,1,4096]{2,1,0:T(1,128)} %param.12) | copy-start | bytes 147460
  0.6 4.8 %copy-start.3 = (s32[1,4096]{1,0:T(1,128)S(1)}, s32[1,4096]{1,0:T(1,128)}, u32[]{:S(2)}) copy-start(s32[1,4096]{1,0:T(1,128)} %param.13) | copy-start | bytes 49156
  0.7 4.8 %copy-start.4 = (s32[1,4096]{1,0:T(1,128)S(1)}, s32[1,4096]{1,0:T(1,128)}, u32[]{:S(2)}) copy-start(s32[1,4096]{1,0:T(1,128)} %param.14) | copy-start | bytes 49156
  0.7 4.8 %copy-start.5 = (f32[128]{0:T(128)S(1)}, f32[128]{0:T(128)}, u32[]{:S(2)}) copy-start(f32[128]{0:T(128)} %param.15) | copy-start | bytes 1540
  0.7 16.9 %copy-start.6 = (f32[3,128]{1,0:T(4,128)S(1)}, f32[3,128]{1,0:T(4,128)}, u32[]{:S(2)}) copy-start(f32[3,128]{1,0:T(4,128)} %param.11) | copy-start | bytes 4612
  2.3 10.4 %collective-permute-start = (f32[392,128]{1,0:T(8,128)S(1)}, f32[392,128]{1,0:T(8,128)S(1)}, u32[]{:S(2)}, u32[]{:S(2)}) collective-permute-start(f32[392,128]{1,0:T(8,128)S(1)} %get-tuple-element.21), channel_id=1, source_target_pairs={{0,8},{8,0},{16,24},{24,16},{1,9},{9,1},{17,25},{25,17},{2,10},{10... | collective-permute-start | bytes 602120 | tf_op jit(solution)/shard_map/ppermute | solution.py:664
  2.8 9.9 %collective-permute-start.1 = (f32[392,128]{1,0:T(8,128)S(1)}, f32[392,128]{1,0:T(8,128)S(1)}, u32[]{:S(2)}, u32[]{:S(2)}) collective-permute-start(f32[392,128]{1,0:T(8,128)S(1)} %get-tuple-element.22), channel_id=1, source_target_pairs={{0,24},{8,16},{16,8},{24,0},{1,25},{9,17},{17,9},{25,1},{2,26},{10... | collective-permute-start | bytes 602120 | tf_op jit(solution)/shard_map/ppermute | solution.py:664
  6.8 13.2 %all-to-all-start = ((f32[8,8,128]{2,1,0:T(8,128)}), f32[8,8,128]{2,1,0:T(8,128)S(1)}, u32[]{:S(2)}, u32[]{:S(2)}) async-start(f32[8,8,128]{2,1,0:T(8,128)} %bitcast.4), calls=%async_computation | async-start | bytes 65536 | tf_op jit(solution)/shard_map/all_to_all | solution.py:697
  12.7 8.0 %collective-permute-start.2 = (f32[200,128]{1,0:T(8,128)S(1)}, f32[200,128]{1,0:T(8,128)S(1)}, u32[]{:S(2)}, u32[]{:S(2)}) collective-permute-start(f32[200,128]{1,0:T(8,128)S(1)} %get-tuple-element.25.own_hi), channel_id=1, source_target_pairs={{0,1},{1,2},{2,3},{3,4},{4,5},{5,6},{6,7},{7,0},{8,9},{9,10},{10,1... | collective-permute-start | bytes 307208 | tf_op jit(solution)/shard_map/ppermute | solution.py:657
  14.8 6.8 %collective-permute-start.3 = (f32[200,128]{1,0:T(8,128)S(1)}, f32[200,128]{1,0:T(8,128)S(1)}, u32[]{:S(2)}, u32[]{:S(2)}) collective-permute-start(f32[200,128]{1,0:T(8,128)S(1)} %get-tuple-element.26.own_lo), channel_id=1, source_target_pairs={{0,7},{1,0},{2,1},{3,2},{4,3},{5,4},{6,5},{7,6},{8,15},{9,8},{10,9... | collective-permute-start | bytes 307208 | tf_op jit(solution)/shard_map/ppermute | solution.py:657
  39.8 11.7 %all-to-all-start.1 = ((f32[8,24,128]{2,1,0:T(8,128)}), f32[8,24,128]{2,1,0:T(8,128)S(1)}, u32[]{:S(2)}, u32[]{:S(2)}) async-start(f32[8,24,128]{2,1,0:T(8,128)} %get-tuple-element.29), calls=%async_computation.1 | async-start | bytes 196608 | tf_op jit(solution)/shard_map/all_to_all | solution.py:708
  44.5 8.6 %copy-start = (f32[1,32,128,128]{3,2,1,0:T(8,128)S(1)}, f32[1,32,128,128]{3,2,1,0:T(8,128)}, u32[]{:S(2)}) copy-start(f32[1,32,128,128]{3,2,1,0:T(8,128)} %param.17) | copy-start | bytes 6291460
  51.6 1.6 %copy-start.1 = (f32[1,32,128,128]{3,2,1,0:T(8,128)S(1)}, f32[1,32,128,128]{3,2,1,0:T(8,128)}, u32[]{:S(2)}) copy-start(f32[1,32,128,128]{3,2,1,0:T(8,128)} %param.16) | copy-start | bytes 6291460
  52.3 2.7 %collective-permute-start.4 = (f32[8,128]{1,0:T(8,128)S(1)}, f32[8,128]{1,0:T(8,128)S(1)}, u32[]{:S(2)}, u32[]{:S(2)}) collective-permute-start(f32[8,128]{1,0:T(8,128)S(1)} %get-tuple-element.34), channel_id=1, source_target_pairs={{0,8},{8,0},{16,24},{24,16},{1,9},{9,1},{17,25},{25,17},{2,10},{10... | collective-permute-start | bytes 12296 | tf_op jit(solution)/shard_map/ppermute | solution.py:664
  52.4 3.1 %collective-permute-start.5 = (f32[8,128]{1,0:T(8,128)S(1)}, f32[8,128]{1,0:T(8,128)S(1)}, u32[]{:S(2)}, u32[]{:S(2)}) collective-permute-start(f32[8,128]{1,0:T(8,128)S(1)} %get-tuple-element.35), channel_id=1, source_target_pairs={{0,24},{8,16},{16,8},{24,0},{1,25},{9,17},{17,9},{25,1},{2,26},{10... | collective-permute-start | bytes 12296 | tf_op jit(solution)/shard_map/ppermute | solution.py:664

commit v5 on v4

--- a/solution.py
+++ b/solution.py
@@ -12,7 +12,7 @@
 STRIP = 16
 UNIT = 4
 TOP = 8
-AHEAD = 4
+AHEAD = 6
 LANES = 128
 SMALL = 16 * 2**20
 LARGE = 52 * 2**20
@@ -75,18 +75,173 @@
     return c + 0.8 * (numer * rcp(denom))
 
 
+def sweep(a, x, planes, strips, fx, mx, fy, my, src, store):
+    for u in range(planes):
+        for k in strips:
+            if k - 1 not in strips:
+                row = TOP + k * STRIP - 8
+                f, mu = flux(a[x + u, pl.ds(row + 1, 8), :] - a[x + u, pl.ds(row, 8), :])
+                fy[u, pl.ds(row, 8), :] = f
+                my[u, pl.ds(row, 8), :] = mu
+    for k in strips:
+        here = pl.ds(TOP + k * STRIP, STRIP)
+        before = pl.ds(TOP + k * STRIP - 1, STRIP)
+        after = pl.ds(TOP + k * STRIP + 1, STRIP)
+        flat = pl.ds(k * STRIP, STRIP)
+        c = a[x, here, :]
+        fp = fx[flat, :]
+        mp = mx[flat, :]
+        for u in range(planes):
+            up = a[x + u + 1, here, :]
+            f, mu = flux(up - c)
+            numer = f - fp
+            denom = mu + mp
+            fp, mp = f, mu
+            f, mu = flux(a[x + u, after, :] - c)
+            fy[u, here, :] = f
+            my[u, here, :] = mu
+            numer = numer + (f - fy[u, before, :])
+            denom = denom + (mu + my[u, before, :])
+            f, mu = z_flux(c)
+            numer = numer + (f + src[u, flat, :])
+            denom = denom + (mu + 1.0)
+            store(u, k, finish(c, numer, denom))
+            c = up
+        fx[flat, :] = fp
+        mx[flat, :] = mp
+
+
+def first_x(a, x, strips, fx, mx):
+    for k in strips:
+        here = pl.ds(TOP + k * STRIP, STRIP)
+        flat = pl.ds(k * STRIP, STRIP)
+        f, mu = flux(a[x + 1, here, :] - a[x, here, :])
+        fx[flat, :] = f
+        mx[flat, :] = mu
+
+
+def keep(flag, v):
+    return jnp.where(flag, v, 0.0)
+
+
+def head_planes(from_a, from_b, ny, flags, side):
+    swap = flags[4] > 0 if side == 0 else flags[4] == 0
+    planes = [jnp.where(swap, from_a[pl.ds(n * ny, ny), :], from_b[pl.ds(n * ny, ny), :]) for n in range(3)]
+    return [keep(flags[side] > 0, planes[0]), keep(flags[side] > 0, planes[1]), planes[2]]
+
+
+def inner_call(nx, ny, nz):
+    n_strip = ny // STRIP
+    strips = range(1, n_strip - 1)
+    inner = ny - 2 * STRIP
+    n_unit = nx // UNIT
+
+    def kernel(p_hbm, s_hbm, from_a, from_b, q_hbm, token, pe, q, sb, fx, mx, fy, my, psem, ssem, qsem):
+        flags = place()
+
+        def pcopy(c):
+            return pltpu.make_async_copy(
+                p_hbm.at[pl.ds(c * UNIT, UNIT), pl.ds(8, ny - 16)],
+                pe.at[pl.ds(2 + c * UNIT, UNIT), pl.ds(TOP + 8, ny - 16)], psem.at[c])
+
+        def scopy(c):
+            return pltpu.make_async_copy(
+                s_hbm.at[pl.ds(c * UNIT, UNIT), pl.ds(STRIP, inner)],
+                sb.at[pl.ds(1 + c * UNIT, UNIT), pl.ds(STRIP, inner)], ssem.at[c])
+
+        def qcopy(c):
+            return pltpu.make_async_copy(q.at[pl.ds(2 + c * UNIT, UNIT)], q_hbm.at[pl.ds(2 + c * UNIT, UNIT)], qsem.at[c])
+
+        first = pltpu.make_async_copy(q.at[pl.ds(0, 2)], q_hbm.at[pl.ds(0, 2)], qsem.at[n_unit])
+
+        def fetch(c):
+            pcopy(c).start()
+            scopy(c).start()
+
+        for c in range(n_unit):
+            fetch(c)
+        token[...] = jnp.zeros_like(token)
+        for side, (at, to) in enumerate((((0, 1), 0), ((nx + 2, nx + 3), nx + 1))):
+            planes = head_planes(from_a, from_b, ny, flags, side)
+            pe[at[0], pl.ds(TOP, ny), :] = planes[0]
+            pe[at[1], pl.ds(TOP, ny), :] = planes[1]
+            sb[to, :, :] = planes[2]
+
+        def part(x, planes, at=None, flag=None):
+            def store(u, k, v):
+                q[x + u + 1, pl.ds((k - 1) * STRIP, STRIP), :] = keep(flag, v) if u == at else v
+
+            sweep(pe, x + 2, planes, strips, fx, mx, fy, my, sb.at[pl.ds(x + 1, planes)], store)
+
+        for c in range(2):
+            pcopy(c).wait()
+            scopy(c).wait()
+        first_x(pe, 0, strips, fx, mx)
+        part(-1, UNIT + 2, 0, flags[0] > 0)
+        first.start()
+        qcopy(0).start()
+
+        def body(b, _):
+            pcopy(b + 1).wait()
+            scopy(b + 1).wait()
+            part(b * UNIT + 1, UNIT)
+            qcopy(b).start()
+            return 0
+
+        lax.fori_loop(1, n_unit - 1, body, 0)
+        part((n_unit - 1) * UNIT + 1, UNIT, UNIT - 1, flags[1] > 0)
+        qcopy(n_unit - 1).start()
+        first.wait()
+        for c in range(n_unit):
+            qcopy(c).wait()
+
+    plane = pltpu.VMEM((ny, nz), F32)
+    edge = pltpu.VMEM((UNIT + 2, ny + 2 * TOP, nz), F32)
+    return pl.pallas_call(
+        kernel,
+        out_shape=(jax.ShapeDtypeStruct((nx + 2, inner, nz), F32), jax.ShapeDtypeStruct((8, LANES), F32)),
+        in_specs=[HBM, HBM, VM, VM],
+        out_specs=(HBM, VM),
+        scratch_shapes=[
+            pltpu.VMEM((nx + 4, ny + 2 * TOP, nz), F32), pltpu.VMEM((nx + 2, inner, nz), F32),
+            pltpu.VMEM((nx + 2, ny, nz), F32), plane, plane, edge, edge,
+            pltpu.SemaphoreType.DMA((n_unit,)), pltpu.SemaphoreType.DMA((n_unit,)),
+            pltpu.SemaphoreType.DMA((n_unit + 1,)),
+        ],
+        compiler_params=pltpu.CompilerParams(vmem_limit_bytes=LARGE),
+        cost_estimate=cost(1, 1),
+        name="sweep_inner",
+    )
+
+
 def relax_call(nx, ny, nz, n_track, cap):
     chunk = UNIT
     per = cap // LANES
     rows = ny + 2 * TOP
 
-    def kernel(p_hbm, s_hbm, from_a, from_b, tlo, thi, own_lo, own_hi, kern, requests, ex_hbm, o_hbm, reply_out,
-               reply, rsem, table, parts, pe, q, sb, ob, fx1, mx1, fx2, mx2, fy1, my1, fy2, my2, psem, ssem, osem):
+    def kernel(p_hbm, s_hbm, from_a, from_b, tlo, thi, own_lo, own_hi, kern, requests, q_hbm, o_hbm, reply_out,
+               reply, rsem, table, parts, pe, q, sb, ob, fx1, mx1, fx2, mx2, fy1, my1, fy2, my2, psem, ssem, osem, qsem):
         n_chunk = nx // chunk
 
-        def pcopy(c):
-            return pltpu.make_async_copy(p_hbm.at[pl.ds(c * chunk, chunk)],
-                                         pe.at[pl.ds(2 + c * chunk, chunk), pl.ds(TOP, ny)], psem.at[c])
+        reach = STRIP + 8
+        inner = ny - 2 * STRIP
+        ends = (0, ny // STRIP - 1)
+        whole = range(ny // STRIP)
+
+        def pcopies(c):
+            return [
+                pltpu.make_async_copy(
+                    p_hbm.at[pl.ds(c * chunk, chunk), pl.ds(row, reach)],
+                    pe.at[pl.ds(2 + c * chunk, chunk), pl.ds(TOP + row, reach)], psem.at[n, c])
+                for n, row in enumerate((0, ny - reach))
+            ]
+
+        def qcopy(c):
+            return pltpu.make_async_copy(q_hbm.at[pl.ds(2 + c * chunk, chunk)],
+                                         q.at[pl.ds(2 + c * chunk, chunk), pl.ds(TOP + STRIP, inner)], qsem.at[c])
+
+        qfirst = pltpu.make_async_copy(q_hbm.at[pl.ds(0, 2)], q.at[pl.ds(0, 2), pl.ds(TOP + STRIP, inner)],
+                                       qsem.at[nx // chunk])
 
         def scopy(c):
             return pltpu.make_async_copy(s_hbm.at[pl.ds(c * chunk, chunk)],
@@ -97,17 +252,23 @@
                                          o_hbm.at[pl.ds(c * chunk, chunk)], osem.at[c])
 
         def fetch(c):
-            pcopy(c).start()
+            for copy in pcopies(c):
+                copy.start()
             scopy(c).start()
-
+            qcopy(c).start()
+
+        def arrive(c):
+            for copy in pcopies(c):
+                copy.wait()
+            scopy(c).wait()
+            qcopy(c).wait()
+
+        qfirst.start()
         for c in range(AHEAD):
             fetch(c)
 
         flags = place()
         has = [flags[n] > 0 for n in range(4)]
-
-        def keep(flag, v):
-            return jnp.where(flag, v, 0.0)
 
         main = pl.ds(TOP, ny)
         odd = flags[4] > 0
@@ -145,51 +306,11 @@
             pe2[pl.ds((nx + 2) * rows + row, 1), :] = above
             q2[pl.ds(rows + row, nx, stride=rows), :] = keep(flag, finish(c, numer, denom))
 
-        def sweep(a, x, planes, fx, mx, fy, my, src, store):
-            for u in range(planes):
-                f, mu = flux(a[x + u, pl.ds(1, TOP), :] - a[x + u, pl.ds(0, TOP), :])
-                fy[u, pl.ds(0, TOP), :] = f
-                my[u, pl.ds(0, TOP), :] = mu
-            for k in range(ny // STRIP):
-                here = pl.ds(TOP + k * STRIP, STRIP)
-                before = pl.ds(TOP + k * STRIP - 1, STRIP)
-                after = pl.ds(TOP + k * STRIP + 1, STRIP)
-                flat = pl.ds(k * STRIP, STRIP)
-                c = a[x, here, :]
-                fp = fx[flat, :]
-                mp = mx[flat, :]
-                for u in range(planes):
-                    up = a[x + u + 1, here, :]
-                    f, mu = flux(up - c)
-                    numer = f - fp
-                    denom = mu + mp
-                    fp, mp = f, mu
-                    f, mu = flux(a[x + u, after, :] - c)
-                    fy[u, here, :] = f
-                    my[u, here, :] = mu
-                    numer = numer + (f - fy[u, before, :])
-                    denom = denom + (mu + my[u, before, :])
-                    f, mu = z_flux(c)
-                    numer = numer + (f + src[u, flat, :])
-                    denom = denom + (mu + 1.0)
-                    store(u, k, finish(c, numer, denom))
-                    c = up
-                fx[flat, :] = fp
-                mx[flat, :] = mp
-
-        def first_x(a, x, fx, mx):
-            for k in range(ny // STRIP):
-                here = pl.ds(TOP + k * STRIP, STRIP)
-                flat = pl.ds(k * STRIP, STRIP)
-                f, mu = flux(a[x + 1, here, :] - a[x, here, :])
-                fx[flat, :] = f
-                mx[flat, :] = mu
-
         def sweep1(x, planes, flag=None):
             def store(u, k, v):
                 q[x + u + 1, pl.ds(TOP + k * STRIP, STRIP), :] = v if flag is None else keep(flag, v)
 
-            sweep(pe, x + 2, planes, fx1, mx1, fy1, my1, sb.at[pl.ds(x + 1, planes)], store)
+            sweep(pe, x + 2, planes, ends, fx1, mx1, fy1, my1, sb.at[pl.ds(x + 1, planes)], store)
 
         kk = both(kern[...])
 
@@ -197,7 +318,7 @@
             def store(u, k, v):
                 ob[x + u + UNIT, pl.ds(k * STRIP, STRIP), :] = v
 
-            sweep(q, x + 1, planes, fx2, mx2, fy2, my2, sb.at[pl.ds(x + 1, planes)], store)
+            sweep(q, x + 1, planes, whole, fx2, mx2, fy2, my2, sb.at[pl.ds(x + 1, planes)], store)
 
         def surface(x, planes):
             nt = (((1,), (1,)), ((), ()))
@@ -210,14 +331,13 @@
                 table[x + u + UNIT] = (a[8:16] + b[0:8]) + a[0:8]
 
         n_unit = nx // UNIT
-        pcopy(0).wait()
-        scopy(0).wait()
-        first_x(pe, 0, fx1, mx1)
+        qfirst.wait()
+        arrive(0)
+        first_x(pe, 0, ends, fx1, mx1)
         sweep1(-1, 1, has[0])
         sweep1(0, 1)
-        first_x(q, 0, fx2, mx2)
-        pcopy(1).wait()
-        scopy(1).wait()
+        first_x(q, 0, whole, fx2, mx2)
+        arrive(1)
         sweep1(1, UNIT)
 
         def body(b, _):
@@ -227,8 +347,7 @@
 
             @pl.when(b < n_unit - 1)
             def _():
-                pcopy(b + 1).wait()
-                scopy(b + 1).wait()
+                arrive(b + 1)
 
             surface((b - 2) * UNIT, UNIT)
             sweep2((b - 1) * UNIT, UNIT)
@@ -283,7 +402,7 @@
             jax.ShapeDtypeStruct((nx, ny, nz), f32),
             jax.ShapeDtypeStruct((n_track, 3 * per, 128), f32),
         ),
-        in_specs=[hbm, hbm] + [vm] * 8 + [pl.BlockSpec(memory_space=pl.ANY)],
+        in_specs=[hbm, hbm] + [vm] * 8 + [hbm],
         out_specs=(hbm, hbm),
         scratch_shapes=[
             pltpu.VMEM((n_track, 3 * per, 128), f32), pltpu.SemaphoreType.DMA((4,)),
@@ -291,8 +410,8 @@
             pltpu.VMEM((nx + 4, rows, nz), f32), pltpu.VMEM((nx + 2, rows, nz), f32),
             pltpu.VMEM((nx + 2, ny, nz), f32), pltpu.VMEM((nx + UNIT, ny, nz), f32),
             plane, plane, plane, plane, edge, edge, edge, edge,
-            pltpu.SemaphoreType.DMA((nx // chunk,)), pltpu.SemaphoreType.DMA((nx // chunk,)),
-            pltpu.SemaphoreType.DMA((nx // chunk,)),
+            pltpu.SemaphoreType.DMA((2, nx // chunk)), pltpu.SemaphoreType.DMA((nx // chunk,)),
+            pltpu.SemaphoreType.DMA((nx // chunk,)), pltpu.SemaphoreType.DMA((nx // chunk + 1,)),
         ],
         compiler_params=pltpu.CompilerParams(vmem_limit_bytes=LARGE),
         cost_estimate=pl.CostEstimate(flops=nx * ny * nz * 100, bytes_accessed=nx * ny * nz * 12, transcendentals=nx * ny * nz * 10),
@@ -494,11 +613,12 @@
     high = both(tiles_ref[k + 2])
     own_hi, own_lo = split(own)
     nxt_hi, nxt_lo = split(nxt)
-    field = fold(
-        mm_nt(here, jnp.concatenate([own_hi, nxt_hi], axis=1)),
-        mm_nt(here, jnp.concatenate([own_lo, nxt_lo], axis=1)),
-    )
-    return field + fold(mm(high, nxt_hi), mm(high, nxt_lo))
+    pairs = [jnp.concatenate(v, axis=1) for v in ((own_hi, nxt_hi), (own_lo, nxt_lo))]
+    before = mm_nt(here, jnp.concatenate(pairs, axis=0))
+    field = fold(before[:, :LANES], before[:, LANES:])
+    only_hi = jnp.where(lax.broadcasted_iota(jnp.int32, high.shape, 0) < 8, high.astype(F32), 0.0).astype(BF16)
+    after = mm(jnp.concatenate([high, only_hi], axis=1), jnp.concatenate([nxt_hi, nxt_lo], axis=0))
+    return field + (after[0:8] + after[8:16])
 
 
 def first_call(n_tiles, ny, start, count):
@@ -699,13 +819,14 @@
     kern = jnp.pad(depth_kernel, ((0, 5), (0, 0)))
     half = n_tiles // 2
     couplings = (self_tiles[0], next_tiles[0], state, from_a, from_b)
-    ex_a = first_call(n_tiles, ny, 0, half)(*couplings)
-    asked = cells_call(n_track * cap // LANES)(asked.reshape(n_track * cap // LANES, LANES), ex_a)
+    q_inner, token = inner_call(nx, ny, nz)(potential, source, from_a, from_b)
+    asked = cells_call(n_track * cap // LANES)(asked.reshape(n_track * cap // LANES, LANES), token)
     relaxed, reply = relax_call(nx, ny, nz, n_track, cap)(
         potential, source, from_a, from_b, left, right, track_lo, track_hi, kern,
-        asked, ex_a,
+        asked, q_inner,
     )
     answers = lax.all_to_all(reply, "track", 0, 0)
+    ex_a = first_call(n_tiles, ny, 0, half)(*couplings)
     ex_b = first_call(n_tiles, ny, half, n_tiles - half)(*couplings)
     applied, state, edge_a, edge_b = section_call(n_tiles, n_track, cap)(
         answers, slots, state, ex_a, ex_b, target

time: 56.7 us -> 55.1 us (0.972)
  waiting for transfers between devices: 6.56 us -> 3.07 us
  Pallas kernels: 29.7 us -> 32.8 us
  starting transfers between devices: 19.1 us -> 17.9 us
    pallas_call x0 -> x1, Pallas kernels: none -> 7.75 us  [per_device(): q_inner, token = inner_call(nx, ny, nz)(potential, source, from_a, from_b)]
    pallas_call x1, Pallas kernels: 18.2 us -> 14.2 us  [per_device(): relax_call(nx, ny, nz, n_track, cap)]
    all_to_all x1, waiting for transfers between devices: 4.52 us -> 2.28 us  [per_device(): answers = lax.all_to_all(reply, 'track', 0, 0)]
    ppermute x2, waiting for transfers between devices: 1.56 us -> 0.01 us  [shifted(): return lax.ppermute(v, axis, [(i, (i + by) % n) for i in range(n)])]
    all_to_all x1, starting transfers between devices: 4.6 us -> 3.37 us  [per_device(): answers = lax.all_to_all(reply, 'track', 0, 0)]
  transfers between devices with their start and end apart: 8 -> 8, of which waited for: 4 -> 2; matrix products, arithmetic and copies ran while one was open for 0% -> 0% of each run, Pallas kernels for 15% -> 28%
where the time goes in v5:
time: 55.1 us; the launch traced here: 54.8 us
  Pallas kernels  32.8 us (60%)
  starting transfers between devices  17.9 us (32%)
  waiting for transfers between devices  3.07 us (6%)
  between operations  0.83 us (2%)
    pallas_call x1, Pallas kernels, per_device(): relax_call(nx, ny, nz, n_track, cap)  14.2 us
    pallas_call x1, Pallas kernels, per_device(): q_inner, token = inner_call(nx, ny, nz)(potential, source, from_a, from_b)  7.75 us
    all_to_all x1, starting transfers between devices, per_device(): lax.all_to_all(requests.reshape(n_track, cap // LANES, LANES), 'track', 0...  5.83 us
    ppermute x2, starting transfers between devices, shifted(): return lax.ppermute(v, axis, [(i, (i + by) % n) for i in range(n)])  4.83 us
    ppermute x4, starting transfers between devices, traded(): return (lax.ppermute(to_a, axis, first), lax.ppermute(to_b, axis, second))  3.86 us
    all_to_all x1, starting transfers between devices, per_device(): answers = lax.all_to_all(reply, 'track', 0, 0)  3.37 us
    pallas_call x1, Pallas kernels, per_device(): ex_b = first_call(n_tiles, ny, half, n_tiles - half)(*couplings)  2.45 us
    pallas_call x1, Pallas kernels, per_device(): ex_a = first_call(n_tiles, ny, 0, half)(*couplings)  2.3 us
  transfers between devices with their start and end apart: 8, of which 2 were waited for; matrix products, arithmetic and copies ran while one was open for 0% of the time, Pallas kernels for 28%

profile of v5, /device:TPU:0, one launch (start us, length us, event | category | flops | bytes accessed | tf_op | source)
XLA Modules:
  0.0 54.8 jit_solution(14467531133085582303)
XLA Ops:
  0.7 1.6 %pack.1 = (f32[392,128]{1,0:T(8,128)S(1)}, f32[392,128]{1,0:T(8,128)S(1)}, f32[200,128]{1,0:T(8,128)S(1)}, f32[200,128]{1,0:T(8,128)S(1)}) custom-call(f32[64,128,128]{2,1,0:T(8,128)} %p_hbm.5, f32[64,128,128]{2,1,0:T(8,128)} %s_hbm.5), custom_call_target="tpu_custom_call" | custom-call | flops 1000000 | bytes 4194304 | tf_op jit(solution)/shard_map/pack/pallas_call | solution.py:808
  2.3 0.5 collective-permute-start
  2.8 2.6 %collective-permute-start.1 = (f32[392,128]{1,0:T(8,128)S(1)}, f32[392,128]{1,0:T(8,128)S(1)}, u32[]{:S(2)}, u32[]{:S(2)}) collective-permute-start(f32[392,128]{1,0:T(8,128)S(1)} %get-tuple-element.24), channel_id=1, source_target_pairs={{0,24},{8,16},{16,8},{24,0},{1,25},{9,17},{17,9},{25,1},{2,26},{10... | collective-permute-start | bytes 602120 | tf_op jit(solution)/shard_map/ppermute | solution.py:784
  5.4 1.4 %requests.1 = (f32[64,128]{1,0:T(8,128)}, s32[32,128]{1,0:T(8,128)S(1)}, f32[32,128]{1,0:T(8,128)S(1)}) custom-call(s32[32,128]{1,0:T(8,128)S(1)} %bitcast.21, s32[32,128]{1,0:T(8,128)S(1)} %bitcast.22, f32[1,128]{1,0:T(1,128)S(1)} %bitcast.23), custom_call_target="tpu_custom_call" | custom-call | flops 100000000 | bytes 1048576 | tf_op jit(solution)/shard_map/requests/pallas_call | solution.py:811
  6.8 5.8 %all-to-all-start = ((f32[8,8,128]{2,1,0:T(8,128)}), f32[8,8,128]{2,1,0:T(8,128)S(1)}, u32[]{:S(2)}, u32[]{:S(2)}) async-start(f32[8,8,128]{2,1,0:T(8,128)} %bitcast.4), calls=%async_computation | async-start | bytes 65536 | tf_op jit(solution)/shard_map/all_to_all | solution.py:817
  12.7 0.0 collective-permute-done.from_a
  12.7 2.1 %collective-permute-start.2 = (f32[200,128]{1,0:T(8,128)S(1)}, f32[200,128]{1,0:T(8,128)S(1)}, u32[]{:S(2)}, u32[]{:S(2)}) collective-permute-start(f32[200,128]{1,0:T(8,128)S(1)} %get-tuple-element.27.own_hi), channel_id=1, source_target_pairs={{0,1},{1,2},{2,3},{3,4},{4,5},{5,6},{6,7},{7,0},{8,9},{9,10},{10,1... | collective-permute-start | bytes 307208 | tf_op jit(solution)/shard_map/ppermute | solution.py:777
  14.8 2.8 %collective-permute-start.3 = (f32[200,128]{1,0:T(8,128)S(1)}, f32[200,128]{1,0:T(8,128)S(1)}, u32[]{:S(2)}, u32[]{:S(2)}) collective-permute-start(f32[200,128]{1,0:T(8,128)S(1)} %get-tuple-element.28.own_lo), channel_id=1, source_target_pairs={{0,7},{1,0},{2,1},{3,2},{4,3},{5,4},{6,5},{7,6},{8,15},{9,8},{10,9... | collective-permute-start | bytes 307208 | tf_op jit(solution)/shard_map/ppermute | solution.py:777
  17.6 7.8 %sweep_inner.1 = (f32[66,96,128]{2,1,0:T(8,128)}, f32[8,128]{1,0:T(8,128)S(1)}) custom-call(f32[64,128,128]{2,1,0:T(8,128)} %p_hbm.5, f32[64,128,128]{2,1,0:T(8,128)} %s_hbm.5, f32[392,128]{1,0:T(8,128)S(1)} %collective-permute-done.from_a, f32[392,128]{1,0:T(8,128)S(1)} %collective-permute-done.1.from_b), custom_call_target="tpu_custom_call" | custom-call | flops 1 | bytes 1 | tf_op jit(solution)/shard_map/sweep_inner/pallas_call | solution.py:822
  25.3 0.0 all-to-all-done
  25.4 14.2 %relax.1 = (f32[64,128,128]{2,1,0:T(8,128)}, f32[8,24,128]{2,1,0:T(8,128)}) custom-call(f32[64,128,128]{2,1,0:T(8,128)} %p_hbm.5, f32[64,128,128]{2,1,0:T(8,128)} %s_hbm.5, f32[392,128]{1,0:T(8,128)S(1)} %collective-permute-done.from_a, f32[392,128]{1,0:T(8,128)S(1)} %collective-permute-done.1.from_b, f32[200,128]{1,0:T(8,128)S(1)} %collective-permute-done.2.tlo, ...), custom_call_target="tpu_custom_call" | custom-call | flops 104857600 | bytes 12582912 | tf_op jit(solution)/shard_map/relax/pallas_call | solution.py:824
  39.6 3.4 %all-to-all-start.1 = ((f32[8,24,128]{2,1,0:T(8,128)}), f32[8,24,128]{2,1,0:T(8,128)S(1)}, u32[]{:S(2)}, u32[]{:S(2)}) async-start(f32[8,24,128]{2,1,0:T(8,128)} %get-tuple-element.33), calls=%async_computation.1 | async-start | bytes 196608 | tf_op jit(solution)/shard_map/all_to_all | solution.py:828
  43.0 2.3 %couple_first.2.ex_a = f32[48,128]{1,0:T(8,128)S(1)} custom-call(f32[32,128,128]{2,1,0:T(8,128)} %bitcast.13, f32[32,128,128]{2,1,0:T(8,128)} %bitcast.9, f32[96,128]{1,0:T(8,128)S(1)} %bitcast.17, f32[392,128]{1,0:T(8,128)S(1)} %collective-permute-done.from_a, f32[392,128]{1,0:T(8,128)S(1)} %collective-permute-done.1.from_b), custom_call_target="tpu_custom_call" | custom-call | flops 1 | bytes 1 | tf_op jit(solution)/shard_map/couple_first/pallas_call | solution.py:829
  45.3 0.0 copy-start
  45.3 2.5 %couple_first.3.ex_b = f32[48,128]{1,0:T(8,128)S(1)} custom-call(f32[32,128,128]{2,1,0:T(8,128)} %bitcast.14, f32[32,128,128]{2,1,0:T(8,128)} %bitcast.10, f32[96,128]{1,0:T(8,128)S(1)} %bitcast.18, f32[392,128]{1,0:T(8,128)S(1)} %collective-permute-done.from_a, f32[392,128]{1,0:T(8,128)S(1)} %collective-permute-done.1.from_b), custom_call_target="tpu_custom_call" | custom-call | flops 1 | bytes 1 | tf_op jit(solution)/shard_map/couple_first/pallas_call | solution.py:830
  47.8 2.3 %all-to-all-done.1.answers = f32[8,24,128]{2,1,0:T(8,128)S(1)} async-done(((f32[8,24,128]{2,1,0:T(8,128)}), f32[8,24,128]{2,1,0:T(8,128)S(1)}, u32[]{:S(2)}, u32[]{:S(2)}) %all-to-all-start.1) | async-done | bytes 98336 | tf_op jit(solution)/shard_map/all_to_all | solution.py:828
  50.0 0.7 %section_first.1 = (f32[96,128]{1,0:T(8,128)S(1)}, f32[96,128]{1,0:T(8,128)S(1)}, f32[8,128]{1,0:T(8,128)S(1)}, f32[8,128]{1,0:T(8,128)S(1)}) custom-call(f32[8,24,128]{2,1,0:T(8,128)S(1)} %all-to-all-done.1.answers, s32[32,128]{1,0:T(8,128)S(1)} %get-tuple-element.34.slots, f32[96,128]{1,0:T(8,128)S(1)} %bitcast.19, f32[48,128]{1,0:T(8,128)S(1)} %couple_first.2.ex_a, ...), custom_call_target="tpu_custom_call" | custom-call | flops 1000000000 | bytes 1048576 | tf_op jit(solution)/shard_map/section_first/pallas_call | solution.py:831
  50.8 0.1 collective-permute-start.4
  50.8 0.7 %collective-permute-start.5 = (f32[8,128]{1,0:T(8,128)S(1)}, f32[8,128]{1,0:T(8,128)S(1)}, u32[]{:S(2)}, u32[]{:S(2)}) collective-permute-start(f32[8,128]{1,0:T(8,128)S(1)} %get-tuple-element.39), channel_id=1, source_target_pairs={{0,24},{8,16},{16,8},{24,0},{1,25},{9,17},{17,9},{25,1},{2,26},{10... | collective-permute-start | bytes 12296 | tf_op jit(solution)/shard_map/ppermute | solution.py:784
  51.5 0.1 copy-done.1
  51.6 1.5 %couple_second.1.ex = f32[96,128]{1,0:T(8,128)S(1)} custom-call(f32[32,128,128]{2,1,0:T(8,128)S(1)} %bitcast.15, f32[32,128,128]{2,1,0:T(8,128)S(1)} %bitcast.11, f32[96,128]{1,0:T(8,128)S(1)} %get-tuple-element.36.m_ref), custom_call_target="tpu_custom_call" | custom-call | flops 1000000000 | bytes 4194304 | tf_op jit(solution)/shard_map/couple_second/pallas_call | solution.py:835
  53.2 0.0 collective-permute-done.4.from_a
  53.2 0.8 %collective-permute-done.5.from_b = f32[8,128]{1,0:T(8,128)S(1)} collective-permute-done((f32[8,128]{1,0:T(8,128)S(1)}, f32[8,128]{1,0:T(8,128)S(1)}, u32[]{:S(2)}, u32[]{:S(2)}) %collective-permute-start.5) | collective-permute-done | bytes 4128 | tf_op jit(solution)/shard_map/ppermute | solution.py:784
  53.9 0.8 %section_last.1 = f32[96,128]{1,0:T(8,128)} custom-call(f32[96,128]{1,0:T(8,128)S(1)} %get-tuple-element.36.m_ref, f32[96,128]{1,0:T(8,128)S(1)} %couple_second.1.ex, f32[96,128]{1,0:T(8,128)S(1)} %get-tuple-element.37.applied, f32[32,128]{1,0:T(8,128)S(1)} %get-tuple-element.35.target, f32[8,128]{1,0:T(8,128)S(1)} %collective-permute-done.4.from_a, ...), custom_call_target="tpu_custom_call" | custom-call | flops 10000000 | bytes 1048576 | tf_op jit(solution)/shard_map/section_last/pallas_call | solution.py:836
  (19 shorter events, 0.1 us)
Async XLA Ops:
  0.6 1.6 %copy-start.2 = (f32[3,1,4096]{2,1,0:T(1,128)S(1)}, f32[3,1,4096]{2,1,0:T(1,128)}, u32[]{:S(2)}) copy-start(f32[3,1,4096]{2,1,0:T(1,128)} %param.12) | copy-start | bytes 147460
  0.6 4.8 %copy-start.3 = (s32[1,4096]{1,0:T(1,128)S(1)}, s32[1,4096]{1,0:T(1,128)}, u32[]{:S(2)}) copy-start(s32[1,4096]{1,0:T(1,128)} %param.13) | copy-start | bytes 49156
  0.7 4.8 %copy-start.4 = (s32[1,4096]{1,0:T(1,128)S(1)}, s32[1,4096]{1,0:T(1,128)}, u32[]{:S(2)}) copy-start(s32[1,4096]{1,0:T(1,128)} %param.14) | copy-start | bytes 49156
  0.7 4.8 %copy-start.5 = (f32[128]{0:T(128)S(1)}, f32[128]{0:T(128)}, u32[]{:S(2)}) copy-start(f32[128]{0:T(128)} %param.15) | copy-start | bytes 1540
  0.7 16.9 %copy-start.6 = (f32[3,128]{1,0:T(4,128)S(1)}, f32[3,128]{1,0:T(4,128)}, u32[]{:S(2)}) copy-start(f32[3,128]{1,0:T(4,128)} %param.11) | copy-start | bytes 4612
  2.3 10.4 %collective-permute-start = (f32[392,128]{1,0:T(8,128)S(1)}, f32[392,128]{1,0:T(8,128)S(1)}, u32[]{:S(2)}, u32[]{:S(2)}) collective-permute-start(f32[392,128]{1,0:T(8,128)S(1)} %get-tuple-element.23), channel_id=1, source_target_pairs={{0,8},{8,0},{16,24},{24,16},{1,9},{9,1},{17,25},{25,17},{2,10},{10... | collective-permute-start | bytes 602120 | tf_op jit(solution)/shard_map/ppermute | solution.py:784
  2.8 9.9 %collective-permute-start.1 = (f32[392,128]{1,0:T(8,128)S(1)}, f32[392,128]{1,0:T(8,128)S(1)}, u32[]{:S(2)}, u32[]{:S(2)}) collective-permute-start(f32[392,128]{1,0:T(8,128)S(1)} %get-tuple-element.24), channel_id=1, source_target_pairs={{0,24},{8,16},{16,8},{24,0},{1,25},{9,17},{17,9},{25,1},{2,26},{10... | collective-permute-start | bytes 602120 | tf_op jit(solution)/shard_map/ppermute | solution.py:784
  6.8 18.5 %all-to-all-start = ((f32[8,8,128]{2,1,0:T(8,128)}), f32[8,8,128]{2,1,0:T(8,128)S(1)}, u32[]{:S(2)}, u32[]{:S(2)}) async-start(f32[8,8,128]{2,1,0:T(8,128)} %bitcast.4), calls=%async_computation | async-start | bytes 65536 | tf_op jit(solution)/shard_map/all_to_all | solution.py:817
  12.7 12.6 %collective-permute-start.2 = (f32[200,128]{1,0:T(8,128)S(1)}, f32[200,128]{1,0:T(8,128)S(1)}, u32[]{:S(2)}, u32[]{:S(2)}) collective-permute-start(f32[200,128]{1,0:T(8,128)S(1)} %get-tuple-element.27.own_hi), channel_id=1, source_target_pairs={{0,1},{1,2},{2,3},{3,4},{4,5},{5,6},{6,7},{7,0},{8,9},{9,10},{10,1... | collective-permute-start | bytes 307208 | tf_op jit(solution)/shard_map/ppermute | solution.py:777
  14.8 10.6 %collective-permute-start.3 = (f32[200,128]{1,0:T(8,128)S(1)}, f32[200,128]{1,0:T(8,128)S(1)}, u32[]{:S(2)}, u32[]{:S(2)}) collective-permute-start(f32[200,128]{1,0:T(8,128)S(1)} %get-tuple-element.28.own_lo), channel_id=1, source_target_pairs={{0,7},{1,0},{2,1},{3,2},{4,3},{5,4},{6,5},{7,6},{8,15},{9,8},{10,9... | collective-permute-start | bytes 307208 | tf_op jit(solution)/shard_map/ppermute | solution.py:777
  39.6 10.4 %all-to-all-start.1 = ((f32[8,24,128]{2,1,0:T(8,128)}), f32[8,24,128]{2,1,0:T(8,128)S(1)}, u32[]{:S(2)}, u32[]{:S(2)}) async-start(f32[8,24,128]{2,1,0:T(8,128)} %get-tuple-element.33), calls=%async_computation.1 | async-start | bytes 196608 | tf_op jit(solution)/shard_map/all_to_all | solution.py:828
  45.3 6.2 %copy-start = (f32[1,32,128,128]{3,2,1,0:T(8,128)S(1)}, f32[1,32,128,128]{3,2,1,0:T(8,128)}, u32[]{:S(2)}) copy-start(f32[1,32,128,128]{3,2,1,0:T(8,128)} %param.17) | copy-start | bytes 6291460
  50.0 1.6 %copy-start.1 = (f32[1,32,128,128]{3,2,1,0:T(8,128)S(1)}, f32[1,32,128,128]{3,2,1,0:T(8,128)}, u32[]{:S(2)}) copy-start(f32[1,32,128,128]{3,2,1,0:T(8,128)} %param.16) | copy-start | bytes 6291460
  50.8 2.4 %collective-permute-start.4 = (f32[8,128]{1,0:T(8,128)S(1)}, f32[8,128]{1,0:T(8,128)S(1)}, u32[]{:S(2)}, u32[]{:S(2)}) collective-permute-start(f32[8,128]{1,0:T(8,128)S(1)} %get-tuple-element.38), channel_id=1, source_target_pairs={{0,8},{8,0},{16,24},{24,16},{1,9},{9,1},{17,25},{25,17},{2,10},{10... | collective-permute-start | bytes 12296 | tf_op jit(solution)/shard_map/ppermute | solution.py:784
  50.8 3.1 %collective-permute-start.5 = (f32[8,128]{1,0:T(8,128)S(1)}, f32[8,128]{1,0:T(8,128)S(1)}, u32[]{:S(2)}, u32[]{:S(2)}) collective-permute-start(f32[8,128]{1,0:T(8,128)S(1)} %get-tuple-element.39), channel_id=1, source_target_pairs={{0,24},{8,16},{16,8},{24,0},{1,25},{9,17},{17,9},{25,1},{2,26},{10... | collective-permute-start | bytes 12296 | tf_op jit(solution)/shard_map/ppermute | solution.py:784

commit v6 on v5

--- a/solution.py
+++ b/solution.py
@@ -10,9 +10,9 @@
 F32 = jnp.float32
 BF16 = jnp.bfloat16
 STRIP = 16
-UNIT = 4
+UNIT = 8
 TOP = 8
-AHEAD = 6
+AHEAD = 4
 LANES = 128
 SMALL = 16 * 2**20
 LARGE = 52 * 2**20

time: 55.1 us -> 54.6 us (level)
  no operation moved by 1% of the time
where the time goes in v6:
time: 54.6 us; the launch traced here: 54.3 us
  Pallas kernels  32.3 us (59%)
  starting transfers between devices  17.9 us (33%)
  waiting for transfers between devices  3.07 us (6%)
  between operations  0.83 us (2%)
    pallas_call x1, Pallas kernels, per_device(): relax_call(nx, ny, nz, n_track, cap)  13.9 us
    pallas_call x1, Pallas kernels, per_device(): q_inner, token = inner_call(nx, ny, nz)(potential, source, from_a, from_b)  7.58 us
    all_to_all x1, starting transfers between devices, per_device(): lax.all_to_all(requests.reshape(n_track, cap // LANES, LANES), 'track', 0...  5.83 us
    ppermute x2, starting transfers between devices, shifted(): return lax.ppermute(v, axis, [(i, (i + by) % n) for i in range(n)])  4.83 us
    ppermute x4, starting transfers between devices, traded(): return (lax.ppermute(to_a, axis, first), lax.ppermute(to_b, axis, second))  3.87 us
    all_to_all x1, starting transfers between devices, per_device(): answers = lax.all_to_all(reply, 'track', 0, 0)  3.37 us
    pallas_call x1, Pallas kernels, per_device(): ex_b = first_call(n_tiles, ny, half, n_tiles - half)(*couplings)  2.45 us
    pallas_call x1, Pallas kernels, per_device(): ex_a = first_call(n_tiles, ny, 0, half)(*couplings)  2.3 us
  transfers between devices with their start and end apart: 8, of which 2 were waited for; matrix products, arithmetic and copies ran while one was open for 0% of the time, Pallas kernels for 28%

profile of v6, /device:TPU:0, one launch (start us, length us, event | category | flops | bytes accessed | tf_op | source)
XLA Modules:
  0.0 54.3 jit_solution(10499266768334008681)
XLA Ops:
  0.7 1.6 %pack.1 = (f32[392,128]{1,0:T(8,128)S(1)}, f32[392,128]{1,0:T(8,128)S(1)}, f32[200,128]{1,0:T(8,128)S(1)}, f32[200,128]{1,0:T(8,128)S(1)}) custom-call(f32[64,128,128]{2,1,0:T(8,128)} %p_hbm.5, f32[64,128,128]{2,1,0:T(8,128)} %s_hbm.5), custom_call_target="tpu_custom_call" | custom-call | flops 1000000 | bytes 4194304 | tf_op jit(solution)/shard_map/pack/pallas_call | solution.py:808
  2.3 0.5 collective-permute-start
  2.8 2.6 %collective-permute-start.1 = (f32[392,128]{1,0:T(8,128)S(1)}, f32[392,128]{1,0:T(8,128)S(1)}, u32[]{:S(2)}, u32[]{:S(2)}) collective-permute-start(f32[392,128]{1,0:T(8,128)S(1)} %get-tuple-element.24), channel_id=1, source_target_pairs={{0,24},{8,16},{16,8},{24,0},{1,25},{9,17},{17,9},{25,1},{2,26},{10... | collective-permute-start | bytes 602120 | tf_op jit(solution)/shard_map/ppermute | solution.py:784
  5.4 1.4 %requests.1 = (f32[64,128]{1,0:T(8,128)}, s32[32,128]{1,0:T(8,128)S(1)}, f32[32,128]{1,0:T(8,128)S(1)}) custom-call(s32[32,128]{1,0:T(8,128)S(1)} %bitcast.21, s32[32,128]{1,0:T(8,128)S(1)} %bitcast.22, f32[1,128]{1,0:T(1,128)S(1)} %bitcast.23), custom_call_target="tpu_custom_call" | custom-call | flops 100000000 | bytes 1048576 | tf_op jit(solution)/shard_map/requests/pallas_call | solution.py:811
  6.8 5.8 %all-to-all-start = ((f32[8,8,128]{2,1,0:T(8,128)}), f32[8,8,128]{2,1,0:T(8,128)S(1)}, u32[]{:S(2)}, u32[]{:S(2)}) async-start(f32[8,8,128]{2,1,0:T(8,128)} %bitcast.4), calls=%async_computation | async-start | bytes 65536 | tf_op jit(solution)/shard_map/all_to_all | solution.py:817
  12.7 0.0 collective-permute-done.1.from_b
  12.7 2.1 %collective-permute-start.2 = (f32[200,128]{1,0:T(8,128)S(1)}, f32[200,128]{1,0:T(8,128)S(1)}, u32[]{:S(2)}, u32[]{:S(2)}) collective-permute-start(f32[200,128]{1,0:T(8,128)S(1)} %get-tuple-element.27.own_hi), channel_id=1, source_target_pairs={{0,1},{1,2},{2,3},{3,4},{4,5},{5,6},{6,7},{7,0},{8,9},{9,10},{10,1... | collective-permute-start | bytes 307208 | tf_op jit(solution)/shard_map/ppermute | solution.py:777
  14.8 2.8 %collective-permute-start.3 = (f32[200,128]{1,0:T(8,128)S(1)}, f32[200,128]{1,0:T(8,128)S(1)}, u32[]{:S(2)}, u32[]{:S(2)}) collective-permute-start(f32[200,128]{1,0:T(8,128)S(1)} %get-tuple-element.28.own_lo), channel_id=1, source_target_pairs={{0,7},{1,0},{2,1},{3,2},{4,3},{5,4},{6,5},{7,6},{8,15},{9,8},{10,9... | collective-permute-start | bytes 307208 | tf_op jit(solution)/shard_map/ppermute | solution.py:777
  17.6 7.6 %sweep_inner.1 = (f32[66,96,128]{2,1,0:T(8,128)}, f32[8,128]{1,0:T(8,128)S(1)}) custom-call(f32[64,128,128]{2,1,0:T(8,128)} %p_hbm.5, f32[64,128,128]{2,1,0:T(8,128)} %s_hbm.5, f32[392,128]{1,0:T(8,128)S(1)} %collective-permute-done.from_a, f32[392,128]{1,0:T(8,128)S(1)} %collective-permute-done.1.from_b), custom_call_target="tpu_custom_call" | custom-call | flops 1 | bytes 1 | tf_op jit(solution)/shard_map/sweep_inner/pallas_call | solution.py:822
  25.2 0.0 collective-permute-done.2.tlo
  25.2 13.9 %relax.1 = (f32[64,128,128]{2,1,0:T(8,128)}, f32[8,24,128]{2,1,0:T(8,128)}) custom-call(f32[64,128,128]{2,1,0:T(8,128)} %p_hbm.5, f32[64,128,128]{2,1,0:T(8,128)} %s_hbm.5, f32[392,128]{1,0:T(8,128)S(1)} %collective-permute-done.from_a, f32[392,128]{1,0:T(8,128)S(1)} %collective-permute-done.1.from_b, f32[200,128]{1,0:T(8,128)S(1)} %collective-permute-done.2.tlo, ...), custom_call_target="tpu_custom_call" | custom-call | flops 104857600 | bytes 12582912 | tf_op jit(solution)/shard_map/relax/pallas_call | solution.py:824
  39.1 3.4 %all-to-all-start.1 = ((f32[8,24,128]{2,1,0:T(8,128)}), f32[8,24,128]{2,1,0:T(8,128)S(1)}, u32[]{:S(2)}, u32[]{:S(2)}) async-start(f32[8,24,128]{2,1,0:T(8,128)} %get-tuple-element.33), calls=%async_computation.1 | async-start | bytes 196608 | tf_op jit(solution)/shard_map/all_to_all | solution.py:828
  42.5 2.3 %couple_first.2.ex_a = f32[48,128]{1,0:T(8,128)S(1)} custom-call(f32[32,128,128]{2,1,0:T(8,128)} %bitcast.13, f32[32,128,128]{2,1,0:T(8,128)} %bitcast.9, f32[96,128]{1,0:T(8,128)S(1)} %bitcast.17, f32[392,128]{1,0:T(8,128)S(1)} %collective-permute-done.from_a, f32[392,128]{1,0:T(8,128)S(1)} %collective-permute-done.1.from_b), custom_call_target="tpu_custom_call" | custom-call | flops 1 | bytes 1 | tf_op jit(solution)/shard_map/couple_first/pallas_call | solution.py:829
  44.8 0.0 copy-start
  44.8 2.5 %couple_first.3.ex_b = f32[48,128]{1,0:T(8,128)S(1)} custom-call(f32[32,128,128]{2,1,0:T(8,128)} %bitcast.14, f32[32,128,128]{2,1,0:T(8,128)} %bitcast.10, f32[96,128]{1,0:T(8,128)S(1)} %bitcast.18, f32[392,128]{1,0:T(8,128)S(1)} %collective-permute-done.from_a, f32[392,128]{1,0:T(8,128)S(1)} %collective-permute-done.1.from_b), custom_call_target="tpu_custom_call" | custom-call | flops 1 | bytes 1 | tf_op jit(solution)/shard_map/couple_first/pallas_call | solution.py:830
  47.3 2.3 %all-to-all-done.1.answers = f32[8,24,128]{2,1,0:T(8,128)S(1)} async-done(((f32[8,24,128]{2,1,0:T(8,128)}), f32[8,24,128]{2,1,0:T(8,128)S(1)}, u32[]{:S(2)}, u32[]{:S(2)}) %all-to-all-start.1) | async-done | bytes 98336 | tf_op jit(solution)/shard_map/all_to_all | solution.py:828
  49.6 0.7 %section_first.1 = (f32[96,128]{1,0:T(8,128)S(1)}, f32[96,128]{1,0:T(8,128)S(1)}, f32[8,128]{1,0:T(8,128)S(1)}, f32[8,128]{1,0:T(8,128)S(1)}) custom-call(f32[8,24,128]{2,1,0:T(8,128)S(1)} %all-to-all-done.1.answers, s32[32,128]{1,0:T(8,128)S(1)} %get-tuple-element.34.slots, f32[96,128]{1,0:T(8,128)S(1)} %bitcast.19, f32[48,128]{1,0:T(8,128)S(1)} %couple_first.2.ex_a, ...), custom_call_target="tpu_custom_call" | custom-call | flops 1000000000 | bytes 1048576 | tf_op jit(solution)/shard_map/section_first/pallas_call | solution.py:831
  50.3 0.1 collective-permute-start.4
  50.4 0.7 %collective-permute-start.5 = (f32[8,128]{1,0:T(8,128)S(1)}, f32[8,128]{1,0:T(8,128)S(1)}, u32[]{:S(2)}, u32[]{:S(2)}) collective-permute-start(f32[8,128]{1,0:T(8,128)S(1)} %get-tuple-element.39), channel_id=1, source_target_pairs={{0,24},{8,16},{16,8},{24,0},{1,25},{9,17},{17,9},{25,1},{2,26},{10... | collective-permute-start | bytes 12296 | tf_op jit(solution)/shard_map/ppermute | solution.py:784
  51.0 0.1 copy-done.1
  51.2 1.5 %couple_second.1.ex = f32[96,128]{1,0:T(8,128)S(1)} custom-call(f32[32,128,128]{2,1,0:T(8,128)S(1)} %bitcast.15, f32[32,128,128]{2,1,0:T(8,128)S(1)} %bitcast.11, f32[96,128]{1,0:T(8,128)S(1)} %get-tuple-element.36.m_ref), custom_call_target="tpu_custom_call" | custom-call | flops 1000000000 | bytes 4194304 | tf_op jit(solution)/shard_map/couple_second/pallas_call | solution.py:835
  52.7 0.0 collective-permute-done.4.from_a
  52.7 0.8 %collective-permute-done.5.from_b = f32[8,128]{1,0:T(8,128)S(1)} collective-permute-done((f32[8,128]{1,0:T(8,128)S(1)}, f32[8,128]{1,0:T(8,128)S(1)}, u32[]{:S(2)}, u32[]{:S(2)}) %collective-permute-start.5) | collective-permute-done | bytes 4128 | tf_op jit(solution)/shard_map/ppermute | solution.py:784
  53.5 0.8 %section_last.1 = f32[96,128]{1,0:T(8,128)} custom-call(f32[96,128]{1,0:T(8,128)S(1)} %get-tuple-element.36.m_ref, f32[96,128]{1,0:T(8,128)S(1)} %couple_second.1.ex, f32[96,128]{1,0:T(8,128)S(1)} %get-tuple-element.37.applied, f32[32,128]{1,0:T(8,128)S(1)} %get-tuple-element.35.target, f32[8,128]{1,0:T(8,128)S(1)} %collective-permute-done.4.from_a, ...), custom_call_target="tpu_custom_call" | custom-call | flops 10000000 | bytes 1048576 | tf_op jit(solution)/shard_map/section_last/pallas_call | solution.py:836
  (19 shorter events, 0.1 us)
Async XLA Ops:
  0.6 1.6 %copy-start.2 = (f32[3,1,4096]{2,1,0:T(1,128)S(1)}, f32[3,1,4096]{2,1,0:T(1,128)}, u32[]{:S(2)}) copy-start(f32[3,1,4096]{2,1,0:T(1,128)} %param.12) | copy-start | bytes 147460
  0.6 4.8 %copy-start.3 = (s32[1,4096]{1,0:T(1,128)S(1)}, s32[1,4096]{1,0:T(1,128)}, u32[]{:S(2)}) copy-start(s32[1,4096]{1,0:T(1,128)} %param.13) | copy-start | bytes 49156
  0.7 4.8 %copy-start.4 = (s32[1,4096]{1,0:T(1,128)S(1)}, s32[1,4096]{1,0:T(1,128)}, u32[]{:S(2)}) copy-start(s32[1,4096]{1,0:T(1,128)} %param.14) | copy-start | bytes 49156
  0.7 4.8 %copy-start.5 = (f32[128]{0:T(128)S(1)}, f32[128]{0:T(128)}, u32[]{:S(2)}) copy-start(f32[128]{0:T(128)} %param.15) | copy-start | bytes 1540
  0.7 16.9 %copy-start.6 = (f32[3,128]{1,0:T(4,128)S(1)}, f32[3,128]{1,0:T(4,128)}, u32[]{:S(2)}) copy-start(f32[3,128]{1,0:T(4,128)} %param.11) | copy-start | bytes 4612
  2.3 10.4 %collective-permute-start = (f32[392,128]{1,0:T(8,128)S(1)}, f32[392,128]{1,0:T(8,128)S(1)}, u32[]{:S(2)}, u32[]{:S(2)}) collective-permute-start(f32[392,128]{1,0:T(8,128)S(1)} %get-tuple-element.23), channel_id=1, source_target_pairs={{0,8},{8,0},{16,24},{24,16},{1,9},{9,1},{17,25},{25,17},{2,10},{10... | collective-permute-start | bytes 602120 | tf_op jit(solution)/shard_map/ppermute | solution.py:784
  2.8 9.9 %collective-permute-start.1 = (f32[392,128]{1,0:T(8,128)S(1)}, f32[392,128]{1,0:T(8,128)S(1)}, u32[]{:S(2)}, u32[]{:S(2)}) collective-permute-start(f32[392,128]{1,0:T(8,128)S(1)} %get-tuple-element.24), channel_id=1, source_target_pairs={{0,24},{8,16},{16,8},{24,0},{1,25},{9,17},{17,9},{25,1},{2,26},{10... | collective-permute-start | bytes 602120 | tf_op jit(solution)/shard_map/ppermute | solution.py:784
  6.8 18.3 %all-to-all-start = ((f32[8,8,128]{2,1,0:T(8,128)}), f32[8,8,128]{2,1,0:T(8,128)S(1)}, u32[]{:S(2)}, u32[]{:S(2)}) async-start(f32[8,8,128]{2,1,0:T(8,128)} %bitcast.4), calls=%async_computation | async-start | bytes 65536 | tf_op jit(solution)/shard_map/all_to_all | solution.py:817
  12.7 12.5 %collective-permute-start.2 = (f32[200,128]{1,0:T(8,128)S(1)}, f32[200,128]{1,0:T(8,128)S(1)}, u32[]{:S(2)}, u32[]{:S(2)}) collective-permute-start(f32[200,128]{1,0:T(8,128)S(1)} %get-tuple-element.27.own_hi), channel_id=1, source_target_pairs={{0,1},{1,2},{2,3},{3,4},{4,5},{5,6},{6,7},{7,0},{8,9},{9,10},{10,1... | collective-permute-start | bytes 307208 | tf_op jit(solution)/shard_map/ppermute | solution.py:777
  14.8 10.4 %collective-permute-start.3 = (f32[200,128]{1,0:T(8,128)S(1)}, f32[200,128]{1,0:T(8,128)S(1)}, u32[]{:S(2)}, u32[]{:S(2)}) collective-permute-start(f32[200,128]{1,0:T(8,128)S(1)} %get-tuple-element.28.own_lo), channel_id=1, source_target_pairs={{0,7},{1,0},{2,1},{3,2},{4,3},{5,4},{6,5},{7,6},{8,15},{9,8},{10,9... | collective-permute-start | bytes 307208 | tf_op jit(solution)/shard_map/ppermute | solution.py:777
  39.1 10.4 %all-to-all-start.1 = ((f32[8,24,128]{2,1,0:T(8,128)}), f32[8,24,128]{2,1,0:T(8,128)S(1)}, u32[]{:S(2)}, u32[]{:S(2)}) async-start(f32[8,24,128]{2,1,0:T(8,128)} %get-tuple-element.33), calls=%async_computation.1 | async-start | bytes 196608 | tf_op jit(solution)/shard_map/all_to_all | solution.py:828
  44.8 6.2 %copy-start = (f32[1,32,128,128]{3,2,1,0:T(8,128)S(1)}, f32[1,32,128,128]{3,2,1,0:T(8,128)}, u32[]{:S(2)}) copy-start(f32[1,32,128,128]{3,2,1,0:T(8,128)} %param.17) | copy-start | bytes 6291460
  49.6 1.6 %copy-start.1 = (f32[1,32,128,128]{3,2,1,0:T(8,128)S(1)}, f32[1,32,128,128]{3,2,1,0:T(8,128)}, u32[]{:S(2)}) copy-start(f32[1,32,128,128]{3,2,1,0:T(8,128)} %param.16) | copy-start | bytes 6291460
  50.3 2.4 %collective-permute-start.4 = (f32[8,128]{1,0:T(8,128)S(1)}, f32[8,128]{1,0:T(8,128)S(1)}, u32[]{:S(2)}, u32[]{:S(2)}) collective-permute-start(f32[8,128]{1,0:T(8,128)S(1)} %get-tuple-element.38), channel_id=1, source_target_pairs={{0,8},{8,0},{16,24},{24,16},{1,9},{9,1},{17,25},{25,17},{2,10},{10... | collective-permute-start | bytes 12296 | tf_op jit(solution)/shard_map/ppermute | solution.py:784
  50.4 3.1 %collective-permute-start.5 = (f32[8,128]{1,0:T(8,128)S(1)}, f32[8,128]{1,0:T(8,128)S(1)}, u32[]{:S(2)}, u32[]{:S(2)}) collective-permute-start(f32[8,128]{1,0:T(8,128)S(1)} %get-tuple-element.39), channel_id=1, source_target_pairs={{0,24},{8,16},{16,8},{24,0},{1,25},{9,17},{17,9},{25,1},{2,26},{10... | collective-permute-start | bytes 12296 | tf_op jit(solution)/shard_map/ppermute | solution.py:784
